TPU v7x, 32 devices: a whole 2x2x4 slice. The times are simulated.
32 devices in a mesh: slab: 4 (over y, x), sample: 8 (over z, core).
Axes of the slice: x: 2, y: 2, z: 4, core: 2. Of those that a mesh axis runs over, the one named last changes fastest.
Arguments:
- activations: bfloat16 [8, 32, 16, 8, 128], P('sample', None, 'slab'), may hold values from -6 to 6
- grad_out: bfloat16 [8, 64, 16, 8, 128], P('sample', 'slab'), may hold values from -6 to 6
- weight: bfloat16 [27, 64, 32], replicated, may hold values from -0.21875 to 0.21875
Outputs:
- grad_inputs: bfloat16 [8, 32, 16, 8, 128], P('sample', None, 'slab')
- grad_weight: float32 [27, 64, 32], replicated
- grad_bias: float32 [64], replicated
All inputs are finite; a program needn't handle non-finite values.
Results may differ from a plain program's by a relative error of at most 0.001.
Values may be sent and summed in bfloat16 or wider, within the bound.
No kernel may reach another device: no remote copies, remote signals or barrier semaphores. Data moves between devices by JAX's collectives and lax.ppermute only.
A program may use at most 64 MiB of HBM per device.

v0:
```python
import math

import jax
import jax.numpy as jnp
from jax import lax
from jax.sharding import PartitionSpec as P


def with_halo(block, sides, width):
    for axis, dim in sides:
        count = lax.axis_size(axis)
        forward = [(i, i + 1) for i in range(count - 1)]
        backward = [(target, source) for source, target in forward]
        low = lax.ppermute(
            lax.slice_in_dim(block, block.shape[dim] - width, None, axis=dim), axis, forward
        )
        high = lax.ppermute(lax.slice_in_dim(block, 0, width, axis=dim), axis, backward)
        block = jnp.concatenate([low, block, high], axis=dim)
    return block


def offsets_list():
    return [
        (shift_z, shift_y, shift_x)
        for shift_z in (-1, 0, 1)
        for shift_y in (-1, 0, 1)
        for shift_x in (-1, 0, 1)
    ]


def local(activations, grad_out, weight):
    samples, in_chan, planes, y_cells, x_cells = activations.shape
    slabs = lax.axis_size("slab")
    x_ext = with_halo(activations, (("slab", 2),), 1)
    regrouped = lax.all_to_all(grad_out, "slab", split_axis=2, concat_axis=1, tiled=True)
    g_ext = with_halo(regrouped, (("slab", 2),), 1)
    widths = ((0, 0), (0, 0), (0, 0), (1, 1), (1, 1))
    padded_in = jnp.pad(x_ext, widths)
    padded_co = jnp.pad(g_ext, widths)
    center = padded_co[:, :, 1 : 1 + planes, 1 : 1 + y_cells, 1 : 1 + x_cells]
    grad_in = jnp.zeros((samples, in_chan, planes, y_cells, x_cells), jnp.float32)
    pieces = []
    for offset, (shift_z, shift_y, shift_x) in enumerate(offsets_list()):
        moved_in = padded_in[
            :,
            :,
            1 + shift_z : 1 + shift_z + planes,
            1 + shift_y : 1 + shift_y + y_cells,
            1 + shift_x : 1 + shift_x + x_cells,
        ]
        moved_co = padded_co[
            :,
            :,
            1 - shift_z : 1 - shift_z + planes,
            1 - shift_y : 1 - shift_y + y_cells,
            1 - shift_x : 1 - shift_x + x_cells,
        ]
        pieces.append(
            jnp.einsum("sozyx,sizyx->oi", center, moved_in, preferred_element_type=jnp.float32)
        )
        grad_in = grad_in + jnp.einsum(
            "oi,sozyx->sizyx", weight[offset], moved_co, preferred_element_type=jnp.float32
        )
    wpart = jnp.stack(pieces)
    bpart = jnp.sum(center.astype(jnp.float32), axis=(0, 2, 3, 4))
    wtotal, btotal = lax.psum((wpart, bpart), ("slab", "sample"))
    all_cells = samples * lax.axis_size("sample") * planes * slabs * y_cells * x_cells
    factor = 1.0 / math.sqrt(all_cells)
    return (grad_in.astype(jnp.bfloat16), wtotal * factor, btotal * factor)


def solution(mesh):
    placed = (P("sample", None, "slab", None, None), P("sample", "slab", None, None, None), P())
    return jax.shard_map(
        local,
        mesh=mesh,
        in_specs=placed,
        out_specs=(P("sample", None, "slab", None, None), P(), P()),
        check_vma=False,
    )
```

profile of v0, /device:TPU:0, one launch (start us, length us, event | category | flops | bytes accessed | tf_op | source)
XLA Modules:
  0.0 226.4 jit_solution(15726194479750979964)
XLA Ops:
  7.2 2.0 copy.41
  9.2 5.2 %all-to-all-start = ((bf16[1,16,16,8,128]{4,3,1,0,2:T(8,128)(2,1)}), bf16[1,16,16,8,128]{4,3,1,0,2:T(8,128)(2,1)S(1)}, u32[]{:S(2)}, u32[]{:S(2)}) async-start(bf16[1,16,16,8,128]{4,3,1,0,2:T(8,128)(2,1)} %copy.41), calls=%async_computation | async-start | bytes 1048576 | tf_op jit(solution)/shard_map/all_to_all | solution.py:35
  14.5 3.9 %collective-permute-start.2 = (bf16[1,32,1,8,128]{4,1,2,3,0:T(8,128)(2,1)S(1)}, bf16[1,32,1,8,128]{4,1,2,3,0:T(8,128)(2,1)S(1)}, u32[]{:S(2)}, u32[]{:S(2)}) collective-permute-start(bf16[1,32,1,8,128]{4,1,2,3,0:T(8,128)(2,1)S(1)} %get-tuple-element.11), channel_id=1, source_target_pairs={{0,8},{8,16},{16,24},{1,9},{9,17},{17,25},{2,10},{10,18},{18,26},{... | collective-permute-start | bytes 196616 | tf_op jit(solution)/shard_map/ppermute | solution.py:14
  18.4 1.3 collective-permute-start.3
  19.7 1.8 collective-permute-done.2
  21.5 3.6 %collective-permute-done.3 = bf16[1,32,1,8,128]{4,1,2,3,0:T(8,128)(2,1)S(1)} collective-permute-done((bf16[1,32,1,8,128]{4,1,2,3,0:T(8,128)(2,1)S(1)}, bf16[1,32,1,8,128]{4,1,2,3,0:T(8,128)(2,1)S(1)}, u32[]{:S(2)}, u32[]{:S(2)}) %collective-permute-start.3) | collective-permute-done | bytes 65568 | tf_op jit(solution)/shard_map/ppermute | solution.py:17
  25.2 0.4 select_maximum_fusion.2
  25.9 39.5 %psum.15 = f32[64]{0:T(128)S(1)} all-reduce(f32[64]{0:T(128)S(1)} %reduce_sum.12), channel_id=1, replica_groups=mesh['slab'=4,'sample'=8] {'slab','sample'}, use_global_device_ids=true, to_apply=%region_2.3 | all-reduce | flops 64 | bytes 512 | tf_op jit(solution)/shard_map/psum | solution.py:66
  65.5 0.5 broadcast_multiply_fusion.1
  66.0 4.2 %collective-permute-start = (bf16[1,64,1,8,128]{4,1,3,2,0:T(8,128)(2,1)S(1)}, bf16[1,64,1,8,128]{4,1,3,2,0:T(8,128)(2,1)S(1)}, u32[]{:S(2)}, u32[]{:S(2)}) collective-permute-start(bf16[1,64,1,8,128]{4,1,3,2,0:T(8,128)(2,1)S(1)} %get-tuple-element.9), channel_id=1, source_target_pairs={{0,8},{8,16},{16,24},{1,9},{9,17},{17,25},{2,10},{10,18},{18,26},{... | collective-permute-start | bytes 393224 | tf_op jit(solution)/shard_map/ppermute | solution.py:14
  70.2 1.3 collective-permute-start.1
  71.7 0.3 fusion.61
  72.1 0.3 fusion.60
  72.4 0.3 fusion.59
  72.7 0.3 fusion.58
  72.9 0.3 fusion.57
  73.5 0.3 fusion.55
  73.9 0.3 fusion.54
  74.5 0.3 fusion.52
  74.8 0.3 fusion.51
  75.7 0.3 fusion.48
  76.3 0.3 fusion.46
  76.6 0.3 fusion.45
  77.2 0.3 fusion.43
  77.5 0.3 fusion.42
  78.4 0.3 fusion.39
  79.0 0.3 fusion.37
  79.3 0.3 fusion.36
  79.7 0.8 copy-done
  80.7 127.1 %all-reduce.4.cloned.1.call-done = f32[27,64,32]{1,2,0:T(8,128)} async-done(((f32[27,64,32]{1,2,0:T(8,128)}), f32[27,64,32]{1,2,0:T(8,128)}) %all-reduce.4.cloned.1.call-update) | async-done | bytes 221200 | tf_op jit(solution)/shard_map/psum | solution.py:66
  207.8 1.8 broadcast_multiply_fusion
  209.6 1.1 select_maximum_fusion
  210.7 0.4 fusion.69
  211.0 0.4 fusion.70
  211.6 0.4 fusion.72
  212.0 0.4 fusion.73
  212.6 0.4 fusion.75
  212.9 0.4 fusion.76
  213.5 0.4 fusion.82
  214.1 0.4 fusion.84
  214.6 0.6 fusion.34
  215.5 0.4 fusion.20
  216.1 0.4 fusion.17
  216.4 0.4 fusion.16
  217.0 0.4 fusion.14
  217.8 0.4 fusion.11
  218.2 0.4 fusion.10
  218.8 0.8 copy.76
  (38 shorter events, 5.8 us)
Async XLA Ops:
  7.2 7.2 %copy-start.1 = (bf16[1,32,4,8,128]{4,3,2,1,0:T(8,128)(2,1)S(1)}, bf16[1,32,4,8,128]{4,3,2,1,0:T(8,128)(2,1)}, u32[]{:S(2)}) copy-start(bf16[1,32,4,8,128]{4,3,2,1,0:T(8,128)(2,1)} %param.3) | copy-start | bytes 786436
  9.2 16.4 %all-to-all-start = ((bf16[1,16,16,8,128]{4,3,1,0,2:T(8,128)(2,1)}), bf16[1,16,16,8,128]{4,3,1,0,2:T(8,128)(2,1)S(1)}, u32[]{:S(2)}, u32[]{:S(2)}) async-start(bf16[1,16,16,8,128]{4,3,1,0,2:T(8,128)(2,1)} %copy.41), calls=%async_computation | async-start | bytes 1048576 | tf_op jit(solution)/shard_map/all_to_all | solution.py:35
  14.3 193.4 %all-reduce.4.cloned.1.call-start = ((), (), s32[]{:S(2)}) async-start(), calls=%async_computation.1 | async-start | bytes 884736 | tf_op jit(solution)/shard_map/psum | solution.py:66
  14.5 7.0 %collective-permute-start.2 = (bf16[1,32,1,8,128]{4,1,2,3,0:T(8,128)(2,1)S(1)}, bf16[1,32,1,8,128]{4,1,2,3,0:T(8,128)(2,1)S(1)}, u32[]{:S(2)}, u32[]{:S(2)}) collective-permute-start(bf16[1,32,1,8,128]{4,1,2,3,0:T(8,128)(2,1)S(1)} %get-tuple-element.11), channel_id=1, source_target_pairs={{0,8},{8,16},{16,24},{1,9},{9,17},{17,25},{2,10},{10,18},{18,26},{... | collective-permute-start | bytes 196616 | tf_op jit(solution)/shard_map/ppermute | solution.py:14
  18.4 6.8 %collective-permute-start.3 = (bf16[1,32,1,8,128]{4,1,2,3,0:T(8,128)(2,1)S(1)}, bf16[1,32,1,8,128]{4,1,2,3,0:T(8,128)(2,1)S(1)}, u32[]{:S(2)}, u32[]{:S(2)}) collective-permute-start(bf16[1,32,1,8,128]{4,1,2,3,0:T(8,128)(2,1)S(1)} %get-tuple-element.12), channel_id=1, source_target_pairs={{8,0},{16,8},{24,16},{9,1},{17,9},{25,17},{10,2},{18,10},{26,18},{... | collective-permute-start | bytes 196616 | tf_op jit(solution)/shard_map/ppermute | solution.py:17
  66.0 143.6 %collective-permute-start = (bf16[1,64,1,8,128]{4,1,3,2,0:T(8,128)(2,1)S(1)}, bf16[1,64,1,8,128]{4,1,3,2,0:T(8,128)(2,1)S(1)}, u32[]{:S(2)}, u32[]{:S(2)}) collective-permute-start(bf16[1,64,1,8,128]{4,1,3,2,0:T(8,128)(2,1)S(1)} %get-tuple-element.9), channel_id=1, source_target_pairs={{0,8},{8,16},{16,24},{1,9},{9,17},{17,25},{2,10},{10,18},{18,26},{... | collective-permute-start | bytes 393224 | tf_op jit(solution)/shard_map/ppermute | solution.py:14
  70.2 139.4 %collective-permute-start.1 = (bf16[1,64,1,8,128]{4,1,3,2,0:T(8,128)(2,1)S(1)}, bf16[1,64,1,8,128]{4,1,3,2,0:T(8,128)(2,1)S(1)}, u32[]{:S(2)}, u32[]{:S(2)}) collective-permute-start(bf16[1,64,1,8,128]{4,1,3,2,0:T(8,128)(2,1)S(1)} %get-tuple-element.10), channel_id=1, source_target_pairs={{8,0},{16,8},{24,16},{9,1},{17,9},{25,17},{10,2},{18,10},{26,18},{... | collective-permute-start | bytes 393224 | tf_op jit(solution)/shard_map/ppermute | solution.py:17
  78.4 2.1 copy-start.2
  79.7 0.8 copy-start
Sparse Core Ops, SparseCore 0:
  80.6 127.1 all-reduce.3
where the time goes:
time: 227 us; the launch traced here: 226 us
  waiting for transfers between devices  133 us (59%)
  blocking collectives  39.5 us (17%)
  matrix products  16.4 us (7%)
  starting transfers between devices  15.9 us (7%)
  between operations  14.2 us (6%)
  other arithmetic  3.95 us (2%)
  local copies, waits for them, and re-layouts  3.91 us (2%)
    psum x1, waiting for transfers between devices, local(): wtotal, btotal = lax.psum((wpart, bpart), ('slab', 'sample'))  127 us
    psum x1, blocking collectives, local(): wtotal, btotal = lax.psum((wpart, bpart), ('slab', 'sample'))  39.5 us
    dot_general x27, matrix products, local(): jnp.einsum('oi,sozyx->sizyx', weight[offset], moved_co, preferred_element...  8.22 us
    dot_general x27, matrix products, local(): jnp.einsum('sozyx,sizyx->oi', center, moved_in, preferred_element_type=jn...  8.15 us
    ppermute x2, starting transfers between devices, with_halo(): lax.ppermute(lax.slice_in_dim(block, block.shape[dim] - width, None, axis...  8.12 us
    all_to_all x1, starting transfers between devices, local(): lax.all_to_all(grad_out, 'slab', split_axis=2, concat_axis=1, tiled=True)  5.16 us
  transfers between devices with their start and end apart: 6, of which 3 were waited for; matrix products, arithmetic and copies ran while one was open for 5% of the time, Pallas kernels for 0%

commit v1 on v0

v1 whole, which is shorter than its diff:
```python
import functools
import math

import jax
import jax.numpy as jnp
from jax import lax
from jax.experimental import pallas as pl
from jax.experimental.pallas import tpu as pltpu
from jax.sharding import PartitionSpec as P

F32 = jnp.float32
BF16 = jnp.bfloat16
NT = (((1,), (1,)), ((), ()))


def iota(shape, dim):
    return lax.broadcasted_iota(jnp.int32, shape, dim)


def vmem():
    return pl.BlockSpec(memory_space=pltpu.VMEM)


def smem():
    return pl.BlockSpec(memory_space=pltpu.SMEM)


def filter_kernel(where, g_own, g_nbr, a_own, a_nbr, out, abuf, gbuf):
    row, col, core = where[0], where[1], where[2]
    chans = g_own.shape[0]
    r = iota((256, 256), 0)
    q = iota((256, 256), 1)
    perm_a = (((q & 7) == (r >> 5)) & ((q >> 3) == (r & 31))).astype(F32).astype(BF16)
    half = (r & 31) >> 4
    perm_g = (
        ((q & 7) == (r >> 5)) & (((q & 127) >> 3) == (r & 15)) & ((q >> 7) == jnp.where(row == 0, half, 1 - half))
    ).astype(F32).astype(BF16)
    lane = iota((256, 128), 1)

    for slot in (0, 1, 10, 11):
        abuf[slot] = jnp.zeros((96, 1024), BF16)
    for source, first in ((a_own, 2 + 4 * col), (a_nbr, 2 + 4 * (1 - col))):
        for plane in range(4):
            turned = jnp.dot(perm_a, source[:, plane].reshape(256, 128), preferred_element_type=F32).astype(BF16)
            for shift in range(3):
                for y in range(8):
                    act_y = y + shift - 1
                    piece = jnp.zeros((32, 128), BF16)
                    if 0 <= act_y < 8:
                        piece = turned[32 * act_y : 32 * act_y + 32]
                    abuf[first + plane, 32 * shift : 32 * shift + 32, 128 * y : 128 * y + 128] = piece

    gbuf[9 * row] = jnp.zeros((96, 1024), BF16)
    total = jnp.zeros((32, 128), F32)
    for plane in range(9):
        both = jnp.concatenate(
            [g_own[:, 7 * row + plane].reshape(8 * chans, 128), g_nbr[:, plane].reshape(8 * chans, 128)], axis=0
        )
        turned = jnp.dot(perm_g, both, preferred_element_type=F32)
        moved = (
            jnp.where(lane == 127, 0.0, pltpu.roll(turned, 127, 1)),
            turned,
            jnp.where(lane == 0, 0.0, pltpu.roll(turned, 1, 1)),
        )
        for shift in range(3):
            packed = moved[shift].astype(BF16)
            for y in range(8):
                gbuf[plane + 1 - row, 32 * shift : 32 * shift + 32, 128 * y : 128 * y + 128] = packed[
                    32 * y : 32 * y + 32
                ]
        cells = turned[0:32]
        for y in range(1, 8):
            cells = cells + turned[32 * y : 32 * y + 32]
        if plane == 0:
            cells = jnp.where(row == 0, cells, 0.0)
        if plane == 8:
            cells = jnp.where(row == 0, 0.0, cells)
        total = total + cells

    acc = jnp.zeros((96, 288), F32)
    for slot in range(10):
        acc = acc + lax.dot_general(
            gbuf[slot], abuf[slot : slot + 3].reshape(288, 1024), NT, preferred_element_type=F32
        )

    tail = jnp.concatenate([acc[24 * m : 24 * m + 24, 256:288] for m in range(4)], axis=1)
    column = jnp.sum(total, axis=1, keepdims=True)
    line = jnp.sum(jnp.where(iota((32, 128), 0) == iota((32, 128), 1), column, 0.0), axis=0, keepdims=True)
    bias = jnp.where(iota((8, 128), 0) == 0, line, 0.0)
    out[core] = jnp.concatenate([acc[:, 0:128], acc[0:16, 128:256]], axis=0)
    out[1 - core] = jnp.concatenate([acc[16:96, 128:256], tail, bias], axis=0)


def filter_partial(where, g_own, g_nbr, a_own, a_nbr):
    return pl.pallas_call(
        filter_kernel,
        out_shape=jax.ShapeDtypeStruct((2, 112, 128), F32),
        in_specs=[smem()] + [vmem()] * 4,
        out_specs=vmem(),
        scratch_shapes=[pltpu.VMEM((12, 96, 1024), BF16), pltpu.VMEM((10, 96, 1024), BF16)],
        compiler_params=pltpu.CompilerParams(vmem_limit_bytes=24 * 2**20),
        cost_estimate=pl.CostEstimate(flops=2 * 10 * 288 * 96 * 1024, bytes_accessed=2**21, transcendentals=0),
        name="filter_partial",
    )(where, g_own, g_nbr, a_own, a_nbr)


def finish_kernel(factor, where, mine, other, weight_out, bias_out):
    col, core = where[1], where[2]
    lane = iota((1, 128), 1)
    line = jnp.zeros((1, 128), F32)
    for x in range(2):
        which = jnp.where(col == x, 0, 1)
        a = mine[which]
        b = other[which]
        low = jnp.where(core == 0, a, b) * factor
        high = jnp.where(core == 0, b, a) * factor
        table = jnp.concatenate([low, high], axis=0)
        for nine in range(9):
            for dx in range(3):
                k = 9 * (nine // 3) + 3 * (nine % 3) + dx
                if nine < 8:
                    first = 96 * (nine // 4) + 32 * dx
                    block = table[first : first + 32, 32 * (nine % 4) : 32 * (nine % 4) + 32]
                else:
                    parts = []
                    for eight in range(4 * dx, 4 * dx + 4):
                        m, at = eight // 3, 192 + 8 * (eight % 3)
                        parts.append(table[at : at + 8, 32 * m : 32 * m + 32])
                    block = jnp.concatenate(parts, axis=0)
                weight_out[k, 16 * x : 16 * x + 16] = block[0:16]
                weight_out[k, 32 + 16 * x : 48 + 16 * x] = block[16:32]
        values = table[216:217]
        first = pltpu.roll(values, 16 * x, 1) if x else values
        second = pltpu.roll(values, 16 + 16 * x, 1)
        line = jnp.where((lane >= 16 * x) & (lane < 16 * x + 16), first, line)
        line = jnp.where((lane >= 32 + 16 * x) & (lane < 48 + 16 * x), second, line)
    bias_out[...] = line[:, 0:64]


def finish(where, mine, other, factor):
    return pl.pallas_call(
        functools.partial(finish_kernel, factor),
        out_shape=(jax.ShapeDtypeStruct((27, 64, 32), F32), jax.ShapeDtypeStruct((1, 64), F32)),
        in_specs=[smem(), vmem(), vmem()],
        out_specs=(vmem(), vmem()),
        cost_estimate=pl.CostEstimate(flops=2**18, bytes_accessed=2**20, transcendentals=0),
        name="filter_finish",
    )(where, mine, other)


def spread_kernel(where, weight, out):
    place = 2 * where[0] + where[1]
    widen = ((iota((256, 32), 0) >> 3) == iota((256, 32), 1)).astype(F32).astype(BF16)
    column = iota((64, 512), 1)
    block = column >> 7
    partner = jnp.where(block == 0, 0, jnp.where(block == 1, 2, jnp.where(block == 2, 1, 3)))
    slab = jnp.bitwise_xor(partner, place)
    repeat = (iota((64, 512), 0) == 16 * slab + ((column & 127) >> 3)).astype(F32).astype(BF16)
    gap = (iota((256, 512), 0) & 7) - (iota((256, 512), 1) & 7)
    for dz in range(3):
        for dx in range(3):
            band = jnp.zeros((256, 512), F32)
            for dy in range(3):
                tall = lax.dot_general(widen, weight[9 * dz + 3 * dy + dx], NT, preferred_element_type=F32)
                wide = jnp.dot(tall.astype(BF16), repeat, preferred_element_type=F32)
                band = jnp.where(gap == dy - 1, wide, band)
            out[3 * dz + dx] = band.astype(BF16)


def spread_filters(where, weight):
    return pl.pallas_call(
        spread_kernel,
        out_shape=jax.ShapeDtypeStruct((9, 256, 512), BF16),
        in_specs=[smem(), vmem()],
        out_specs=vmem(),
        compiler_params=pltpu.CompilerParams(vmem_limit_bytes=16 * 2**20),
        cost_estimate=pl.CostEstimate(flops=2 * 27 * 256 * 64 * 512, bytes_accessed=2**21, transcendentals=0),
        name="spread_filters",
    )(where, weight)


def input_kernel(where, spread, g_own, g_nbr, g_far, out):
    row, col = where[0], where[1]
    offset = row + col
    lane = iota((256, 128), 1)

    def plane_of(index):
        at = offset + index
        inside = (at >= 0) & (at < 6)
        at = jnp.clip(at, 0, 5)
        parts = [
            g_own[:, 7 * row + 3 * col + at].reshape(128, 128),
            g_nbr[:, 3 * col + at].reshape(128, 128),
            g_far[:, at].reshape(256, 128),
        ]
        value = jnp.concatenate(parts, axis=0)
        if index in (-1, 4):
            value = jnp.where(inside, value, jnp.zeros_like(value))
        return value

    planes = [plane_of(index) for index in range(-1, 5)]
    stacks = [jnp.concatenate([planes[1 + z - dz] for z in range(4)], axis=1) for dz in (-1, 0, 1)]
    sums = []
    for dx in range(3):
        acc = jnp.dot(spread[dx], stacks[0], preferred_element_type=F32)
        for dz in (1, 2):
            acc = acc + jnp.dot(spread[3 * dz + dx], stacks[dz], preferred_element_type=F32)
        sums.append(acc)
    for z in range(4):
        cut = slice(128 * z, 128 * z + 128)
        value = sums[1][:, cut]
        value = value + jnp.where(lane == 127, 0.0, pltpu.roll(sums[0][:, cut], 127, 1))
        value = value + jnp.where(lane == 0, 0.0, pltpu.roll(sums[2][:, cut], 1, 1))
        out[:, z] = value.astype(BF16).reshape(32, 8, 128)


def input_gradient(where, spread, g_own, g_nbr, g_far):
    return pl.pallas_call(
        input_kernel,
        out_shape=jax.ShapeDtypeStruct((32, 4, 8, 128), BF16),
        in_specs=[smem()] + [vmem()] * 4,
        out_specs=vmem(),
        compiler_params=pltpu.CompilerParams(vmem_limit_bytes=24 * 2**20),
        cost_estimate=pl.CostEstimate(flops=2 * 9 * 256 * 512 * 512, bytes_accessed=2**22, transcendentals=0),
        name="input_gradient",
    )(where, spread, g_own, g_nbr, g_far)


def swap(block, axis, bits):
    count = lax.axis_size(axis)
    return lax.ppermute(block, axis, [(i, i ^ bits) for i in range(count)])


def local_grid(activations, grad_out, weight):
    slab = lax.axis_index("slab")
    row, col = slab // 2, slab % 2
    core = lax.axis_index("sample") % 2
    where = jnp.stack([row, col, core]).astype(jnp.int32)
    act = activations[0]
    g_own = grad_out[0]

    g_out = lax.dynamic_slice_in_dim(g_own, 7 * (1 - row), 9, axis=1)
    g_nbr = swap(g_out, "slab", 2)
    a_nbr = swap(act, "slab", 1)
    spread = spread_filters(where, weight)

    g_pass = jnp.concatenate(
        [
            lax.dynamic_slice_in_dim(g_own, 7 * row + 3 * (1 - col), 6, axis=1),
            lax.dynamic_slice_in_dim(g_nbr, 3 * (1 - col), 6, axis=1),
        ],
        axis=0,
    )
    g_far = swap(g_pass, "slab", 1)

    halves = filter_partial(where, g_own, g_nbr, act, a_nbr)
    chip = halves[0] + swap(halves[1], "sample", 1)
    line = (chip + swap(chip, "sample", 2)) + (swap(chip, "sample", 4) + swap(chip, "sample", 6))
    mine = jnp.stack([line + swap(line, "slab", 2), swap(line, "slab", 1) + swap(line, "slab", 3)])
    other = swap(mine, "sample", 1)

    grad_in = input_gradient(where, spread, g_own, g_nbr, g_far)
    cells = 8 * 128 * 4 * lax.axis_size("slab") * lax.axis_size("sample")
    grad_weight, grad_bias = finish(where, mine, other, 1.0 / math.sqrt(cells))
    return grad_in[None], grad_weight, grad_bias.reshape(64)


def with_halo(block, sides, width):
    for axis, dim in sides:
        count = lax.axis_size(axis)
        forward = [(i, i + 1) for i in range(count - 1)]
        backward = [(target, source) for source, target in forward]
        low = lax.ppermute(
            lax.slice_in_dim(block, block.shape[dim] - width, None, axis=dim), axis, forward
        )
        high = lax.ppermute(lax.slice_in_dim(block, 0, width, axis=dim), axis, backward)
        block = jnp.concatenate([low, block, high], axis=dim)
    return block


def offsets_list():
    return [
        (shift_z, shift_y, shift_x)
        for shift_z in (-1, 0, 1)
        for shift_y in (-1, 0, 1)
        for shift_x in (-1, 0, 1)
    ]


def local_any(activations, grad_out, weight):
    samples, in_chan, planes, y_cells, x_cells = activations.shape
    slabs = lax.axis_size("slab")
    regrouped = lax.all_to_all(grad_out, "slab", split_axis=2, concat_axis=1, tiled=True)
    g_ext = with_halo(regrouped, (("slab", 2),), 1)
    widths = ((0, 0), (0, 0), (0, 0), (1, 1), (1, 1))
    padded_co = jnp.pad(g_ext, widths)
    grad_in = jnp.zeros((samples, in_chan, planes, y_cells, x_cells), F32)
    pieces = []
    for offset, (shift_z, shift_y, shift_x) in enumerate(offsets_list()):
        moved_co = padded_co[
            :,
            :,
            1 - shift_z : 1 - shift_z + planes,
            1 - shift_y : 1 - shift_y + y_cells,
            1 - shift_x : 1 - shift_x + x_cells,
        ]
        pieces.append(jnp.einsum("sozyx,sizyx->oi", moved_co, activations, preferred_element_type=F32))
        grad_in = grad_in + jnp.einsum("oi,sozyx->sizyx", weight[offset], moved_co, preferred_element_type=F32)
    wpart = jnp.stack(pieces)
    bpart = jnp.sum(regrouped.astype(F32), axis=(0, 2, 3, 4))
    wtotal, btotal = lax.psum((wpart, bpart), ("slab", "sample"))
    all_cells = samples * lax.axis_size("sample") * planes * slabs * y_cells * x_cells
    factor = 1.0 / math.sqrt(all_cells)
    return (grad_in.astype(BF16), wtotal * factor, btotal * factor)


def local(activations, grad_out, weight):
    grid = (
        lax.axis_size("slab") == 4
        and lax.axis_size("sample") == 8
        and activations.shape == (1, 32, 4, 8, 128)
        and grad_out.shape == (1, 16, 16, 8, 128)
    )
    return (local_grid if grid else local_any)(activations, grad_out, weight)


def solution(mesh):
    placed = (P("sample", None, "slab", None, None), P("sample", "slab", None, None, None), P())
    return jax.shard_map(
        local,
        mesh=mesh,
        in_specs=placed,
        out_specs=(P("sample", None, "slab", None, None), P(), P()),
        check_vma=False,
    )
```

time: 227 us -> 60.3 us (0.27)
  waiting for transfers between devices: 133 us -> 20.6 us
  blocking collectives: 39.5 us -> 0 us
  matrix products: 16.4 us -> 0 us
  Pallas kernels: 0 us -> 16.1 us
  between operations: 14.2 us -> 0.8 us
  local copies, waits for them, and re-layouts: 3.91 us -> 7.28 us
  other arithmetic: 3.95 us -> 0.93 us
    psum x1 -> x0, waiting for transfers between devices: 127 us -> none  [local(): wtotal, btotal = lax.psum((wpart, bpart), ('slab', 'sample'))]
    psum x1 -> x0, blocking collectives: 39.5 us -> none  [local(): wtotal, btotal = lax.psum((wpart, bpart), ('slab', 'sample'))]
    dot_general x54 -> x0, matrix products: 16.4 us -> none  [the longest x27 8.22 us: local(): jnp.einsum('oi,sozyx->sizyx', weight[offset], moved_co, preferred_element...]
    pallas_call x0 -> x4, Pallas kernels: none -> 16.1 us  [the longest x1 6.12 us: spread_filters(): pl.pallas_call(spread_kernel, out_shape=jax.ShapeDtypeStruct((9, 256, 512...]
    ppermute x4 -> x11, waiting for transfers between devices: 5.46 us -> 20.6 us  [swap(): return lax.ppermute(block, axis, [(i, i ^ bits) for i in range(count)])]
    all_to_all x1 -> x0, starting transfers between devices: 5.16 us -> none  [local(): lax.all_to_all(grad_out, 'slab', split_axis=2, concat_axis=1, tiled=True)]
    ppermute x4 -> x11, starting transfers between devices: 10.7 us -> 13.9 us  [swap(): return lax.ppermute(block, axis, [(i, i ^ bits) for i in range(count)])]
    unnamed x9 -> x20, local copies, waits for them, and re-layouts: 3.68 us -> 6.24 us
  transfers between devices with their start and end apart: 6 -> 11, of which waited for: 3 -> 6; matrix products, arithmetic and copies ran while one was open for 5% -> 6% of each run, Pallas kernels for 0% -> 14%
where the time goes in v1:
time: 60.3 us; the launch traced here: 59.7 us
  waiting for transfers between devices  20.6 us (34%)
  Pallas kernels  16.1 us (27%)
  starting transfers between devices  13.9 us (23%)
  local copies, waits for them, and re-layouts  7.28 us (12%)
  other arithmetic  0.93 us (2%)
  between operations  0.8 us (1%)
    ppermute x11, waiting for transfers between devices, swap(): return lax.ppermute(block, axis, [(i, i ^ bits) for i in range(count)])  20.6 us
    ppermute x11, starting transfers between devices, swap(): return lax.ppermute(block, axis, [(i, i ^ bits) for i in range(count)])  13.9 us
    unnamed x20, local copies, waits for them, and re-layouts  6.24 us
    pallas_call x1, Pallas kernels, spread_filters(): pl.pallas_call(spread_kernel, out_shape=jax.ShapeDtypeStruct((9, 256, 512...  6.12 us
    pallas_call x1, Pallas kernels, filter_partial(): pl.pallas_call(filter_kernel, out_shape=jax.ShapeDtypeStruct((2, 112, 128...  4.47 us
    pallas_call x1, Pallas kernels, input_gradient(): pl.pallas_call(input_kernel, out_shape=jax.ShapeDtypeStruct((32, 4, 8, 12...  3.27 us
    pallas_call x1, Pallas kernels, finish(): pl.pallas_call(functools.partial(finish_kernel, factor), out_shape=(jax.S...  2.21 us
  transfers between devices with their start and end apart: 11, of which 6 were waited for; matrix products, arithmetic and copies ran while one was open for 6% of the time, Pallas kernels for 14%

profile of v1, /device:TPU:0, one launch (start us, length us, event | category | flops | bytes accessed | tf_op | source)
XLA Modules:
  0.0 59.7 jit_solution(8882433536092443929)
XLA Ops:
  0.7 1.0 %dynamic-slice_bitcast_fusion = bf16[16,9,8,128]{3,2,1,0:T(8,128)(2,1)S(1)} fusion(bf16[1,16,16,8,128]{4,3,2,1,0:T(8,128)(2,1)} %param.4, s32[]{:T(128)S(6)} %select_n.27), kind=kLoop, calls=%fused_computation.1 | loop fusion | bytes 589828 | tf_op jit(solution)/shard_map/dynamic_slice | solution.py:242
  1.6 3.0 %collective-permute-start = (bf16[16,9,8,128]{3,2,1,0:T(8,128)(2,1)S(1)}, bf16[16,9,8,128]{3,2,1,0:T(8,128)(2,1)S(1)}, u32[]{:S(2)}, u32[]{:S(2)}) collective-permute-start(bf16[16,9,8,128]{3,2,1,0:T(8,128)(2,1)S(1)} %dynamic-slice_bitcast_fusion), channel_id=1, source_target_pairs={{0,16},{8,24},{16,0},{24,8},{1,17},{9,25},{17,1},{25,9},{2,18},{10... | collective-permute-start | bytes 884744 | tf_op jit(solution)/shard_map/ppermute | solution.py:231
  4.7 1.5 %collective-permute-start.2 = (bf16[32,4,8,128]{3,2,1,0:T(8,128)(2,1)}, bf16[32,4,8,128]{3,2,1,0:T(8,128)(2,1)S(1)}, u32[]{:S(2)}, u32[]{:S(2)}) collective-permute-start(bf16[32,4,8,128]{3,2,1,0:T(8,128)(2,1)} %bitcast.23), channel_id=1, source_target_pairs={{0,8},{8,0},{16,24},{24,16},{1,9},{9,1},{17,25},{25,17},{2,10},{10... | collective-permute-start | bytes 786440 | tf_op jit(solution)/shard_map/ppermute | solution.py:231
  6.2 0.1 pad_add_fusion.where
  6.2 0.0 copy-start.4
  6.3 6.4 %collective-permute-done.2.a_nbr = bf16[32,4,8,128]{3,2,1,0:T(8,128)(2,1)S(1)} collective-permute-done((bf16[32,4,8,128]{3,2,1,0:T(8,128)(2,1)}, bf16[32,4,8,128]{3,2,1,0:T(8,128)(2,1)S(1)}, u32[]{:S(2)}, u32[]{:S(2)}) %collective-permute-start.2) | collective-permute-done | bytes 262176 | tf_op jit(solution)/shard_map/ppermute | solution.py:231
  12.7 0.0 collective-permute-done.g_nbr
  12.7 0.0 copy-start.2
  12.7 0.0 copy-start
  12.7 1.1 %copy-done = bf16[1,16,16,8,128]{4,3,2,1,0:T(8,128)(2,1)S(1)} copy-done((bf16[1,16,16,8,128]{4,3,2,1,0:T(8,128)(2,1)S(1)}, bf16[1,16,16,8,128]{4,3,2,1,0:T(8,128)(2,1)}, u32[]{:S(2)}) %copy-start) | copy-done | bytes 524312
  13.8 0.9 %copy-done.6 = bf16[1,32,4,8,128]{4,3,2,1,0:T(8,128)(2,1)S(1)} copy-done((bf16[1,32,4,8,128]{4,3,2,1,0:T(8,128)(2,1)S(1)}, bf16[1,32,4,8,128]{4,3,2,1,0:T(8,128)(2,1)}, u32[]{:S(2)}) %copy-start.6) | copy-done | bytes 262168
  14.8 0.0 copy-start.8
  14.8 4.5 %filter_partial.1 = f32[2,112,128]{2,1,0:T(8,128)S(1)} custom-call(s32[3]{0:T(128)S(1)} %pad_add_fusion.where, bf16[16,16,8,128]{3,2,1,0:T(8,128)(2,1)S(1)} %bitcast.21, bf16[16,9,8,128]{3,2,1,0:T(8,128)(2,1)S(1)} %collective-permute-done.g_nbr, bf16[32,4,8,128]{3,2,1,0:T(8,128)(2,1)S(1)} %bitcast.24, bf16[32,4,8,128]{3,2,1,0:T(8,128)(2,1)S(1)} %collective-permute-done.2.a_nbr), custom_call_target="tpu_custom_call" | custom-call | flops 566231040 | bytes 2097152 | tf_op jit(solution)/shard_map/filter_partial/pallas_call | solution.py:95
  19.3 0.1 collective-permute-start.3
  19.4 1.2 %collective-permute-done.3 = f32[112,128]{1,0:T(8,128)S(1)} collective-permute-done((f32[112,128]{1,0:T(8,128)S(1)}, f32[112,128]{1,0:T(8,128)S(1)}, u32[]{:S(2)}, u32[]{:S(2)}) %collective-permute-start.3) | collective-permute-done | bytes 57376 | tf_op jit(solution)/shard_map/ppermute | solution.py:231
  20.6 2.7 %collective-permute-start.5 = (f32[112,128]{1,0:T(8,128)S(1)}, f32[112,128]{1,0:T(8,128)S(1)}, u32[]{:S(2)}, u32[]{:S(2)}) collective-permute-start(f32[112,128]{1,0:T(8,128)S(1)} %fusion), channel_id=1, source_target_pairs={{0,4},{1,5},{2,6},{3,7},{4,0},{5,1},{6,2},{7,3},{8,12},{9,13},{10,... | collective-permute-start | bytes 172040 | tf_op jit(solution)/shard_map/ppermute | solution.py:231
  23.2 1.3 %collective-permute-start.6 = (f32[112,128]{1,0:T(8,128)S(1)}, f32[112,128]{1,0:T(8,128)S(1)}, u32[]{:S(2)}, u32[]{:S(2)}) collective-permute-start(f32[112,128]{1,0:T(8,128)S(1)} %fusion), channel_id=1, source_target_pairs={{0,6},{1,7},{2,4},{3,5},{4,2},{5,3},{6,0},{7,1},{8,14},{9,15},{10,... | collective-permute-start | bytes 172040 | tf_op jit(solution)/shard_map/ppermute | solution.py:231
  24.6 0.2 collective-permute-start.4
  24.8 2.3 %collective-permute-done.5 = f32[112,128]{1,0:T(8,128)S(1)} collective-permute-done((f32[112,128]{1,0:T(8,128)S(1)}, f32[112,128]{1,0:T(8,128)S(1)}, u32[]{:S(2)}, u32[]{:S(2)}) %collective-permute-start.5) | collective-permute-done | bytes 57376 | tf_op jit(solution)/shard_map/ppermute | solution.py:231
  27.1 2.3 %collective-permute-done.6 = f32[112,128]{1,0:T(8,128)S(1)} collective-permute-done((f32[112,128]{1,0:T(8,128)S(1)}, f32[112,128]{1,0:T(8,128)S(1)}, u32[]{:S(2)}, u32[]{:S(2)}) %collective-permute-start.6) | collective-permute-done | bytes 57376 | tf_op jit(solution)/shard_map/ppermute | solution.py:231
  29.4 0.0 collective-permute-done.4
  29.4 0.8 %collective-permute-start.7 = (f32[112,128]{1,0:T(8,128)S(1)}, f32[112,128]{1,0:T(8,128)S(1)}, u32[]{:S(2)}, u32[]{:S(2)}) collective-permute-start(f32[112,128]{1,0:T(8,128)S(1)} %add_add_fusion), channel_id=1, source_target_pairs={{0,16},{8,24},{16,0},{24,8},{1,17},{9,25},{17,1},{25,9},{2,18},{10... | collective-permute-start | bytes 172040 | tf_op jit(solution)/shard_map/ppermute | solution.py:231
  30.3 0.8 %pad_maximum_fusion = bf16[32,6,8,128]{3,2,1,0:T(8,128)(2,1)} fusion(bf16[16,6,8,128]{3,2,1,0:T(8,128)(2,1)S(1)} %constant_dynamic-slice_fusion, bf16[16,6,8,128]{3,2,1,0:T(8,128)(2,1)S(1)} %dynamic-slice_bitcast_fusion.1), kind=kLoop, calls=%fused_computation | loop fusion | flops 196608 | bytes 786432 | tf_op jit(solution)/shard_map/concatenate | solution.py:247
  31.0 1.5 %collective-permute-start.1 = (bf16[32,6,8,128]{3,2,1,0:T(8,128)(2,1)}, bf16[32,6,8,128]{3,2,1,0:T(8,128)(2,1)}, u32[]{:S(2)}, u32[]{:S(2)}) collective-permute-start(bf16[32,6,8,128]{3,2,1,0:T(8,128)(2,1)} %pad_maximum_fusion), channel_id=1, source_target_pairs={{0,8},{8,0},{16,24},{24,16},{1,9},{9,1},{17,25},{25,17},{2,10},{10... | collective-permute-start | bytes 1179656 | tf_op jit(solution)/shard_map/ppermute | solution.py:231
  32.5 0.5 collective-permute-start.8
  33.1 2.2 %collective-permute-start.9 = (f32[112,128]{1,0:T(8,128)S(1)}, f32[112,128]{1,0:T(8,128)S(1)}, u32[]{:S(2)}, u32[]{:S(2)}) collective-permute-start(f32[112,128]{1,0:T(8,128)S(1)} %add_add_fusion), channel_id=1, source_target_pairs={{0,24},{8,16},{16,8},{24,0},{1,25},{9,17},{17,9},{25,1},{2,26},{10... | collective-permute-start | bytes 172040 | tf_op jit(solution)/shard_map/ppermute | solution.py:231
  35.3 0.0 collective-permute-done.7
  35.3 7.2 %collective-permute-done.8 = f32[112,128]{1,0:T(8,128)S(1)} collective-permute-done((f32[112,128]{1,0:T(8,128)S(1)}, f32[112,128]{1,0:T(8,128)S(1)}, u32[]{:S(2)}, u32[]{:S(2)}) %collective-permute-start.8) | collective-permute-done | bytes 57376 | tf_op jit(solution)/shard_map/ppermute | solution.py:231
  42.4 1.3 %collective-permute-done.9 = f32[112,128]{1,0:T(8,128)S(1)} collective-permute-done((f32[112,128]{1,0:T(8,128)S(1)}, f32[112,128]{1,0:T(8,128)S(1)}, u32[]{:S(2)}, u32[]{:S(2)}) %collective-permute-start.9) | collective-permute-done | bytes 57376 | tf_op jit(solution)/shard_map/ppermute | solution.py:231
  43.8 0.0 copy-done.2
  43.8 0.0 copy-start.7
  43.8 0.0 copy-start.1
  43.8 0.1 collective-permute-start.10
  43.9 0.0 copy-done.8
  43.9 0.3 copy.6.weight
  44.2 0.0 copy-done.4
  44.2 6.1 %spread_filters.1.spread = bf16[9,256,512]{2,1,0:T(8,128)(2,1)S(1)} custom-call(s32[3]{0:T(128)S(1)} %pad_add_fusion.where, bf16[27,64,32]{2,1,0:T(8,128)(2,1)S(1)} %copy.6.weight), custom_call_target="tpu_custom_call" | custom-call | flops 452984832 | bytes 2097152 | tf_op jit(solution)/shard_map/spread_filters/pallas_call | solution.py:171
  50.3 0.0 collective-permute-done.10.other
  50.3 0.0 copy-done.7
  50.3 2.2 %filter_finish.1 = (f32[27,64,32]{2,1,0:T(8,128)}, f32[1,64]{1,0:T(1,128)}) custom-call(s32[3]{0:T(128)} %copy-done.4, f32[2,112,128]{2,1,0:T(8,128)} %copy-done.7, f32[2,112,128]{2,1,0:T(8,128)} %collective-permute-done.10.other), custom_call_target="tpu_custom_call" | custom-call | flops 262144 | bytes 1048576 | tf_op jit(solution)/shard_map/filter_finish/pallas_call | solution.py:141
  52.5 2.2 %copy.7 = f32[27,64,32]{1,2,0:T(8,128)} copy(f32[27,64,32]{2,1,0:T(8,128)} %get-tuple-element.8) | data formatting | bytes 442368
  54.8 0.0 collective-permute-done.1.g_far
  54.8 0.0 copy-done.1
  54.8 0.0 copy-start.3
  54.8 1.0 %copy-done.3 = bf16[16,9,8,128]{3,2,1,0:T(8,128)(2,1)S(1)} copy-done((bf16[16,9,8,128]{3,2,1,0:T(8,128)(2,1)S(1)}, bf16[16,9,8,128]{3,2,1,0:T(8,128)(2,1)}, u32[]{:S(2)}) %copy-start.3) | copy-done | bytes 294936
  55.7 0.0 copy-start.5
  55.7 0.7 %copy-done.5 = s32[3]{0:T(128)S(1)} copy-done((s32[3]{0:T(128)S(1)}, s32[3]{0:T(128)}, u32[]{:S(2)}) %copy-start.5) | copy-done | bytes 36
  56.4 3.3 %input_gradient.1 = bf16[32,4,8,128]{3,2,1,0:T(8,128)(2,1)} custom-call(s32[3]{0:T(128)S(1)} %copy-done.5, bf16[9,256,512]{2,1,0:T(8,128)(2,1)S(1)} %spread_filters.1.spread, bf16[16,16,8,128]{3,2,1,0:T(8,128)(2,1)S(1)} %bitcast.22, bf16[16,9,8,128]{3,2,1,0:T(8,128)(2,1)S(1)} %copy-done.3, bf16[32,6,8,128]{3,2,1,0:T(8,128)(2,1)} %collective-permute-done.1.g_far), custom_call_target="tpu_custom_call" | custom-call | flops 1207959552 | bytes 4194304 | tf_op jit(solution)/shard_map/input_gradient/pallas_call | solution.py:218
  (9 shorter events, 0.1 us)
Async XLA Ops:
  1.6 11.0 %collective-permute-start = (bf16[16,9,8,128]{3,2,1,0:T(8,128)(2,1)S(1)}, bf16[16,9,8,128]{3,2,1,0:T(8,128)(2,1)S(1)}, u32[]{:S(2)}, u32[]{:S(2)}) collective-permute-start(bf16[16,9,8,128]{3,2,1,0:T(8,128)(2,1)S(1)} %dynamic-slice_bitcast_fusion), channel_id=1, source_target_pairs={{0,16},{8,24},{16,0},{24,8},{1,17},{9,25},{17,1},{25,9},{2,18},{10... | collective-permute-start | bytes 884744 | tf_op jit(solution)/shard_map/ppermute | solution.py:231
  4.7 8.0 %collective-permute-start.2 = (bf16[32,4,8,128]{3,2,1,0:T(8,128)(2,1)}, bf16[32,4,8,128]{3,2,1,0:T(8,128)(2,1)S(1)}, u32[]{:S(2)}, u32[]{:S(2)}) collective-permute-start(bf16[32,4,8,128]{3,2,1,0:T(8,128)(2,1)} %bitcast.23), channel_id=1, source_target_pairs={{0,8},{8,0},{16,24},{24,16},{1,9},{9,1},{17,25},{25,17},{2,10},{10... | collective-permute-start | bytes 786440 | tf_op jit(solution)/shard_map/ppermute | solution.py:231
  6.2 37.9 %copy-start.4 = (s32[3]{0:T(128)}, s32[3]{0:T(128)S(1)}, u32[]{:S(2)}) copy-start(s32[3]{0:T(128)S(1)} %pad_add_fusion.where) | copy-start | bytes 40
  12.7 31.1 %copy-start.2 = (bf16[16,9,8,128]{3,2,1,0:T(8,128)(2,1)}, bf16[16,9,8,128]{3,2,1,0:T(8,128)(2,1)S(1)}, u32[]{:S(2)}) copy-start(bf16[16,9,8,128]{3,2,1,0:T(8,128)(2,1)S(1)} %collective-permute-done.g_nbr) | copy-start | bytes 884740
  12.7 1.2 %copy-start = (bf16[1,16,16,8,128]{4,3,2,1,0:T(8,128)(2,1)S(1)}, bf16[1,16,16,8,128]{4,3,2,1,0:T(8,128)(2,1)}, u32[]{:S(2)}) copy-start(bf16[1,16,16,8,128]{4,3,2,1,0:T(8,128)(2,1)} %param.4) | copy-start | bytes 1572868
  13.8 0.9 %copy-start.6 = (bf16[1,32,4,8,128]{4,3,2,1,0:T(8,128)(2,1)S(1)}, bf16[1,32,4,8,128]{4,3,2,1,0:T(8,128)(2,1)}, u32[]{:S(2)}) copy-start(bf16[1,32,4,8,128]{4,3,2,1,0:T(8,128)(2,1)} %param.3) | copy-start | bytes 786436
  14.8 29.1 %copy-start.8 = (bf16[27,64,32]{1,2,0:T(8,128)(2,1)S(1)}, bf16[27,64,32]{1,2,0:T(8,128)(2,1)}, u32[]{:S(2)}) copy-start(bf16[27,64,32]{1,2,0:T(8,128)(2,1)} %param.5) | copy-start | bytes 331780
  19.3 1.3 %collective-permute-start.3 = (f32[112,128]{1,0:T(8,128)S(1)}, f32[112,128]{1,0:T(8,128)S(1)}, u32[]{:S(2)}, u32[]{:S(2)}) collective-permute-start(f32[112,128]{1,0:T(8,128)S(1)} %slice_bitcast_fusion), channel_id=1, source_target_pairs={{0,1},{1,0},{2,3},{3,2},{4,5},{5,4},{6,7},{7,6},{8,9},{9,8},{10,11... | collective-permute-start | bytes 172040 | tf_op jit(solution)/shard_map/ppermute | solution.py:231
  20.6 6.5 %collective-permute-start.5 = (f32[112,128]{1,0:T(8,128)S(1)}, f32[112,128]{1,0:T(8,128)S(1)}, u32[]{:S(2)}, u32[]{:S(2)}) collective-permute-start(f32[112,128]{1,0:T(8,128)S(1)} %fusion), channel_id=1, source_target_pairs={{0,4},{1,5},{2,6},{3,7},{4,0},{5,1},{6,2},{7,3},{8,12},{9,13},{10,... | collective-permute-start | bytes 172040 | tf_op jit(solution)/shard_map/ppermute | solution.py:231
  23.2 6.1 %collective-permute-start.6 = (f32[112,128]{1,0:T(8,128)S(1)}, f32[112,128]{1,0:T(8,128)S(1)}, u32[]{:S(2)}, u32[]{:S(2)}) collective-permute-start(f32[112,128]{1,0:T(8,128)S(1)} %fusion), channel_id=1, source_target_pairs={{0,6},{1,7},{2,4},{3,5},{4,2},{5,3},{6,0},{7,1},{8,14},{9,15},{10,... | collective-permute-start | bytes 172040 | tf_op jit(solution)/shard_map/ppermute | solution.py:231
  24.6 4.8 %collective-permute-start.4 = (f32[112,128]{1,0:T(8,128)S(1)}, f32[112,128]{1,0:T(8,128)S(1)}, u32[]{:S(2)}, u32[]{:S(2)}) collective-permute-start(f32[112,128]{1,0:T(8,128)S(1)} %fusion), channel_id=1, source_target_pairs={{0,2},{1,3},{2,0},{3,1},{4,6},{5,7},{6,4},{7,5},{8,10},{9,11},{10,... | collective-permute-start | bytes 172040 | tf_op jit(solution)/shard_map/ppermute | solution.py:231
  29.4 5.8 %collective-permute-start.7 = (f32[112,128]{1,0:T(8,128)S(1)}, f32[112,128]{1,0:T(8,128)S(1)}, u32[]{:S(2)}, u32[]{:S(2)}) collective-permute-start(f32[112,128]{1,0:T(8,128)S(1)} %add_add_fusion), channel_id=1, source_target_pairs={{0,16},{8,24},{16,0},{24,8},{1,17},{9,25},{17,1},{25,9},{2,18},{10... | collective-permute-start | bytes 172040 | tf_op jit(solution)/shard_map/ppermute | solution.py:231
  31.0 23.7 %collective-permute-start.1 = (bf16[32,6,8,128]{3,2,1,0:T(8,128)(2,1)}, bf16[32,6,8,128]{3,2,1,0:T(8,128)(2,1)}, u32[]{:S(2)}, u32[]{:S(2)}) collective-permute-start(bf16[32,6,8,128]{3,2,1,0:T(8,128)(2,1)} %pad_maximum_fusion), channel_id=1, source_target_pairs={{0,8},{8,0},{16,24},{24,16},{1,9},{9,1},{17,25},{25,17},{2,10},{10... | collective-permute-start | bytes 1179656 | tf_op jit(solution)/shard_map/ppermute | solution.py:231
  32.5 9.9 %collective-permute-start.8 = (f32[112,128]{1,0:T(8,128)S(1)}, f32[112,128]{1,0:T(8,128)S(1)}, u32[]{:S(2)}, u32[]{:S(2)}) collective-permute-start(f32[112,128]{1,0:T(8,128)S(1)} %add_add_fusion), channel_id=1, source_target_pairs={{0,8},{8,0},{16,24},{24,16},{1,9},{9,1},{17,25},{25,17},{2,10},{10... | collective-permute-start | bytes 172040 | tf_op jit(solution)/shard_map/ppermute | solution.py:231
  33.1 10.7 %collective-permute-start.9 = (f32[112,128]{1,0:T(8,128)S(1)}, f32[112,128]{1,0:T(8,128)S(1)}, u32[]{:S(2)}, u32[]{:S(2)}) collective-permute-start(f32[112,128]{1,0:T(8,128)S(1)} %add_add_fusion), channel_id=1, source_target_pairs={{0,24},{8,16},{16,8},{24,0},{1,25},{9,17},{17,9},{25,1},{2,26},{10... | collective-permute-start | bytes 172040 | tf_op jit(solution)/shard_map/ppermute | solution.py:231
  43.8 6.5 %copy-start.7 = (f32[2,112,128]{2,1,0:T(8,128)}, f32[2,112,128]{2,1,0:T(8,128)S(1)}, u32[]{:S(2)}) copy-start(f32[2,112,128]{2,1,0:T(8,128)S(1)} %pad_maximum_fusion.1.mine) | copy-start | bytes 344068
  43.8 11.0 %copy-start.1 = (bf16[1,16,16,8,128]{4,3,2,1,0:T(8,128)(2,1)S(1)}, bf16[1,16,16,8,128]{4,3,2,1,0:T(8,128)(2,1)}, u32[]{:S(2)}) copy-start(bf16[1,16,16,8,128]{4,3,2,1,0:T(8,128)(2,1)} %param.4) | copy-start | bytes 1572868
  43.8 6.5 %collective-permute-start.10 = (f32[2,112,128]{2,1,0:T(8,128)S(1)}, f32[2,112,128]{2,1,0:T(8,128)}, u32[]{:S(2)}, u32[]{:S(2)}) collective-permute-start(f32[2,112,128]{2,1,0:T(8,128)S(1)} %pad_maximum_fusion.1.mine), channel_id=1, source_target_pairs={{0,1},{1,0},{2,3},{3,2},{4,5},{5,4},{6,7},{7,6},{8,9},{9,8},{10,11... | collective-permute-start | bytes 344072 | tf_op jit(solution)/shard_map/ppermute | solution.py:231
  54.8 1.0 %copy-start.3 = (bf16[16,9,8,128]{3,2,1,0:T(8,128)(2,1)S(1)}, bf16[16,9,8,128]{3,2,1,0:T(8,128)(2,1)}, u32[]{:S(2)}) copy-start(bf16[16,9,8,128]{3,2,1,0:T(8,128)(2,1)} %copy-done.2) | copy-start | bytes 884740
  55.7 0.7 %copy-start.5 = (s32[3]{0:T(128)S(1)}, s32[3]{0:T(128)}, u32[]{:S(2)}) copy-start(s32[3]{0:T(128)} %copy-done.4) | copy-start | bytes 40

commit v2 on v1

v2 whole, which is shorter than its diff:
```python
import functools
import math

import jax
import jax.numpy as jnp
from jax import lax
from jax.experimental import pallas as pl
from jax.experimental.pallas import tpu as pltpu
from jax.sharding import PartitionSpec as P

F32 = jnp.float32
BF16 = jnp.bfloat16
NT = (((1,), (1,)), ((), ()))


def iota(shape, dim):
    return lax.broadcasted_iota(jnp.int32, shape, dim)


def vmem():
    return pl.BlockSpec(memory_space=pltpu.VMEM)


def smem():
    return pl.BlockSpec(memory_space=pltpu.SMEM)


def one(mask):
    return mask.astype(F32).astype(BF16)


def act_rows(source, put):
    r, q = iota((256, 256), 0), iota((256, 256), 1)
    perm = one(((q & 7) == (r >> 5)) & ((q >> 3) == (r & 31)))
    both = jnp.concatenate([source[:, plane].reshape(256, 128) for plane in range(4)], axis=1)
    turned = jnp.dot(perm, both, preferred_element_type=F32).astype(BF16)
    for plane in range(4):
        for shift in range(3):
            for y in range(8):
                act_y = y + shift - 1
                piece = jnp.zeros((32, 128), BF16)
                if 0 <= act_y < 8:
                    piece = turned[32 * act_y : 32 * act_y + 32, 128 * plane : 128 * plane + 128]
                put(plane, slice(32 * shift, 32 * shift + 32), slice(128 * y, 128 * y + 128), piece)


def cot_rows(source, first, row, put):
    r, q = iota((128, 128), 0), iota((128, 128), 1)
    perm = one(((q & 7) == (r >> 4)) & ((q >> 3) == (r & 15)))
    lane = iota((128, 128), 1)
    total = jnp.zeros((16, 128), F32)
    for plane in range(9):
        turned = jnp.dot(perm, source[:, first + plane].reshape(128, 128), preferred_element_type=F32)
        moved = (
            jnp.where(lane == 127, 0.0, pltpu.roll(turned, 127, 1)),
            turned,
            jnp.where(lane == 0, 0.0, pltpu.roll(turned, 1, 1)),
        )
        for shift in range(3):
            packed = moved[shift].astype(BF16)
            for y in range(8):
                put(plane, slice(16 * shift, 16 * shift + 16), slice(128 * y, 128 * y + 128), packed[16 * y : 16 * y + 16])
        cells = turned[0:16]
        for y in range(1, 8):
            cells = cells + turned[16 * y : 16 * y + 16]
        if plane == 0:
            cells = jnp.where(row == 0, cells, 0.0)
        if plane == 8:
            cells = jnp.where(row == 0, 0.0, cells)
        total = total + cells
    return total


def near_kernel(where, g_own, a_own, a_rows, g_rows, sums):
    row = where[0]
    def put_a(plane, rows, lanes, piece):
        a_rows[plane, rows, lanes] = piece
    def put_g(plane, rows, lanes, piece):
        g_rows[plane, rows, lanes] = piece
    act_rows(a_own, put_a)
    sums[...] = cot_rows(g_own, 7 * row, row, put_g)


def near_rows(where, g_own, a_own):
    return pl.pallas_call(
        near_kernel,
        out_shape=(jax.ShapeDtypeStruct((4, 96, 1024), BF16), jax.ShapeDtypeStruct((9, 48, 1024), BF16), jax.ShapeDtypeStruct((16, 128), F32)),
        in_specs=[smem(), vmem(), vmem()],
        out_specs=(vmem(), vmem(), vmem()),
        compiler_params=pltpu.CompilerParams(vmem_limit_bytes=8 * 2**20),
        cost_estimate=pl.CostEstimate(flops=2**28, bytes_accessed=2**21, transcendentals=0),
        name="near_rows",
    )(where, g_own, a_own)


def filter_kernel(where, a_rows, g_rows, sums, g_own, g_nbr, a_nbr, after, keep, send, g_pass, abuf, gbuf):
    row, col, core = where[0], where[1], where[2]
    for slot in (0, 1, 10, 11):
        abuf[slot] = jnp.zeros((96, 1024), BF16)
    gbuf[9 * row] = jnp.zeros((96, 1024), BF16)
    near, far = 2 + 4 * col, 6 - 4 * col

    def place(shift, whose):
        return pl.ds(pl.multiple_of(32 * shift + 16 * whose, 16), 16)

    for plane in range(4):
        abuf[near + plane] = a_rows[plane]
    for plane in range(9):
        for shift in range(3):
            gbuf[plane + 1 - row, place(shift, row)] = g_rows[plane, 16 * shift : 16 * shift + 16]

    def put_a(plane, rows, lanes, piece):
        abuf[far + plane, rows, lanes] = piece

    def put_g(plane, rows, lanes, piece):
        gbuf[plane + 1 - row, place(rows.start // 16, 1 - row), lanes] = piece

    act_rows(a_nbr, put_a)
    far_sums = cot_rows(g_nbr, 0, row, put_g)

    wide = jnp.zeros((192, 384), F32)
    for slot in range(0, 10, 2):
        wide = wide + lax.dot_general(
            gbuf[slot : slot + 2].reshape(192, 1024),
            abuf[slot : slot + 4].reshape(384, 1024),
            NT,
            preferred_element_type=F32,
        )
    acc = (wide[0:96, 0:288] + wide[96:192, 96:384]).T
    side = jnp.concatenate([acc[216:288, 32 * m : 32 * m + 32] for m in range(3)], axis=0)
    table = jnp.concatenate([acc[0:216], side], axis=1)
    first = jnp.where(row == 0, sums[...], far_sums)
    second = jnp.where(row == 0, far_sums, sums[...])
    column = jnp.sum(jnp.concatenate([first, second], axis=0), axis=1, keepdims=True)
    line = jnp.sum(jnp.where(iota((32, 128), 0) == iota((32, 128), 1), column, 0.0), axis=0, keepdims=True)
    bias = jnp.where(iota((8, 128), 0) == 0, line, 0.0)
    low = table[0:112]
    high = jnp.concatenate([table[112:216], bias], axis=0)
    keep[...] = jnp.where(core == 0, low, high)
    send[...] = jnp.where(core == 0, high, low)
    for plane in range(6):
        g_pass[0:16, plane] = g_own[:, 7 * row + 3 * (1 - col) + plane]
        g_pass[16:32, plane] = g_nbr[:, 3 * (1 - col) + plane]


def filter_partial(where, a_rows, g_rows, sums, g_own, g_nbr, a_nbr, after):
    return pl.pallas_call(
        filter_kernel,
        out_shape=(jax.ShapeDtypeStruct((112, 128), F32), jax.ShapeDtypeStruct((112, 128), F32), jax.ShapeDtypeStruct((32, 6, 8, 128), BF16)),
        in_specs=[smem()] + [vmem()] * 6 + [pl.BlockSpec(memory_space=pl.ANY)],
        out_specs=(vmem(), vmem(), vmem()),
        scratch_shapes=[pltpu.VMEM((12, 96, 1024), BF16), pltpu.VMEM((10, 96, 1024), BF16)],
        compiler_params=pltpu.CompilerParams(vmem_limit_bytes=14 * 2**20),
        cost_estimate=pl.CostEstimate(flops=2 * 10 * 288 * 96 * 1024, bytes_accessed=2**21, transcendentals=0),
        name="filter_partial",
    )(where, a_rows, g_rows, sums, g_own, g_nbr, a_nbr, after)


def finish_kernel(factor, where, mine, other, weight_out, bias_out):
    col, core = where[1], where[2]
    lane = iota((224, 128), 1)
    tables = []
    for x in range(2):
        which = jnp.where(col == x, 0, 1)
        a, b = mine[which], other[which]
        low, high = jnp.where(core == 0, a, b), jnp.where(core == 0, b, a)
        tables.append(jnp.concatenate([low, high], axis=0) * factor)
    even = (lane & 16) == 0
    first = jnp.where(even, tables[0], pltpu.roll(tables[1], 16, 1))
    second = jnp.where(even, pltpu.roll(tables[0], 112, 1), tables[1])
    whole = []
    for dx in range(4):
        left = pltpu.roll(first, 128 - 32 * dx, 1) if dx else first
        right = pltpu.roll(second, (160 - 32 * dx) % 128, 1) if dx != 1 else second
        whole.append(jnp.where(lane < 32, left, right))
    for nine in range(9):
        for dx in range(3):
            k = 9 * (nine // 3) + 3 * (nine % 3) + dx
            if nine < 6:
                weight_out[k] = whole[dx][32 * nine : 32 * nine + 32, 0:64]
            elif nine == 6:
                weight_out[k, 0:24] = whole[dx][192:216, 0:64]
                weight_out[k, 24:32] = whole[3][72 * dx : 72 * dx + 8, 0:64]
            else:
                at = 72 * dx + 32 * nine - 216
                weight_out[k] = whole[3][at : at + 32, 0:64]
    bias_out[...] = whole[0][216:217, 0:64]


def finish(where, mine, other, factor):
    return pl.pallas_call(
        functools.partial(finish_kernel, factor),
        out_shape=(jax.ShapeDtypeStruct((27, 32, 64), F32), jax.ShapeDtypeStruct((1, 64), F32)),
        in_specs=[smem(), vmem(), vmem()],
        out_specs=(vmem(), vmem()),
        compiler_params=pltpu.CompilerParams(vmem_limit_bytes=4 * 2**20),
        cost_estimate=pl.CostEstimate(flops=2**18, bytes_accessed=2**20, transcendentals=0),
        name="filter_finish",
    )(where, mine, other)


def spread_kernel(where, weight, out):
    place = 2 * where[0] + where[1]
    column = iota((64, 512), 1)
    block = column >> 7
    partner = jnp.where(block == 0, 0, jnp.where(block == 1, 2, jnp.where(block == 2, 1, 3)))
    slab = jnp.bitwise_xor(partner, place)
    repeat = one(iota((64, 512), 0) == 16 * slab + ((column & 127) >> 3))
    gap = iota((8, 128), 0) - (iota((8, 128), 1) & 7)
    masks = [gap == dy - 1 for dy in range(3)]
    for dz in range(3):
        for dx in range(3):
            wides = [
                jnp.dot(weight[9 * dz + 3 * dy + dx], repeat, preferred_element_type=F32) for dy in range(3)
            ]
            for m in range(4):
                cut = slice(128 * m, 128 * m + 128)
                band = jnp.zeros((32, 8, 128), F32)
                for dy in range(3):
                    w = jnp.broadcast_to(wides[dy][:, cut].reshape(32, 1, 128), (32, 8, 128))
                    band = jnp.where(jnp.broadcast_to(masks[dy][None], (32, 8, 128)), w, band)
                out[dx, :, 512 * dz + 128 * m : 512 * dz + 128 * m + 128] = band.reshape(256, 128).astype(BF16)


def spread_filters(where, weight):
    return pl.pallas_call(
        spread_kernel,
        out_shape=jax.ShapeDtypeStruct((3, 256, 1536), BF16),
        in_specs=[smem(), vmem()],
        out_specs=vmem(),
        compiler_params=pltpu.CompilerParams(vmem_limit_bytes=8 * 2**20),
        cost_estimate=pl.CostEstimate(flops=2 * 27 * 256 * 64 * 512, bytes_accessed=2**21, transcendentals=0),
        name="spread_filters",
    )(where, weight)


def input_kernel(where, spread, g_own, g_nbr, g_far, out, stack):
    row, col = where[0], where[1]
    offset = row + col
    lane = iota((256, 128), 1)
    for index in range(-1, 5):
        at = offset + index
        inside = (at >= 0) & (at < 6)
        at = jnp.clip(at, 0, 5)
        parts = [
            g_own[:, 7 * row + 3 * col + at].reshape(128, 128),
            g_nbr[:, 3 * col + at].reshape(128, 128),
            g_far[:, at].reshape(256, 128),
        ]
        for part, first in zip(parts, (0, 128, 256)):
            if index in (-1, 4):
                part = jnp.where(inside, part, jnp.zeros_like(part))
            for dz in range(3):
                z = index + dz - 1
                if 0 <= z < 4:
                    stack[512 * dz + first : 512 * dz + first + part.shape[0], 128 * z : 128 * z + 128] = part
    sums = [jnp.dot(spread[dx], stack[...], preferred_element_type=F32) for dx in range(3)]
    for z in range(4):
        cut = slice(128 * z, 128 * z + 128)
        value = sums[1][:, cut]
        value = value + jnp.where(lane == 127, 0.0, pltpu.roll(sums[0][:, cut], 127, 1))
        value = value + jnp.where(lane == 0, 0.0, pltpu.roll(sums[2][:, cut], 1, 1))
        out[:, z] = value.astype(BF16).reshape(32, 8, 128)


def input_gradient(where, spread, g_own, g_nbr, g_far):
    return pl.pallas_call(
        input_kernel,
        out_shape=jax.ShapeDtypeStruct((32, 4, 8, 128), BF16),
        in_specs=[smem()] + [vmem()] * 4,
        out_specs=vmem(),
        scratch_shapes=[pltpu.VMEM((1536, 512), BF16)],
        compiler_params=pltpu.CompilerParams(vmem_limit_bytes=14 * 2**20),
        cost_estimate=pl.CostEstimate(flops=2 * 9 * 256 * 512 * 512, bytes_accessed=2**22, transcendentals=0),
        name="input_gradient",
    )(where, spread, g_own, g_nbr, g_far)


def swap(block, axis, bits):
    count = lax.axis_size(axis)
    return lax.ppermute(block, axis, [(i, i ^ bits) for i in range(count)])


def line_kernel(chip, two, four, six, after, out):
    out[...] = (chip[...] + two[...]) + (four[...] + six[...])


def line_sum(chip, two, four, six, after):
    return pl.pallas_call(
        line_kernel,
        out_shape=jax.ShapeDtypeStruct(chip.shape, F32),
        in_specs=[vmem()] * 4 + [pl.BlockSpec(memory_space=pl.ANY)],
        out_specs=vmem(),
        compiler_params=pltpu.CompilerParams(vmem_limit_bytes=2**20),
        cost_estimate=pl.CostEstimate(flops=2**16, bytes_accessed=2**18, transcendentals=0),
        name="line_sum",
    )(chip, two, four, six, after)


def slab_kernel(line, across, beside, diagonal, after, out):
    out[0] = line[...] + across[...]
    out[1] = beside[...] + diagonal[...]


def slab_sum(line, across, beside, diagonal, after):
    return pl.pallas_call(
        slab_kernel,
        out_shape=jax.ShapeDtypeStruct((2,) + line.shape, F32),
        in_specs=[vmem()] * 4 + [pl.BlockSpec(memory_space=pl.ANY)],
        out_specs=vmem(),
        compiler_params=pltpu.CompilerParams(vmem_limit_bytes=2**20),
        cost_estimate=pl.CostEstimate(flops=2**16, bytes_accessed=2**18, transcendentals=0),
        name="slab_sum",
    )(line, across, beside, diagonal, after)


def local_grid(activations, grad_out, weight):
    slab = lax.axis_index("slab")
    row, col = slab // 2, slab % 2
    core = lax.axis_index("sample") % 2
    where = jnp.stack([row, col, core]).astype(jnp.int32)
    act = activations[0]
    g_own = grad_out[0]

    a_nbr = swap(act, "slab", 1)
    g_nbr = swap(lax.dynamic_slice_in_dim(g_own, 7 * (1 - row), 9, axis=1), "slab", 2)
    a_rows, g_rows, sums = near_rows(where, g_own, act)
    spread = spread_filters(where, jnp.swapaxes(weight, 1, 2))

    keep, send, g_pass = filter_partial(where, a_rows, g_rows, sums, g_own, g_nbr, a_nbr, spread)
    g_far = swap(g_pass, "slab", 1)
    chip = keep + swap(send, "sample", 1)
    line = line_sum(chip, swap(chip, "sample", 2), swap(chip, "sample", 4), swap(chip, "sample", 6), g_far)
    grad_in = input_gradient(where, spread, g_own, g_nbr, g_far)
    mine = slab_sum(line, swap(line, "slab", 2), swap(line, "slab", 1), swap(line, "slab", 3), grad_in)
    other = swap(mine, "sample", 1)
    cells = 8 * 128 * 4 * lax.axis_size("slab") * lax.axis_size("sample")
    grad_weight, grad_bias = finish(where, mine, other, 1.0 / math.sqrt(cells))
    return grad_in[None], jnp.swapaxes(grad_weight, 1, 2), grad_bias.reshape(64)


def with_halo(block, sides, width):
    for axis, dim in sides:
        count = lax.axis_size(axis)
        forward = [(i, i + 1) for i in range(count - 1)]
        backward = [(target, source) for source, target in forward]
        low = lax.ppermute(
            lax.slice_in_dim(block, block.shape[dim] - width, None, axis=dim), axis, forward
        )
        high = lax.ppermute(lax.slice_in_dim(block, 0, width, axis=dim), axis, backward)
        block = jnp.concatenate([low, block, high], axis=dim)
    return block


def offsets_list():
    return [
        (shift_z, shift_y, shift_x)
        for shift_z in (-1, 0, 1)
        for shift_y in (-1, 0, 1)
        for shift_x in (-1, 0, 1)
    ]


def local_any(activations, grad_out, weight):
    samples, in_chan, planes, y_cells, x_cells = activations.shape
    slabs = lax.axis_size("slab")
    regrouped = lax.all_to_all(grad_out, "slab", split_axis=2, concat_axis=1, tiled=True)
    g_ext = with_halo(regrouped, (("slab", 2),), 1)
    widths = ((0, 0), (0, 0), (0, 0), (1, 1), (1, 1))
    padded_co = jnp.pad(g_ext, widths)
    grad_in = jnp.zeros((samples, in_chan, planes, y_cells, x_cells), F32)
    pieces = []
    for offset, (shift_z, shift_y, shift_x) in enumerate(offsets_list()):
        moved_co = padded_co[
            :,
            :,
            1 - shift_z : 1 - shift_z + planes,
            1 - shift_y : 1 - shift_y + y_cells,
            1 - shift_x : 1 - shift_x + x_cells,
        ]
        pieces.append(jnp.einsum("sozyx,sizyx->oi", moved_co, activations, preferred_element_type=F32))
        grad_in = grad_in + jnp.einsum("oi,sozyx->sizyx", weight[offset], moved_co, preferred_element_type=F32)
    wpart = jnp.stack(pieces)
    bpart = jnp.sum(regrouped.astype(F32), axis=(0, 2, 3, 4))
    wtotal, btotal = lax.psum((wpart, bpart), ("slab", "sample"))
    all_cells = samples * lax.axis_size("sample") * planes * slabs * y_cells * x_cells
    factor = 1.0 / math.sqrt(all_cells)
    return (grad_in.astype(BF16), wtotal * factor, btotal * factor)


def local(activations, grad_out, weight):
    grid = (
        lax.axis_size("slab") == 4
        and lax.axis_size("sample") == 8
        and activations.shape == (1, 32, 4, 8, 128)
        and grad_out.shape == (1, 16, 16, 8, 128)
    )
    return (local_grid if grid else local_any)(activations, grad_out, weight)


def solution(mesh):
    placed = (P("sample", None, "slab", None, None), P("sample", "slab", None, None, None), P())
    return jax.shard_map(
        local,
        mesh=mesh,
        in_specs=placed,
        out_specs=(P("sample", None, "slab", None, None), P(), P()),
        check_vma=False,
    )
```

time: 60.3 us -> 38.3 us (0.64)
  waiting for transfers between devices: 20.6 us -> 7.17 us
  Pallas kernels: 16.1 us -> 11.2 us
  local copies, waits for them, and re-layouts: 7.28 us -> 4.92 us
  other arithmetic: 0.93 us -> 0.08 us
    ppermute x11, waiting for transfers between devices: 20.6 us -> 7.17 us  [swap(): return lax.ppermute(block, axis, [(i, i ^ bits) for i in range(count)])]
    pallas_call x2 -> x5, Pallas kernels: 10.6 us -> 6.66 us  [the longest x1 2.93 us: filter_partial(): pl.pallas_call(filter_kernel, out_shape=(jax.ShapeDtypeStruct((112, 128),...]
    unnamed x20 -> x10, local copies, waits for them, and re-layouts: 6.24 us -> 3.88 us
    concatenate x1 -> x0, other arithmetic: 0.8 us -> none  [local_grid(): jnp.concatenate([lax.dynamic_slice_in_dim(g_own, 7 * row + 3 * (1 - col),...]
  transfers between devices with their start and end apart: 11 -> 11, of which waited for: 6 -> 4; matrix products, arithmetic and copies ran while one was open for 6% -> 0% of each run, Pallas kernels for 14% -> 17%
where the time goes in v2:
time: 38.3 us; the launch traced here: 38 us
  starting transfers between devices  13.9 us (36%)
  Pallas kernels  11.2 us (29%)
  waiting for transfers between devices  7.17 us (19%)
  local copies, waits for them, and re-layouts  4.92 us (13%)
  between operations  0.75 us (2%)
    ppermute x11, starting transfers between devices, swap(): return lax.ppermute(block, axis, [(i, i ^ bits) for i in range(count)])  13.9 us
    ppermute x11, waiting for transfers between devices, swap(): return lax.ppermute(block, axis, [(i, i ^ bits) for i in range(count)])  7.17 us
    unnamed x10, local copies, waits for them, and re-layouts  3.88 us
    pallas_call x1, Pallas kernels, filter_partial(): pl.pallas_call(filter_kernel, out_shape=(jax.ShapeDtypeStruct((112, 128),...  2.93 us
    pallas_call x1, Pallas kernels, input_gradient(): pl.pallas_call(input_kernel, out_shape=jax.ShapeDtypeStruct((32, 4, 8, 12...  2.91 us
    pallas_call x1, Pallas kernels, spread_filters(): pl.pallas_call(spread_kernel, out_shape=jax.ShapeDtypeStruct((3, 256, 153...  2.68 us
    pallas_call x1, Pallas kernels, finish(): pl.pallas_call(functools.partial(finish_kernel, factor), out_shape=(jax.S...  1.65 us
    dynamic_slice x1, local copies, waits for them, and re-layouts, local_grid(): lax.dynamic_slice_in_dim(g_own, 7 * (1 - row), 9, axis=1)  1.05 us
  transfers between devices with their start and end apart: 11, of which 4 were waited for; matrix products, arithmetic and copies ran while one was open for 0% of the time, Pallas kernels for 17%

profile of v2, /device:TPU:0, one launch (start us, length us, event | category | flops | bytes accessed | tf_op | source)
XLA Modules:
  0.0 38.0 jit_solution(3854446290088704091)
XLA Ops:
  0.6 0.0 copy-start.1
  0.7 1.0 %dynamic-slice_bitcast_fusion = bf16[16,9,8,128]{3,2,1,0:T(8,128)(2,1)S(1)} fusion(bf16[1,16,16,8,128]{4,3,2,1,0:T(8,128)(2,1)} %param.4, s32[]{:T(128)S(6)} %select_n.21), kind=kLoop, calls=%fused_computation | loop fusion | bytes 589828 | tf_op jit(solution)/shard_map/dynamic_slice | solution.py:326
  1.7 3.0 %collective-permute-start = (bf16[16,9,8,128]{3,2,1,0:T(8,128)(2,1)S(1)}, bf16[16,9,8,128]{3,2,1,0:T(8,128)(2,1)S(1)}, u32[]{:S(2)}, u32[]{:S(2)}) collective-permute-start(bf16[16,9,8,128]{3,2,1,0:T(8,128)(2,1)S(1)} %dynamic-slice_bitcast_fusion), channel_id=1, source_target_pairs={{0,16},{8,24},{16,0},{24,8},{1,17},{9,25},{17,1},{25,9},{2,18},{10... | collective-permute-start | bytes 884744 | tf_op jit(solution)/shard_map/ppermute | solution.py:281
  4.7 1.5 %collective-permute-start.1 = (bf16[32,4,8,128]{3,2,1,0:T(8,128)(2,1)}, bf16[32,4,8,128]{3,2,1,0:T(8,128)(2,1)S(1)}, u32[]{:S(2)}, u32[]{:S(2)}) collective-permute-start(bf16[32,4,8,128]{3,2,1,0:T(8,128)(2,1)} %bitcast.16), channel_id=1, source_target_pairs={{0,8},{8,0},{16,24},{24,16},{1,9},{9,1},{17,25},{25,17},{2,10},{10... | collective-permute-start | bytes 786440 | tf_op jit(solution)/shard_map/ppermute | solution.py:281
  6.2 0.1 pad_add_fusion.where
  6.3 0.0 copy-start
  6.3 1.0 %copy-done = bf16[1,16,16,8,128]{4,3,2,1,0:T(8,128)(2,1)S(1)} copy-done((bf16[1,16,16,8,128]{4,3,2,1,0:T(8,128)(2,1)S(1)}, bf16[1,16,16,8,128]{4,3,2,1,0:T(8,128)(2,1)}, u32[]{:S(2)}) %copy-start) | copy-done | bytes 524312
  7.4 0.0 copy-start.4
  7.4 0.9 %copy-done.4 = bf16[1,32,4,8,128]{4,3,2,1,0:T(8,128)(2,1)S(1)} copy-done((bf16[1,32,4,8,128]{4,3,2,1,0:T(8,128)(2,1)S(1)}, bf16[1,32,4,8,128]{4,3,2,1,0:T(8,128)(2,1)}, u32[]{:S(2)}) %copy-start.4) | copy-done | bytes 262168
  8.3 1.0 %near_rows.1 = (bf16[4,96,1024]{2,1,0:T(8,128)(2,1)S(1)}, bf16[9,48,1024]{2,1,0:T(8,128)(2,1)S(1)}, f32[16,128]{1,0:T(8,128)S(1)}) custom-call(s32[3]{0:T(128)S(1)} %pad_add_fusion.where, bf16[16,16,8,128]{3,2,1,0:T(8,128)(2,1)S(1)} %bitcast.11, bf16[32,4,8,128]{3,2,1,0:T(8,128)(2,1)S(1)} %bitcast.17), custom_call_target="tpu_custom_call" | custom-call | flops 268435456 | bytes 2097152 | tf_op jit(solution)/shard_map/near_rows/pallas_call | solution.py:85
  9.3 0.0 copy-start.3
  9.3 0.9 %copy-done.3 = bf16[27,64,32]{1,2,0:T(8,128)(2,1)S(1)} copy-done((bf16[27,64,32]{1,2,0:T(8,128)(2,1)S(1)}, bf16[27,64,32]{1,2,0:T(8,128)(2,1)}, u32[]{:S(2)}) %copy-start.3) | copy-done | bytes 110616
  10.3 2.7 %spread_filters.1.after.spread = bf16[3,256,1536]{2,1,0:T(8,128)(2,1)S(1)} custom-call(s32[3]{0:T(128)S(1)} %pad_add_fusion.where, bf16[27,32,64]{2,1,0:T(8,128)(2,1)S(1)} %bitcast.15), custom_call_target="tpu_custom_call" | custom-call | flops 452984832 | bytes 2097152 | tf_op jit(solution)/shard_map/spread_filters/pallas_call | solution.py:226
  13.0 0.0 collective-permute-done.1.a_nbr
  13.0 0.0 collective-permute-done.g_nbr
  13.0 0.0 copy-done.1
  13.0 2.9 %filter_partial.1 = (f32[112,128]{1,0:T(8,128)S(1)}, f32[112,128]{1,0:T(8,128)S(1)}, bf16[32,6,8,128]{3,2,1,0:T(8,128)(2,1)S(1)}) custom-call(s32[3]{0:T(128)S(1)} %pad_add_fusion.where, bf16[4,96,1024]{2,1,0:T(8,128)(2,1)S(1)} %get-tuple-element.11.a_rows, bf16[9,48,1024]{2,1,0:T(8,128)(2,1)S(1)} %get-tuple-element.12.g_rows, ...), custom_call_target="tpu_custom_call" | custom-call | flops 566231040 | bytes 2097152 | tf_op jit(solution)/shard_map/filter_partial/pallas_call | solution.py:147
  15.9 1.3 %collective-permute-start.2 = (bf16[32,6,8,128]{3,2,1,0:T(8,128)(2,1)S(1)}, bf16[32,6,8,128]{3,2,1,0:T(8,128)(2,1)S(1)}, u32[]{:S(2)}, u32[]{:S(2)}) collective-permute-start(bf16[32,6,8,128]{3,2,1,0:T(8,128)(2,1)S(1)} %get-tuple-element.14), channel_id=1, source_target_pairs={{0,8},{8,0},{16,24},{24,16},{1,9},{9,1},{17,25},{25,17},{2,10},{10... | collective-permute-start | bytes 1179656 | tf_op jit(solution)/shard_map/ppermute | solution.py:281
  17.2 0.0 collective-permute-start.3
  17.2 1.2 %collective-permute-done.3 = f32[112,128]{1,0:T(8,128)S(1)} collective-permute-done((f32[112,128]{1,0:T(8,128)S(1)}, f32[112,128]{1,0:T(8,128)S(1)}, u32[]{:S(2)}, u32[]{:S(2)}) %collective-permute-start.3) | collective-permute-done | bytes 57376 | tf_op jit(solution)/shard_map/ppermute | solution.py:281
  18.5 3.7 %collective-permute-start.6 = (f32[112,128]{1,0:T(8,128)S(1)}, f32[112,128]{1,0:T(8,128)S(1)}, u32[]{:S(2)}, u32[]{:S(2)}) collective-permute-start(f32[112,128]{1,0:T(8,128)S(1)} %add.17.chip), channel_id=1, source_target_pairs={{0,6},{1,7},{2,4},{3,5},{4,2},{5,3},{6,0},{7,1},{8,14},{9,15},{10,... | collective-permute-start | bytes 172040 | tf_op jit(solution)/shard_map/ppermute | solution.py:281
  22.1 0.0 collective-permute-start.5
  22.1 0.8 %collective-permute-start.4 = (f32[112,128]{1,0:T(8,128)S(1)}, f32[112,128]{1,0:T(8,128)S(1)}, u32[]{:S(2)}, u32[]{:S(2)}) collective-permute-start(f32[112,128]{1,0:T(8,128)S(1)} %add.17.chip), channel_id=1, source_target_pairs={{0,2},{1,3},{2,0},{3,1},{4,6},{5,7},{6,4},{7,5},{8,10},{9,11},{10,... | collective-permute-start | bytes 172040 | tf_op jit(solution)/shard_map/ppermute | solution.py:281
  22.9 1.8 %collective-permute-done.6.six = f32[112,128]{1,0:T(8,128)S(1)} collective-permute-done((f32[112,128]{1,0:T(8,128)S(1)}, f32[112,128]{1,0:T(8,128)S(1)}, u32[]{:S(2)}, u32[]{:S(2)}) %collective-permute-start.6) | collective-permute-done | bytes 57376 | tf_op jit(solution)/shard_map/ppermute | solution.py:281
  24.7 2.8 %collective-permute-done.5.four = f32[112,128]{1,0:T(8,128)S(1)} collective-permute-done((f32[112,128]{1,0:T(8,128)S(1)}, f32[112,128]{1,0:T(8,128)S(1)}, u32[]{:S(2)}, u32[]{:S(2)}) %collective-permute-start.5) | collective-permute-done | bytes 57376 | tf_op jit(solution)/shard_map/ppermute | solution.py:281
  27.5 0.0 collective-permute-done.4.two
  27.5 0.0 collective-permute-done.2.g_far.after
  27.5 0.8 %collective-permute-start.9 = (f32[112,128]{1,0:T(8,128)S(1)}, f32[112,128]{1,0:T(8,128)S(1)}, u32[]{:S(2)}, u32[]{:S(2)}) collective-permute-start(f32[112,128]{1,0:T(8,128)S(1)} %line_sum.1.line), channel_id=1, source_target_pairs={{0,24},{8,16},{16,8},{24,0},{1,25},{9,17},{17,9},{25,1},{2,26},{10... | collective-permute-start | bytes 172040 | tf_op jit(solution)/shard_map/ppermute | solution.py:281
  28.4 1.5 %collective-permute-start.8 = (f32[112,128]{1,0:T(8,128)S(1)}, f32[112,128]{1,0:T(8,128)S(1)}, u32[]{:S(2)}, u32[]{:S(2)}) collective-permute-start(f32[112,128]{1,0:T(8,128)S(1)} %line_sum.1.line), channel_id=1, source_target_pairs={{0,8},{8,0},{16,24},{24,16},{1,9},{9,1},{17,25},{25,17},{2,10},{10... | collective-permute-start | bytes 172040 | tf_op jit(solution)/shard_map/ppermute | solution.py:281
  29.8 1.3 %collective-permute-start.7 = (f32[112,128]{1,0:T(8,128)S(1)}, f32[112,128]{1,0:T(8,128)S(1)}, u32[]{:S(2)}, u32[]{:S(2)}) collective-permute-start(f32[112,128]{1,0:T(8,128)S(1)} %line_sum.1.line), channel_id=1, source_target_pairs={{0,16},{8,24},{16,0},{24,8},{1,17},{9,25},{17,1},{25,9},{2,18},{10... | collective-permute-start | bytes 172040 | tf_op jit(solution)/shard_map/ppermute | solution.py:281
  31.1 2.9 %input_gradient.1.after = bf16[32,4,8,128]{3,2,1,0:T(8,128)(2,1)} custom-call(s32[3]{0:T(128)S(1)} %pad_add_fusion.where, bf16[3,256,1536]{2,1,0:T(8,128)(2,1)S(1)} %spread_filters.1.after.spread, bf16[16,16,8,128]{3,2,1,0:T(8,128)(2,1)S(1)} %bitcast.13, bf16[16,9,8,128]{3,2,1,0:T(8,128)(2,1)S(1)} %collective-permute-done.g_nbr, ...), custom_call_target="tpu_custom_call" | custom-call | flops 1207959552 | bytes 4194304 | tf_op jit(solution)/shard_map/input_gradient/pallas_call | solution.py:267
  34.0 0.0 collective-permute-done.9.diagonal
  34.0 0.0 collective-permute-done.8.beside
  34.0 0.0 collective-permute-done.7.across
  34.0 0.0 copy-start.2
  34.0 0.9 %copy-done.2 = bf16[32,4,8,128]{3,2,1,0:T(8,128)(2,1)S(1)} copy-done((bf16[32,4,8,128]{3,2,1,0:T(8,128)(2,1)S(1)}, bf16[32,4,8,128]{3,2,1,0:T(8,128)(2,1)}, u32[]{:S(2)}) %copy-start.2) | copy-done | bytes 262168
  35.0 0.1 collective-permute-start.10
  35.1 1.3 %collective-permute-done.10.other = f32[2,112,128]{2,1,0:T(8,128)S(1)} collective-permute-done((f32[2,112,128]{2,1,0:T(8,128)S(1)}, f32[2,112,128]{2,1,0:T(8,128)S(1)}, u32[]{:S(2)}, u32[]{:S(2)}) %collective-permute-start.10) | collective-permute-done | bytes 114720 | tf_op jit(solution)/shard_map/ppermute | solution.py:281
  36.4 1.6 %filter_finish.1 = (f32[27,32,64]{2,1,0:T(8,128)}, f32[1,64]{1,0:T(1,128)}) custom-call(s32[3]{0:T(128)S(1)} %pad_add_fusion.where, f32[2,112,128]{2,1,0:T(8,128)S(1)} %slab_sum.1.mine, f32[2,112,128]{2,1,0:T(8,128)S(1)} %collective-permute-done.10.other), custom_call_target="tpu_custom_call" | custom-call | flops 262144 | bytes 1048576 | tf_op jit(solution)/shard_map/filter_finish/pallas_call | solution.py:191
  (3 shorter events, 0.0 us)
Async XLA Ops:
  0.6 12.3 %copy-start.1 = (bf16[1,16,16,8,128]{4,3,2,1,0:T(8,128)(2,1)S(1)}, bf16[1,16,16,8,128]{4,3,2,1,0:T(8,128)(2,1)}, u32[]{:S(2)}) copy-start(bf16[1,16,16,8,128]{4,3,2,1,0:T(8,128)(2,1)} %param.4) | copy-start | bytes 1572868
  1.7 11.3 %collective-permute-start = (bf16[16,9,8,128]{3,2,1,0:T(8,128)(2,1)S(1)}, bf16[16,9,8,128]{3,2,1,0:T(8,128)(2,1)S(1)}, u32[]{:S(2)}, u32[]{:S(2)}) collective-permute-start(bf16[16,9,8,128]{3,2,1,0:T(8,128)(2,1)S(1)} %dynamic-slice_bitcast_fusion), channel_id=1, source_target_pairs={{0,16},{8,24},{16,0},{24,8},{1,17},{9,25},{17,1},{25,9},{2,18},{10... | collective-permute-start | bytes 884744 | tf_op jit(solution)/shard_map/ppermute | solution.py:281
  4.7 8.2 %collective-permute-start.1 = (bf16[32,4,8,128]{3,2,1,0:T(8,128)(2,1)}, bf16[32,4,8,128]{3,2,1,0:T(8,128)(2,1)S(1)}, u32[]{:S(2)}, u32[]{:S(2)}) collective-permute-start(bf16[32,4,8,128]{3,2,1,0:T(8,128)(2,1)} %bitcast.16), channel_id=1, source_target_pairs={{0,8},{8,0},{16,24},{24,16},{1,9},{9,1},{17,25},{25,17},{2,10},{10... | collective-permute-start | bytes 786440 | tf_op jit(solution)/shard_map/ppermute | solution.py:281
  6.3 1.0 %copy-start = (bf16[1,16,16,8,128]{4,3,2,1,0:T(8,128)(2,1)S(1)}, bf16[1,16,16,8,128]{4,3,2,1,0:T(8,128)(2,1)}, u32[]{:S(2)}) copy-start(bf16[1,16,16,8,128]{4,3,2,1,0:T(8,128)(2,1)} %param.4) | copy-start | bytes 1572868
  7.4 0.9 %copy-start.4 = (bf16[1,32,4,8,128]{4,3,2,1,0:T(8,128)(2,1)S(1)}, bf16[1,32,4,8,128]{4,3,2,1,0:T(8,128)(2,1)}, u32[]{:S(2)}) copy-start(bf16[1,32,4,8,128]{4,3,2,1,0:T(8,128)(2,1)} %param.3) | copy-start | bytes 786436
  9.3 0.9 %copy-start.3 = (bf16[27,64,32]{1,2,0:T(8,128)(2,1)S(1)}, bf16[27,64,32]{1,2,0:T(8,128)(2,1)}, u32[]{:S(2)}) copy-start(bf16[27,64,32]{1,2,0:T(8,128)(2,1)} %param.5) | copy-start | bytes 331780
  15.9 11.6 %collective-permute-start.2 = (bf16[32,6,8,128]{3,2,1,0:T(8,128)(2,1)S(1)}, bf16[32,6,8,128]{3,2,1,0:T(8,128)(2,1)S(1)}, u32[]{:S(2)}, u32[]{:S(2)}) collective-permute-start(bf16[32,6,8,128]{3,2,1,0:T(8,128)(2,1)S(1)} %get-tuple-element.14), channel_id=1, source_target_pairs={{0,8},{8,0},{16,24},{24,16},{1,9},{9,1},{17,25},{25,17},{2,10},{10... | collective-permute-start | bytes 1179656 | tf_op jit(solution)/shard_map/ppermute | solution.py:281
  17.2 1.2 %collective-permute-start.3 = (f32[112,128]{1,0:T(8,128)S(1)}, f32[112,128]{1,0:T(8,128)S(1)}, u32[]{:S(2)}, u32[]{:S(2)}) collective-permute-start(f32[112,128]{1,0:T(8,128)S(1)} %get-tuple-element.16), channel_id=1, source_target_pairs={{0,1},{1,0},{2,3},{3,2},{4,5},{5,4},{6,7},{7,6},{8,9},{9,8},{10,11... | collective-permute-start | bytes 172040 | tf_op jit(solution)/shard_map/ppermute | solution.py:281
  18.5 6.2 %collective-permute-start.6 = (f32[112,128]{1,0:T(8,128)S(1)}, f32[112,128]{1,0:T(8,128)S(1)}, u32[]{:S(2)}, u32[]{:S(2)}) collective-permute-start(f32[112,128]{1,0:T(8,128)S(1)} %add.17.chip), channel_id=1, source_target_pairs={{0,6},{1,7},{2,4},{3,5},{4,2},{5,3},{6,0},{7,1},{8,14},{9,15},{10,... | collective-permute-start | bytes 172040 | tf_op jit(solution)/shard_map/ppermute | solution.py:281
  22.1 5.4 %collective-permute-start.5 = (f32[112,128]{1,0:T(8,128)S(1)}, f32[112,128]{1,0:T(8,128)S(1)}, u32[]{:S(2)}, u32[]{:S(2)}) collective-permute-start(f32[112,128]{1,0:T(8,128)S(1)} %add.17.chip), channel_id=1, source_target_pairs={{0,4},{1,5},{2,6},{3,7},{4,0},{5,1},{6,2},{7,3},{8,12},{9,13},{10,... | collective-permute-start | bytes 172040 | tf_op jit(solution)/shard_map/ppermute | solution.py:281
  22.1 5.4 %collective-permute-start.4 = (f32[112,128]{1,0:T(8,128)S(1)}, f32[112,128]{1,0:T(8,128)S(1)}, u32[]{:S(2)}, u32[]{:S(2)}) collective-permute-start(f32[112,128]{1,0:T(8,128)S(1)} %add.17.chip), channel_id=1, source_target_pairs={{0,2},{1,3},{2,0},{3,1},{4,6},{5,7},{6,4},{7,5},{8,10},{9,11},{10,... | collective-permute-start | bytes 172040 | tf_op jit(solution)/shard_map/ppermute | solution.py:281
  27.5 6.5 %collective-permute-start.9 = (f32[112,128]{1,0:T(8,128)S(1)}, f32[112,128]{1,0:T(8,128)S(1)}, u32[]{:S(2)}, u32[]{:S(2)}) collective-permute-start(f32[112,128]{1,0:T(8,128)S(1)} %line_sum.1.line), channel_id=1, source_target_pairs={{0,24},{8,16},{16,8},{24,0},{1,25},{9,17},{17,9},{25,1},{2,26},{10... | collective-permute-start | bytes 172040 | tf_op jit(solution)/shard_map/ppermute | solution.py:281
  28.4 5.7 %collective-permute-start.8 = (f32[112,128]{1,0:T(8,128)S(1)}, f32[112,128]{1,0:T(8,128)S(1)}, u32[]{:S(2)}, u32[]{:S(2)}) collective-permute-start(f32[112,128]{1,0:T(8,128)S(1)} %line_sum.1.line), channel_id=1, source_target_pairs={{0,8},{8,0},{16,24},{24,16},{1,9},{9,1},{17,25},{25,17},{2,10},{10... | collective-permute-start | bytes 172040 | tf_op jit(solution)/shard_map/ppermute | solution.py:281
  29.8 4.2 %collective-permute-start.7 = (f32[112,128]{1,0:T(8,128)S(1)}, f32[112,128]{1,0:T(8,128)S(1)}, u32[]{:S(2)}, u32[]{:S(2)}) collective-permute-start(f32[112,128]{1,0:T(8,128)S(1)} %line_sum.1.line), channel_id=1, source_target_pairs={{0,16},{8,24},{16,0},{24,8},{1,17},{9,25},{17,1},{25,9},{2,18},{10... | collective-permute-start | bytes 172040 | tf_op jit(solution)/shard_map/ppermute | solution.py:281
  34.0 1.0 %copy-start.2 = (bf16[32,4,8,128]{3,2,1,0:T(8,128)(2,1)S(1)}, bf16[32,4,8,128]{3,2,1,0:T(8,128)(2,1)}, u32[]{:S(2)}) copy-start(bf16[32,4,8,128]{3,2,1,0:T(8,128)(2,1)} %input_gradient.1.after) | copy-start | bytes 786436
  35.0 1.4 %collective-permute-start.10 = (f32[2,112,128]{2,1,0:T(8,128)S(1)}, f32[2,112,128]{2,1,0:T(8,128)S(1)}, u32[]{:S(2)}, u32[]{:S(2)}) collective-permute-start(f32[2,112,128]{2,1,0:T(8,128)S(1)} %slab_sum.1.mine), channel_id=1, source_target_pairs={{0,1},{1,0},{2,3},{3,2},{4,5},{5,4},{6,7},{7,6},{8,9},{9,8},{10,11... | collective-permute-start | bytes 344072 | tf_op jit(solution)/shard_map/ppermute | solution.py:281

commit v3 on v2

v3 whole, which is shorter than its diff:
```python
import functools
import math

import jax
import jax.numpy as jnp
from jax import lax
from jax.experimental import pallas as pl
from jax.experimental.pallas import tpu as pltpu
from jax.sharding import PartitionSpec as P

F32 = jnp.float32
BF16 = jnp.bfloat16
NT = (((1,), (1,)), ((), ()))


def iota(shape, dim):
    return lax.broadcasted_iota(jnp.int32, shape, dim)


def grid_place():
    slab = lax.axis_index("slab")
    return slab // 2, lax.rem(slab, 2), lax.rem(lax.axis_index("sample"), 2)


def vmem():
    return pl.BlockSpec(memory_space=pltpu.VMEM)


def anywhere():
    return pl.BlockSpec(memory_space=pl.ANY)


def one(mask):
    return mask.astype(F32).astype(BF16)


def turn_planes(turned, shift_rows, store):
    pass


def act_rows(source, put):
    r, q = iota((256, 256), 0), iota((256, 256), 1)
    perm = one(((q & 7) == (r >> 5)) & ((q >> 3) == (r & 31)))
    both = jnp.concatenate([source[:, plane].reshape(256, 128) for plane in range(4)], axis=1)
    turned = jnp.dot(perm, both, preferred_element_type=F32).astype(BF16)
    for plane in range(4):
        for y in range(8):
            put(plane, y, turned[32 * y : 32 * y + 32, 128 * plane : 128 * plane + 128])


def cot_rows(source, first, row, put):
    r, q = iota((128, 128), 0), iota((128, 128), 1)
    perm = one(((q & 7) == (r >> 4)) & ((q >> 3) == (r & 15)))
    lane = iota((128, 128), 1)
    total = jnp.zeros((16, 128), F32)
    for plane in range(9):
        turned = jnp.dot(perm, source[:, first + plane].reshape(128, 128), preferred_element_type=F32)
        moved = (
            jnp.where(lane == 127, 0.0, pltpu.roll(turned, 127, 1)),
            turned,
            jnp.where(lane == 0, 0.0, pltpu.roll(turned, 1, 1)),
        )
        for shift in range(3):
            packed = moved[shift].astype(BF16)
            for y in range(8):
                put(plane, shift, y, packed[16 * y : 16 * y + 16])
        cells = turned[0:16]
        for y in range(1, 8):
            cells = cells + turned[16 * y : 16 * y + 16]
        if plane == 0:
            cells = jnp.where(row == 0, cells, 0.0)
        if plane == 8:
            cells = jnp.where(row == 0, 0.0, cells)
        total = total + cells
    return total


def act_put(abuf, first):
    def put(plane, y, piece):
        abuf[first + plane, :, 128 * y + 128 : 128 * y + 256] = piece

    return put


def cot_put(gbuf, row, whose):
    def put(plane, shift, y, piece):
        rows = pl.ds(pl.multiple_of(32 * shift + 16 * whose, 16), 16)
        gbuf[plane + 1 - row, rows, 128 * y : 128 * y + 128] = piece

    return put


def near_kernel(g_own, a_own, abuf, gbuf, sums):
    row, col, _ = grid_place()
    for slot in range(12):
        if slot in (0, 1, 10, 11):
            abuf[slot] = jnp.zeros((32, 1280), BF16)
        else:
            abuf[slot, :, 0:128] = jnp.zeros((32, 128), BF16)
            abuf[slot, :, 1152:1280] = jnp.zeros((32, 128), BF16)
    for slot in range(10):
        gbuf[slot, 96:128] = jnp.zeros((32, 1024), BF16)
    gbuf[9 * row] = jnp.zeros((128, 1024), BF16)
    act_rows(a_own, act_put(abuf, 2 + 4 * col))
    sums[...] = cot_rows(g_own, 7 * row, row, cot_put(gbuf, row, row))


ROWS = (
    jax.ShapeDtypeStruct((12, 32, 1280), BF16),
    jax.ShapeDtypeStruct((10, 128, 1024), BF16),
)


def near_rows(g_own, a_own):
    return pl.pallas_call(
        near_kernel,
        out_shape=ROWS + (jax.ShapeDtypeStruct((16, 128), F32),),
        in_specs=[vmem(), vmem()],
        out_specs=(vmem(), vmem(), vmem()),
        compiler_params=pltpu.CompilerParams(vmem_limit_bytes=10 * 2**20),
        cost_estimate=pl.CostEstimate(flops=2**28, bytes_accessed=2**21, transcendentals=0),
        name="near_rows",
    )(g_own, a_own)


def filter_kernel(a_in, g_in, sums, g_nbr, a_nbr, abuf, gbuf, keep, send):
    row, col, core = grid_place()
    act_rows(a_nbr, act_put(abuf, 6 - 4 * col))
    far_sums = cot_rows(g_nbr, 0, row, cot_put(gbuf, row, 1 - row))
    wide = jnp.zeros((384, 256), F32)
    for slot in range(0, 10, 2):
        moved = [
            abuf[slot + plane, :, 128 * shift : 128 * shift + 1024] for plane in range(4) for shift in range(3)
        ]
        wide = wide + lax.dot_general(
            jnp.concatenate(moved, axis=0),
            gbuf[slot : slot + 2].reshape(256, 1024),
            NT,
            preferred_element_type=F32,
        )
    acc = wide[0:288, 0:128] + wide[96:384, 128:256]
    side = jnp.concatenate([acc[216:288, 32 * m : 32 * m + 32] for m in range(3)], axis=0)
    table = jnp.concatenate([acc[0:216, 0:96], side], axis=1)
    first = jnp.where(row == 0, sums[...], far_sums)
    second = jnp.where(row == 0, far_sums, sums[...])
    column = jnp.sum(jnp.concatenate([first, second], axis=0), axis=1, keepdims=True)
    line = jnp.sum(jnp.where(iota((32, 128), 0) == iota((32, 128), 1), column, 0.0), axis=0, keepdims=True)
    bias = jnp.where(iota((8, 128), 0) == 0, line, 0.0)
    low = table[0:112]
    high = jnp.concatenate([table[112:216], bias], axis=0)
    keep[...] = jnp.where(core == 0, low, high)
    send[...] = jnp.where(core == 0, high, low)


def filter_partial(a_rows, g_rows, sums, g_nbr, a_nbr):
    half = jax.ShapeDtypeStruct((112, 128), F32)
    return pl.pallas_call(
        filter_kernel,
        out_shape=ROWS + (half, half),
        in_specs=[vmem()] * 5,
        out_specs=(vmem(),) * 4,
        input_output_aliases={0: 0, 1: 1},
        compiler_params=pltpu.CompilerParams(vmem_limit_bytes=12 * 2**20),
        cost_estimate=pl.CostEstimate(flops=2 * 10 * 288 * 96 * 1024, bytes_accessed=2**21, transcendentals=0),
        name="filter_partial",
    )(a_rows, g_rows, sums, g_nbr, a_nbr)[2:]


def pass_kernel(g_own, g_nbr, after, out):
    row, col, _ = grid_place()
    for plane in range(6):
        out[0:16, plane] = g_own[:, 7 * row + 3 * (1 - col) + plane]
        out[16:32, plane] = g_nbr[:, 3 * (1 - col) + plane]


def pass_on(g_own, g_nbr, after):
    return pl.pallas_call(
        pass_kernel,
        out_shape=jax.ShapeDtypeStruct((32, 6, 8, 128), BF16),
        in_specs=[vmem(), vmem(), anywhere()],
        out_specs=vmem(),
        compiler_params=pltpu.CompilerParams(vmem_limit_bytes=4 * 2**20),
        cost_estimate=pl.CostEstimate(flops=2**30, bytes_accessed=2**23, transcendentals=0),
        name="pass_on",
    )(g_own, g_nbr, after)


def finish_kernel(factor, mine, other, weight_out, bias_out):
    _, col, core = grid_place()
    lane = iota((224, 128), 1)
    tables = []
    for x in range(2):
        which = jnp.where(col == x, 0, 1)
        a, b = mine[which], other[which]
        low, high = jnp.where(core == 0, a, b), jnp.where(core == 0, b, a)
        tables.append(jnp.concatenate([low, high], axis=0) * factor)
    even = (lane & 16) == 0
    first = jnp.where(even, tables[0], pltpu.roll(tables[1], 16, 1))
    second = jnp.where(even, pltpu.roll(tables[0], 112, 1), tables[1])
    whole = []
    for dx in range(4):
        left = pltpu.roll(first, 128 - 32 * dx, 1) if dx else first
        right = pltpu.roll(second, (160 - 32 * dx) % 128, 1) if dx != 1 else second
        whole.append(jnp.where(lane < 32, left, right))
    for nine in range(9):
        for dx in range(3):
            k = 3 * nine + dx
            if nine < 6:
                weight_out[k] = whole[dx][32 * nine : 32 * nine + 32, 0:64]
            elif nine == 6:
                weight_out[k, 0:24] = whole[dx][192:216, 0:64]
                weight_out[k, 24:32] = whole[3][72 * dx : 72 * dx + 8, 0:64]
            else:
                at = 72 * dx + 32 * nine - 216
                weight_out[k] = whole[3][at : at + 32, 0:64]
    bias_out[...] = whole[0][216:217, 0:64]


def finish(mine, other, factor):
    return pl.pallas_call(
        functools.partial(finish_kernel, factor),
        out_shape=(jax.ShapeDtypeStruct((27, 32, 64), F32), jax.ShapeDtypeStruct((1, 64), F32)),
        in_specs=[vmem(), vmem()],
        out_specs=(vmem(), vmem()),
        compiler_params=pltpu.CompilerParams(vmem_limit_bytes=4 * 2**20),
        cost_estimate=pl.CostEstimate(flops=2**18, bytes_accessed=2**20, transcendentals=0),
        name="filter_finish",
    )(mine, other)


def spread_kernel(weight, after, out):
    place = lax.axis_index("slab")
    column = iota((64, 512), 1)
    block = column >> 7
    partner = jnp.where(block == 0, 0, jnp.where(block == 1, 2, jnp.where(block == 2, 1, 3)))
    slab = jnp.bitwise_xor(partner, place)
    repeat = one(iota((64, 512), 0) == 16 * slab + ((column & 127) >> 3))
    gap = iota((8, 128), 0) - (iota((8, 128), 1) & 7)
    masks = [gap == dy - 1 for dy in range(3)]
    for dz in range(3):
        for dx in range(3):
            wides = [
                jnp.dot(weight[9 * dz + 3 * dy + dx], repeat, preferred_element_type=F32) for dy in range(3)
            ]
            for m in range(4):
                cut = slice(128 * m, 128 * m + 128)
                band = jnp.zeros((32, 8, 128), F32)
                for dy in range(3):
                    w = jnp.broadcast_to(wides[dy][:, cut].reshape(32, 1, 128), (32, 8, 128))
                    band = jnp.where(jnp.broadcast_to(masks[dy][None], (32, 8, 128)), w, band)
                first = 256 * dz + 128 * (m % 2)
                out[m // 2, dx, :, first : first + 128] = band.reshape(256, 128).astype(BF16)


def spread_filters(weight, after):
    return pl.pallas_call(
        spread_kernel,
        out_shape=jax.ShapeDtypeStruct((2, 3, 256, 768), BF16),
        in_specs=[vmem(), anywhere()],
        out_specs=vmem(),
        compiler_params=pltpu.CompilerParams(vmem_limit_bytes=8 * 2**20),
        cost_estimate=pl.CostEstimate(flops=2**33, bytes_accessed=2**25, transcendentals=0),
        name="spread_filters",
    )(weight, after)


def stack_planes(offset, parts, stack):
    for index in range(-1, 5):
        at = offset + index
        inside = (at >= 0) & (at < 6)
        at = jnp.clip(at, 0, 5)
        for source, place, first in parts:
            chans = source.shape[0]
            value = source[:, place + at].reshape(8 * chans, 128)
            if index in (-1, 4):
                value = jnp.where(inside, value, jnp.zeros_like(value))
            for dz in range(3):
                z = index + dz - 1
                if 0 <= z < 4:
                    stack[256 * dz + first : 256 * dz + first + 8 * chans, 128 * z : 128 * z + 128] = value


def banded(spread, half, stack):
    lane = iota((256, 512), 1) & 127
    sums = [jnp.dot(spread[half, dx], stack[...], preferred_element_type=F32) for dx in range(3)]
    left = jnp.concatenate([pltpu.roll(sums[0][:, 128 * z : 128 * z + 128], 127, 1) for z in range(4)], axis=1)
    right = jnp.concatenate([pltpu.roll(sums[2][:, 128 * z : 128 * z + 128], 1, 1) for z in range(4)], axis=1)
    return sums[1] + jnp.where(lane == 127, 0.0, left) + jnp.where(lane == 0, 0.0, right)


def near_input_kernel(spread, g_own, g_nbr, out, stack):
    row, col, _ = grid_place()
    stack_planes(row + col, [(g_own, 7 * row + 3 * col, 0), (g_nbr, 3 * col, 128)], stack)
    out[...] = banded(spread, 0, stack)


def near_input(spread, g_own, g_nbr):
    return pl.pallas_call(
        near_input_kernel,
        out_shape=jax.ShapeDtypeStruct((256, 512), F32),
        in_specs=[vmem()] * 3,
        out_specs=vmem(),
        scratch_shapes=[pltpu.VMEM((768, 512), BF16)],
        compiler_params=pltpu.CompilerParams(vmem_limit_bytes=10 * 2**20),
        cost_estimate=pl.CostEstimate(flops=2**33, bytes_accessed=2**25, transcendentals=0),
        name="near_input",
    )(spread, g_own, g_nbr)


def far_input_kernel(spread, g_far, near, out, mark, stack):
    row, col, _ = grid_place()
    stack_planes(row + col, [(g_far, 0, 0)], stack)
    total = (banded(spread, 1, stack) + near[...]).astype(BF16)
    for z in range(4):
        out[:, z] = total[:, 128 * z : 128 * z + 128].reshape(32, 8, 128)
    mark[...] = jnp.zeros((8, 128), F32)


def far_input(spread, g_far, near):
    return pl.pallas_call(
        far_input_kernel,
        out_shape=(jax.ShapeDtypeStruct((32, 4, 8, 128), BF16), jax.ShapeDtypeStruct((8, 128), F32)),
        in_specs=[vmem()] * 3,
        out_specs=(vmem(), vmem()),
        scratch_shapes=[pltpu.VMEM((768, 512), BF16)],
        compiler_params=pltpu.CompilerParams(vmem_limit_bytes=10 * 2**20),
        cost_estimate=pl.CostEstimate(flops=9 * 256 * 256 * 512, bytes_accessed=2**22, transcendentals=0),
        name="far_input",
    )(spread, g_far, near)


def swap(block, axis, bits):
    count = lax.axis_size(axis)
    return lax.ppermute(block, axis, [(i, i ^ bits) for i in range(count)])


def line_kernel(chip, two, four, six, after, out):
    out[...] = (chip[...] + two[...]) + (four[...] + six[...])


def line_sum(chip, two, four, six, after):
    return pl.pallas_call(
        line_kernel,
        out_shape=jax.ShapeDtypeStruct(chip.shape, F32),
        in_specs=[vmem()] * 4 + [anywhere()],
        out_specs=vmem(),
        compiler_params=pltpu.CompilerParams(vmem_limit_bytes=2**20),
        cost_estimate=pl.CostEstimate(flops=2**16, bytes_accessed=2**18, transcendentals=0),
        name="line_sum",
    )(chip, two, four, six, after)


def slab_kernel(line, across, beside, diagonal, after, out):
    out[0] = line[...] + across[...]
    out[1] = beside[...] + diagonal[...]


def slab_sum(line, across, beside, diagonal, after):
    return pl.pallas_call(
        slab_kernel,
        out_shape=jax.ShapeDtypeStruct((2,) + line.shape, F32),
        in_specs=[vmem()] * 4 + [anywhere()],
        out_specs=vmem(),
        compiler_params=pltpu.CompilerParams(vmem_limit_bytes=2**20),
        cost_estimate=pl.CostEstimate(flops=2**16, bytes_accessed=2**18, transcendentals=0),
        name="slab_sum",
    )(line, across, beside, diagonal, after)


def local_grid(activations, grad_out, weight):
    slab = lax.axis_index("slab")
    row = slab // 2
    act = activations[0]
    g_own = grad_out[0]

    a_nbr = swap(act, "slab", 1)
    g_nbr = swap(lax.dynamic_slice_in_dim(g_own, 7 * (1 - row), 9, axis=1), "slab", 2)
    a_rows, g_rows, sums = near_rows(g_own, act)
    keep, send = filter_partial(a_rows, g_rows, sums, g_nbr, a_nbr)
    chip = keep + swap(send, "sample", 1)
    g_far = swap(pass_on(g_own, g_nbr, keep), "slab", 1)
    spread = spread_filters(jnp.swapaxes(weight, 1, 2), chip)
    near = near_input(spread, g_own, g_nbr)
    line = line_sum(chip, swap(chip, "sample", 2), swap(chip, "sample", 4), swap(chip, "sample", 6), near)
    grad_in, mark = far_input(spread, g_far, near)
    mine = slab_sum(line, swap(line, "slab", 2), swap(line, "slab", 1), swap(line, "slab", 3), mark)
    other = swap(mine, "sample", 1)
    cells = 8 * 128 * 4 * lax.axis_size("slab") * lax.axis_size("sample")
    grad_weight, grad_bias = finish(mine, other, 1.0 / math.sqrt(cells))
    return grad_in[None], jnp.swapaxes(grad_weight, 1, 2), grad_bias.reshape(64)


def with_halo(block, sides, width):
    for axis, dim in sides:
        count = lax.axis_size(axis)
        forward = [(i, i + 1) for i in range(count - 1)]
        backward = [(target, source) for source, target in forward]
        low = lax.ppermute(
            lax.slice_in_dim(block, block.shape[dim] - width, None, axis=dim), axis, forward
        )
        high = lax.ppermute(lax.slice_in_dim(block, 0, width, axis=dim), axis, backward)
        block = jnp.concatenate([low, block, high], axis=dim)
    return block


def offsets_list():
    return [
        (shift_z, shift_y, shift_x)
        for shift_z in (-1, 0, 1)
        for shift_y in (-1, 0, 1)
        for shift_x in (-1, 0, 1)
    ]


def local_any(activations, grad_out, weight):
    samples, in_chan, planes, y_cells, x_cells = activations.shape
    slabs = lax.axis_size("slab")
    regrouped = lax.all_to_all(grad_out, "slab", split_axis=2, concat_axis=1, tiled=True)
    g_ext = with_halo(regrouped, (("slab", 2),), 1)
    widths = ((0, 0), (0, 0), (0, 0), (1, 1), (1, 1))
    padded_co = jnp.pad(g_ext, widths)
    grad_in = jnp.zeros((samples, in_chan, planes, y_cells, x_cells), F32)
    pieces = []
    for offset, (shift_z, shift_y, shift_x) in enumerate(offsets_list()):
        moved_co = padded_co[
            :,
            :,
            1 - shift_z : 1 - shift_z + planes,
            1 - shift_y : 1 - shift_y + y_cells,
            1 - shift_x : 1 - shift_x + x_cells,
        ]
        pieces.append(jnp.einsum("sozyx,sizyx->oi", moved_co, activations, preferred_element_type=F32))
        grad_in = grad_in + jnp.einsum("oi,sozyx->sizyx", weight[offset], moved_co, preferred_element_type=F32)
    wpart = jnp.stack(pieces)
    bpart = jnp.sum(regrouped.astype(F32), axis=(0, 2, 3, 4))
    wtotal, btotal = lax.psum((wpart, bpart), ("slab", "sample"))
    all_cells = samples * lax.axis_size("sample") * planes * slabs * y_cells * x_cells
    factor = 1.0 / math.sqrt(all_cells)
    return (grad_in.astype(BF16), wtotal * factor, btotal * factor)


def local(activations, grad_out, weight):
    grid = (
        lax.axis_size("slab") == 4
        and lax.axis_size("sample") == 8
        and activations.shape == (1, 32, 4, 8, 128)
        and grad_out.shape == (1, 16, 16, 8, 128)
    )
    return (local_grid if grid else local_any)(activations, grad_out, weight)


def solution(mesh):
    placed = (P("sample", None, "slab", None, None), P("sample", "slab", None, None, None), P())
    return jax.shard_map(
        local,
        mesh=mesh,
        in_specs=placed,
        out_specs=(P("sample", None, "slab", None, None), P(), P()),
        check_vma=False,
    )
```

time: 38.3 us -> 34.6 us (0.903)
  Pallas kernels: 11.2 us -> 8.15 us
  local copies, waits for them, and re-layouts: 4.92 us -> 3.05 us
  waiting for transfers between devices: 7.17 us -> 8.17 us
    pallas_call x4 -> x6, Pallas kernels: 9.53 us -> 7.01 us  [the longest x1 2.13 us: spread_filters(): pl.pallas_call(spread_kernel, out_shape=jax.ShapeDtypeStruct((2, 3, 256,...]
    unnamed x10 -> x8, local copies, waits for them, and re-layouts: 3.88 us -> 2 us
    ppermute x11, waiting for transfers between devices: 7.17 us -> 8.17 us  [swap(): return lax.ppermute(block, axis, [(i, i ^ bits) for i in range(count)])]
    pallas_call x1, Pallas kernels: 1.65 us -> 1.1 us  [finish(): pl.pallas_call(functools.partial(finish_kernel, factor), out_shape=(jax.S...]
  transfers between devices with their start and end apart: 11 -> 11, of which waited for: 4 -> 5; matrix products, arithmetic and copies ran while one was open for 0% -> 0% of each run, Pallas kernels for 17% -> 15%
where the time goes in v3:
time: 34.6 us; the launch traced here: 34.4 us
  starting transfers between devices  14.2 us (41%)
  waiting for transfers between devices  8.17 us (24%)
  Pallas kernels  8.15 us (24%)
  local copies, waits for them, and re-layouts  3.05 us (9%)
  between operations  0.75 us (2%)
    ppermute x11, starting transfers between devices, swap(): return lax.ppermute(block, axis, [(i, i ^ bits) for i in range(count)])  14.2 us
    ppermute x11, waiting for transfers between devices, swap(): return lax.ppermute(block, axis, [(i, i ^ bits) for i in range(count)])  8.17 us
    pallas_call x1, Pallas kernels, spread_filters(): pl.pallas_call(spread_kernel, out_shape=jax.ShapeDtypeStruct((2, 3, 256,...  2.13 us
    unnamed x8, local copies, waits for them, and re-layouts  2 us
    pallas_call x1, Pallas kernels, filter_partial(): pl.pallas_call(filter_kernel, out_shape=ROWS + (half, half), in_specs=[vm...  1.84 us
    pallas_call x1, Pallas kernels, far_input(): pl.pallas_call(far_input_kernel, out_shape=(jax.ShapeDtypeStruct((32, 4,...  1.6 us
    pallas_call x1, Pallas kernels, finish(): pl.pallas_call(functools.partial(finish_kernel, factor), out_shape=(jax.S...  1.1 us
    dynamic_slice x1, local copies, waits for them, and re-layouts, local_grid(): lax.dynamic_slice_in_dim(g_own, 7 * (1 - row), 9, axis=1)  1.05 us
  transfers between devices with their start and end apart: 11, of which 5 were waited for; matrix products, arithmetic and copies ran while one was open for 0% of the time, Pallas kernels for 15%

profile of v3, /device:TPU:0, one launch (start us, length us, event | category | flops | bytes accessed | tf_op | source)
XLA Modules:
  0.0 34.4 jit_solution(15585630937093082719)
XLA Ops:
  0.6 0.0 copy-start.1
  0.7 1.1 %dynamic-slice_bitcast_fusion = bf16[16,9,8,128]{3,2,1,0:T(8,128)(2,1)S(1)} fusion(bf16[1,16,16,8,128]{4,3,2,1,0:T(8,128)(2,1)} %param.4, s32[]{:T(128)S(6)} %select_n.9), kind=kLoop, calls=%fused_computation | loop fusion | bytes 589828 | tf_op jit(solution)/shard_map/dynamic_slice | solution.py:377
  1.7 3.0 %collective-permute-start = (bf16[16,9,8,128]{3,2,1,0:T(8,128)(2,1)S(1)}, bf16[16,9,8,128]{3,2,1,0:T(8,128)(2,1)S(1)}, u32[]{:S(2)}, u32[]{:S(2)}) collective-permute-start(bf16[16,9,8,128]{3,2,1,0:T(8,128)(2,1)S(1)} %dynamic-slice_bitcast_fusion), channel_id=1, source_target_pairs={{0,16},{8,24},{16,0},{24,8},{1,17},{9,25},{17,1},{25,9},{2,18},{10... | collective-permute-start | bytes 884744 | tf_op jit(solution)/shard_map/ppermute | solution.py:334
  4.7 1.5 %collective-permute-start.1 = (bf16[32,4,8,128]{3,2,1,0:T(8,128)(2,1)}, bf16[32,4,8,128]{3,2,1,0:T(8,128)(2,1)S(1)}, u32[]{:S(2)}, u32[]{:S(2)}) collective-permute-start(bf16[32,4,8,128]{3,2,1,0:T(8,128)(2,1)} %bitcast.11), channel_id=1, source_target_pairs={{0,8},{8,0},{16,24},{24,16},{1,9},{9,1},{17,25},{25,17},{2,10},{10... | collective-permute-start | bytes 786440 | tf_op jit(solution)/shard_map/ppermute | solution.py:334
  6.2 0.0 copy-start
  6.2 1.0 %copy-done = bf16[1,16,16,8,128]{4,3,2,1,0:T(8,128)(2,1)S(1)} copy-done((bf16[1,16,16,8,128]{4,3,2,1,0:T(8,128)(2,1)S(1)}, bf16[1,16,16,8,128]{4,3,2,1,0:T(8,128)(2,1)}, u32[]{:S(2)}) %copy-start) | copy-done | bytes 524312
  7.3 0.0 copy-start.2
  7.3 0.9 %copy-done.2 = bf16[1,32,4,8,128]{4,3,2,1,0:T(8,128)(2,1)S(1)} copy-done((bf16[1,32,4,8,128]{4,3,2,1,0:T(8,128)(2,1)S(1)}, bf16[1,32,4,8,128]{4,3,2,1,0:T(8,128)(2,1)}, u32[]{:S(2)}) %copy-start.2) | copy-done | bytes 262168
  8.2 0.5 %near_rows.1 = (bf16[12,32,1280]{2,1,0:T(8,128)(2,1)S(1)}, bf16[10,128,1024]{2,1,0:T(8,128)(2,1)S(1)}, f32[16,128]{1,0:T(8,128)S(1)}) custom-call(bf16[16,16,8,128]{3,2,1,0:T(8,128)(2,1)S(1)} %bitcast.8, bf16[32,4,8,128]{3,2,1,0:T(8,128)(2,1)S(1)} %bitcast.12), custom_call_target="tpu_custom_call" | custom-call | flops 268435456 | bytes 2097152 | tf_op jit(solution)/shard_map/near_rows/pallas_call | solution.py:115
  8.8 4.0 %collective-permute-done.1.a_nbr = bf16[32,4,8,128]{3,2,1,0:T(8,128)(2,1)S(1)} collective-permute-done((bf16[32,4,8,128]{3,2,1,0:T(8,128)(2,1)}, bf16[32,4,8,128]{3,2,1,0:T(8,128)(2,1)S(1)}, u32[]{:S(2)}, u32[]{:S(2)}) %collective-permute-start.1) | collective-permute-done | bytes 262176 | tf_op jit(solution)/shard_map/ppermute | solution.py:334
  12.7 0.0 collective-permute-done.g_nbr
  12.7 1.8 %filter_partial.1 = (bf16[12,32,1280]{2,1,0:T(8,128)(2,1)S(1)}, bf16[10,128,1024]{2,1,0:T(8,128)(2,1)S(1)}, f32[112,128]{1,0:T(8,128)S(1)}, f32[112,128]{1,0:T(8,128)S(1)}) custom-call(bf16[12,32,1280]{2,1,0:T(8,128)(2,1)S(1)} %get-tuple-element.12.a_in, ...), custom_call_target="tpu_custom_call", output_to_operand_aliasing={{0}: (0, {}), {1}: (1, {})} | custom-call | flops 566231040 | bytes 2097152 | tf_op jit(solution)/shard_map/filter_partial/pallas_call | solution.py:157
  14.6 0.0 copy-start.3
  14.6 0.1 collective-permute-start.2
  14.7 0.0 copy-done.1
  14.7 1.6 %collective-permute-start.3 = (bf16[32,6,8,128]{3,2,1,0:T(8,128)(2,1)S(1)}, bf16[32,6,8,128]{3,2,1,0:T(8,128)(2,1)S(1)}, u32[]{:S(2)}, u32[]{:S(2)}) collective-permute-start(bf16[32,6,8,128]{3,2,1,0:T(8,128)(2,1)S(1)} %pass_on.1), channel_id=1, source_target_pairs={{0,8},{8,0},{16,24},{24,16},{1,9},{9,1},{17,25},{25,17},{2,10},{10... | collective-permute-start | bytes 1179656 | tf_op jit(solution)/shard_map/ppermute | solution.py:334
  16.3 0.0 collective-permute-done.2
  16.3 3.7 %collective-permute-start.6 = (f32[112,128]{1,0:T(8,128)S(1)}, f32[112,128]{1,0:T(8,128)S(1)}, u32[]{:S(2)}, u32[]{:S(2)}) collective-permute-start(f32[112,128]{1,0:T(8,128)S(1)} %add.8.after.chip), channel_id=1, source_target_pairs={{0,6},{1,7},{2,4},{3,5},{4,2},{5,3},{6,0},{7,1},{8,14},{9,15},{10,... | collective-permute-start | bytes 172040 | tf_op jit(solution)/shard_map/ppermute | solution.py:334
  20.0 0.0 collective-permute-start.5
  20.0 0.8 %collective-permute-start.4 = (f32[112,128]{1,0:T(8,128)S(1)}, f32[112,128]{1,0:T(8,128)S(1)}, u32[]{:S(2)}, u32[]{:S(2)}) collective-permute-start(f32[112,128]{1,0:T(8,128)S(1)} %add.8.after.chip), channel_id=1, source_target_pairs={{0,2},{1,3},{2,0},{3,1},{4,6},{5,7},{6,4},{7,5},{8,10},{9,11},{10,... | collective-permute-start | bytes 172040 | tf_op jit(solution)/shard_map/ppermute | solution.py:334
  20.8 0.0 copy-done.3
  20.8 2.1 %spread_filters.1.spread = bf16[2,3,256,768]{3,2,1,0:T(8,128)(2,1)S(1)} custom-call(bf16[27,32,64]{2,1,0:T(8,128)(2,1)S(1)} %bitcast.13, f32[112,128]{1,0:T(8,128)S(1)} %add.8.after.chip), custom_call_target="tpu_custom_call" | custom-call | flops 8589934592 | bytes 33554432 | tf_op jit(solution)/shard_map/spread_filters/pallas_call | solution.py:256
  22.9 0.9 %near_input.1.near.after = f32[256,512]{1,0:T(8,128)S(1)} custom-call(bf16[2,3,256,768]{3,2,1,0:T(8,128)(2,1)S(1)} %spread_filters.1.spread, bf16[16,16,8,128]{3,2,1,0:T(8,128)(2,1)S(1)} %bitcast.10, bf16[16,9,8,128]{3,2,1,0:T(8,128)(2,1)S(1)} %collective-permute-done.g_nbr), custom_call_target="tpu_custom_call" | custom-call | flops 8589934592 | bytes 33554432 | tf_op jit(solution)/shard_map/near_input/pallas_call | solution.py:298
  23.8 0.0 collective-permute-done.6.six
  23.8 1.6 %collective-permute-done.5.four = f32[112,128]{1,0:T(8,128)S(1)} collective-permute-done((f32[112,128]{1,0:T(8,128)S(1)}, f32[112,128]{1,0:T(8,128)S(1)}, u32[]{:S(2)}, u32[]{:S(2)}) %collective-permute-start.5) | collective-permute-done | bytes 57376 | tf_op jit(solution)/shard_map/ppermute | solution.py:334
  25.4 0.0 collective-permute-done.4.two
  25.4 1.4 %collective-permute-start.9 = (f32[112,128]{1,0:T(8,128)S(1)}, f32[112,128]{1,0:T(8,128)S(1)}, u32[]{:S(2)}, u32[]{:S(2)}) collective-permute-start(f32[112,128]{1,0:T(8,128)S(1)} %line_sum.1.line), channel_id=1, source_target_pairs={{0,24},{8,16},{16,8},{24,0},{1,25},{9,17},{17,9},{25,1},{2,26},{10... | collective-permute-start | bytes 172040 | tf_op jit(solution)/shard_map/ppermute | solution.py:334
  26.7 0.9 %collective-permute-start.8 = (f32[112,128]{1,0:T(8,128)S(1)}, f32[112,128]{1,0:T(8,128)S(1)}, u32[]{:S(2)}, u32[]{:S(2)}) collective-permute-start(f32[112,128]{1,0:T(8,128)S(1)} %line_sum.1.line), channel_id=1, source_target_pairs={{0,8},{8,0},{16,24},{24,16},{1,9},{9,1},{17,25},{25,17},{2,10},{10... | collective-permute-start | bytes 172040 | tf_op jit(solution)/shard_map/ppermute | solution.py:334
  27.7 1.3 %collective-permute-start.7 = (f32[112,128]{1,0:T(8,128)S(1)}, f32[112,128]{1,0:T(8,128)S(1)}, u32[]{:S(2)}, u32[]{:S(2)}) collective-permute-start(f32[112,128]{1,0:T(8,128)S(1)} %line_sum.1.line), channel_id=1, source_target_pairs={{0,16},{8,24},{16,0},{24,8},{1,17},{9,25},{17,1},{25,9},{2,18},{10... | collective-permute-start | bytes 172040 | tf_op jit(solution)/shard_map/ppermute | solution.py:334
  28.9 0.0 collective-permute-done.3.g_far
  28.9 1.6 %far_input.1 = (bf16[32,4,8,128]{3,2,1,0:T(8,128)(2,1)}, f32[8,128]{1,0:T(8,128)S(1)}) custom-call(bf16[2,3,256,768]{3,2,1,0:T(8,128)(2,1)S(1)} %spread_filters.1.spread, bf16[32,6,8,128]{3,2,1,0:T(8,128)(2,1)S(1)} %collective-permute-done.3.g_far, f32[256,512]{1,0:T(8,128)S(1)} %near_input.1.near.after), custom_call_target="tpu_custom_call" | custom-call | flops 301989888 | bytes 4194304 | tf_op jit(solution)/shard_map/far_input/pallas_call | solution.py:320
  30.5 0.0 collective-permute-done.9.diagonal
  30.5 0.4 %collective-permute-done.8.beside = f32[112,128]{1,0:T(8,128)S(1)} collective-permute-done((f32[112,128]{1,0:T(8,128)S(1)}, f32[112,128]{1,0:T(8,128)S(1)}, u32[]{:S(2)}, u32[]{:S(2)}) %collective-permute-start.8) | collective-permute-done | bytes 57376 | tf_op jit(solution)/shard_map/ppermute | solution.py:334
  30.9 0.9 %collective-permute-done.7.across = f32[112,128]{1,0:T(8,128)S(1)} collective-permute-done((f32[112,128]{1,0:T(8,128)S(1)}, f32[112,128]{1,0:T(8,128)S(1)}, u32[]{:S(2)}, u32[]{:S(2)}) %collective-permute-start.7) | collective-permute-done | bytes 57376 | tf_op jit(solution)/shard_map/ppermute | solution.py:334
  31.9 0.1 collective-permute-start.10
  31.9 1.3 %collective-permute-done.10.other = f32[2,112,128]{2,1,0:T(8,128)S(1)} collective-permute-done((f32[2,112,128]{2,1,0:T(8,128)S(1)}, f32[2,112,128]{2,1,0:T(8,128)S(1)}, u32[]{:S(2)}, u32[]{:S(2)}) %collective-permute-start.10) | collective-permute-done | bytes 114720 | tf_op jit(solution)/shard_map/ppermute | solution.py:334
  33.3 1.1 %filter_finish.1 = (f32[27,32,64]{2,1,0:T(8,128)}, f32[1,64]{1,0:T(1,128)}) custom-call(f32[2,112,128]{2,1,0:T(8,128)S(1)} %slab_sum.1.mine, f32[2,112,128]{2,1,0:T(8,128)S(1)} %collective-permute-done.10.other), custom_call_target="tpu_custom_call" | custom-call | flops 262144 | bytes 1048576 | tf_op jit(solution)/shard_map/filter_finish/pallas_call | solution.py:220
  (4 shorter events, 0.1 us)
Async XLA Ops:
  0.6 14.0 %copy-start.1 = (bf16[1,16,16,8,128]{4,3,2,1,0:T(8,128)(2,1)S(1)}, bf16[1,16,16,8,128]{4,3,2,1,0:T(8,128)(2,1)}, u32[]{:S(2)}) copy-start(bf16[1,16,16,8,128]{4,3,2,1,0:T(8,128)(2,1)} %param.4) | copy-start | bytes 1572868
  1.7 11.0 %collective-permute-start = (bf16[16,9,8,128]{3,2,1,0:T(8,128)(2,1)S(1)}, bf16[16,9,8,128]{3,2,1,0:T(8,128)(2,1)S(1)}, u32[]{:S(2)}, u32[]{:S(2)}) collective-permute-start(bf16[16,9,8,128]{3,2,1,0:T(8,128)(2,1)S(1)} %dynamic-slice_bitcast_fusion), channel_id=1, source_target_pairs={{0,16},{8,24},{16,0},{24,8},{1,17},{9,25},{17,1},{25,9},{2,18},{10... | collective-permute-start | bytes 884744 | tf_op jit(solution)/shard_map/ppermute | solution.py:334
  4.7 8.0 %collective-permute-start.1 = (bf16[32,4,8,128]{3,2,1,0:T(8,128)(2,1)}, bf16[32,4,8,128]{3,2,1,0:T(8,128)(2,1)S(1)}, u32[]{:S(2)}, u32[]{:S(2)}) collective-permute-start(bf16[32,4,8,128]{3,2,1,0:T(8,128)(2,1)} %bitcast.11), channel_id=1, source_target_pairs={{0,8},{8,0},{16,24},{24,16},{1,9},{9,1},{17,25},{25,17},{2,10},{10... | collective-permute-start | bytes 786440 | tf_op jit(solution)/shard_map/ppermute | solution.py:334
  6.2 1.0 %copy-start = (bf16[1,16,16,8,128]{4,3,2,1,0:T(8,128)(2,1)S(1)}, bf16[1,16,16,8,128]{4,3,2,1,0:T(8,128)(2,1)}, u32[]{:S(2)}) copy-start(bf16[1,16,16,8,128]{4,3,2,1,0:T(8,128)(2,1)} %param.4) | copy-start | bytes 1572868
  7.3 0.9 %copy-start.2 = (bf16[1,32,4,8,128]{4,3,2,1,0:T(8,128)(2,1)S(1)}, bf16[1,32,4,8,128]{4,3,2,1,0:T(8,128)(2,1)}, u32[]{:S(2)}) copy-start(bf16[1,32,4,8,128]{4,3,2,1,0:T(8,128)(2,1)} %param.3) | copy-start | bytes 786436
  14.6 6.2 %copy-start.3 = (bf16[27,64,32]{1,2,0:T(8,128)(2,1)S(1)}, bf16[27,64,32]{1,2,0:T(8,128)(2,1)}, u32[]{:S(2)}) copy-start(bf16[27,64,32]{1,2,0:T(8,128)(2,1)} %param.5) | copy-start | bytes 331780
  14.6 1.7 %collective-permute-start.2 = (f32[112,128]{1,0:T(8,128)S(1)}, f32[112,128]{1,0:T(8,128)S(1)}, u32[]{:S(2)}, u32[]{:S(2)}) collective-permute-start(f32[112,128]{1,0:T(8,128)S(1)} %get-tuple-element.16), channel_id=1, source_target_pairs={{0,1},{1,0},{2,3},{3,2},{4,5},{5,4},{6,7},{7,6},{8,9},{9,8},{10,11... | collective-permute-start | bytes 172040 | tf_op jit(solution)/shard_map/ppermute | solution.py:334
  14.7 14.2 %collective-permute-start.3 = (bf16[32,6,8,128]{3,2,1,0:T(8,128)(2,1)S(1)}, bf16[32,6,8,128]{3,2,1,0:T(8,128)(2,1)S(1)}, u32[]{:S(2)}, u32[]{:S(2)}) collective-permute-start(bf16[32,6,8,128]{3,2,1,0:T(8,128)(2,1)S(1)} %pass_on.1), channel_id=1, source_target_pairs={{0,8},{8,0},{16,24},{24,16},{1,9},{9,1},{17,25},{25,17},{2,10},{10... | collective-permute-start | bytes 1179656 | tf_op jit(solution)/shard_map/ppermute | solution.py:334
  16.3 7.5 %collective-permute-start.6 = (f32[112,128]{1,0:T(8,128)S(1)}, f32[112,128]{1,0:T(8,128)S(1)}, u32[]{:S(2)}, u32[]{:S(2)}) collective-permute-start(f32[112,128]{1,0:T(8,128)S(1)} %add.8.after.chip), channel_id=1, source_target_pairs={{0,6},{1,7},{2,4},{3,5},{4,2},{5,3},{6,0},{7,1},{8,14},{9,15},{10,... | collective-permute-start | bytes 172040 | tf_op jit(solution)/shard_map/ppermute | solution.py:334
  20.0 5.4 %collective-permute-start.5 = (f32[112,128]{1,0:T(8,128)S(1)}, f32[112,128]{1,0:T(8,128)S(1)}, u32[]{:S(2)}, u32[]{:S(2)}) collective-permute-start(f32[112,128]{1,0:T(8,128)S(1)} %add.8.after.chip), channel_id=1, source_target_pairs={{0,4},{1,5},{2,6},{3,7},{4,0},{5,1},{6,2},{7,3},{8,12},{9,13},{10,... | collective-permute-start | bytes 172040 | tf_op jit(solution)/shard_map/ppermute | solution.py:334
  20.0 5.4 %collective-permute-start.4 = (f32[112,128]{1,0:T(8,128)S(1)}, f32[112,128]{1,0:T(8,128)S(1)}, u32[]{:S(2)}, u32[]{:S(2)}) collective-permute-start(f32[112,128]{1,0:T(8,128)S(1)} %add.8.after.chip), channel_id=1, source_target_pairs={{0,2},{1,3},{2,0},{3,1},{4,6},{5,7},{6,4},{7,5},{8,10},{9,11},{10,... | collective-permute-start | bytes 172040 | tf_op jit(solution)/shard_map/ppermute | solution.py:334
  25.4 5.2 %collective-permute-start.9 = (f32[112,128]{1,0:T(8,128)S(1)}, f32[112,128]{1,0:T(8,128)S(1)}, u32[]{:S(2)}, u32[]{:S(2)}) collective-permute-start(f32[112,128]{1,0:T(8,128)S(1)} %line_sum.1.line), channel_id=1, source_target_pairs={{0,24},{8,16},{16,8},{24,0},{1,25},{9,17},{17,9},{25,1},{2,26},{10... | collective-permute-start | bytes 172040 | tf_op jit(solution)/shard_map/ppermute | solution.py:334
  26.7 4.2 %collective-permute-start.8 = (f32[112,128]{1,0:T(8,128)S(1)}, f32[112,128]{1,0:T(8,128)S(1)}, u32[]{:S(2)}, u32[]{:S(2)}) collective-permute-start(f32[112,128]{1,0:T(8,128)S(1)} %line_sum.1.line), channel_id=1, source_target_pairs={{0,8},{8,0},{16,24},{24,16},{1,9},{9,1},{17,25},{25,17},{2,10},{10... | collective-permute-start | bytes 172040 | tf_op jit(solution)/shard_map/ppermute | solution.py:334
  27.7 4.2 %collective-permute-start.7 = (f32[112,128]{1,0:T(8,128)S(1)}, f32[112,128]{1,0:T(8,128)S(1)}, u32[]{:S(2)}, u32[]{:S(2)}) collective-permute-start(f32[112,128]{1,0:T(8,128)S(1)} %line_sum.1.line), channel_id=1, source_target_pairs={{0,16},{8,24},{16,0},{24,8},{1,17},{9,25},{17,1},{25,9},{2,18},{10... | collective-permute-start | bytes 172040 | tf_op jit(solution)/shard_map/ppermute | solution.py:334
  31.9 1.4 %collective-permute-start.10 = (f32[2,112,128]{2,1,0:T(8,128)S(1)}, f32[2,112,128]{2,1,0:T(8,128)S(1)}, u32[]{:S(2)}, u32[]{:S(2)}) collective-permute-start(f32[2,112,128]{2,1,0:T(8,128)S(1)} %slab_sum.1.mine), channel_id=1, source_target_pairs={{0,1},{1,0},{2,3},{3,2},{4,5},{5,4},{6,7},{7,6},{8,9},{9,8},{10,11... | collective-permute-start | bytes 344072 | tf_op jit(solution)/shard_map/ppermute | solution.py:334

commit v4 on v3

--- a/solution.py
+++ b/solution.py
@@ -92,21 +92,18 @@
 
 def near_kernel(g_own, a_own, abuf, gbuf, sums):
     row, col, _ = grid_place()
-    for slot in range(12):
-        if slot in (0, 1, 10, 11):
-            abuf[slot] = jnp.zeros((32, 1280), BF16)
-        else:
-            abuf[slot, :, 0:128] = jnp.zeros((32, 128), BF16)
-            abuf[slot, :, 1152:1280] = jnp.zeros((32, 128), BF16)
+    for plane in range(8):
+        abuf[plane, :, 0:128] = jnp.zeros((32, 128), BF16)
+        abuf[plane, :, 1152:1280] = jnp.zeros((32, 128), BF16)
     for slot in range(10):
         gbuf[slot, 96:128] = jnp.zeros((32, 1024), BF16)
     gbuf[9 * row] = jnp.zeros((128, 1024), BF16)
-    act_rows(a_own, act_put(abuf, 2 + 4 * col))
+    act_rows(a_own, act_put(abuf, 4 * col))
     sums[...] = cot_rows(g_own, 7 * row, row, cot_put(gbuf, row, row))
 
 
 ROWS = (
-    jax.ShapeDtypeStruct((12, 32, 1280), BF16),
+    jax.ShapeDtypeStruct((8, 32, 1280), BF16),
     jax.ShapeDtypeStruct((10, 128, 1024), BF16),
 )
 
@@ -125,19 +122,22 @@
 
 def filter_kernel(a_in, g_in, sums, g_nbr, a_nbr, abuf, gbuf, keep, send):
     row, col, core = grid_place()
-    act_rows(a_nbr, act_put(abuf, 6 - 4 * col))
+    act_rows(a_nbr, act_put(abuf, 4 - 4 * col))
     far_sums = cot_rows(g_nbr, 0, row, cot_put(gbuf, row, 1 - row))
-    wide = jnp.zeros((384, 256), F32)
+    parts = []
     for slot in range(0, 10, 2):
-        moved = [
-            abuf[slot + plane, :, 128 * shift : 128 * shift + 1024] for plane in range(4) for shift in range(3)
-        ]
-        wide = wide + lax.dot_general(
-            jnp.concatenate(moved, axis=0),
-            gbuf[slot : slot + 2].reshape(256, 1024),
-            NT,
-            preferred_element_type=F32,
+        planes = range(max(slot - 2, 0), min(slot + 2, 8))
+        moved = [abuf[plane, :, 128 * shift : 128 * shift + 1024] for plane in planes for shift in range(3)]
+        parts.append(
+            lax.dot_general(
+                jnp.concatenate(moved, axis=0),
+                gbuf[slot : slot + 2].reshape(256, 1024),
+                NT,
+                preferred_element_type=F32,
+            )
         )
+    whole = parts[1] + parts[2] + parts[3]
+    wide = jnp.concatenate([whole[0:192] + parts[4], whole[192:384] + parts[0]], axis=0)
     acc = wide[0:288, 0:128] + wide[96:384, 128:256]
     side = jnp.concatenate([acc[216:288, 32 * m : 32 * m + 32] for m in range(3)], axis=0)
     table = jnp.concatenate([acc[0:216, 0:96], side], axis=1)
@@ -334,11 +334,11 @@
     return lax.ppermute(block, axis, [(i, i ^ bits) for i in range(count)])
 
 
-def line_kernel(chip, two, four, six, after, out):
+def line_kernel(chip, two, six, four, after, out):
     out[...] = (chip[...] + two[...]) + (four[...] + six[...])
 
 
-def line_sum(chip, two, four, six, after):
+def line_sum(chip, two, six, four, after):
     return pl.pallas_call(
         line_kernel,
         out_shape=jax.ShapeDtypeStruct(chip.shape, F32),
@@ -347,7 +347,7 @@
         compiler_params=pltpu.CompilerParams(vmem_limit_bytes=2**20),
         cost_estimate=pl.CostEstimate(flops=2**16, bytes_accessed=2**18, transcendentals=0),
         name="line_sum",
-    )(chip, two, four, six, after)
+    )(chip, two, six, four, after)
 
 
 def slab_kernel(line, across, beside, diagonal, after, out):
@@ -381,7 +381,7 @@
     g_far = swap(pass_on(g_own, g_nbr, keep), "slab", 1)
     spread = spread_filters(jnp.swapaxes(weight, 1, 2), chip)
     near = near_input(spread, g_own, g_nbr)
-    line = line_sum(chip, swap(chip, "sample", 2), swap(chip, "sample", 4), swap(chip, "sample", 6), near)
+    line = line_sum(chip, swap(chip, "sample", 2), swap(chip, "sample", 6), swap(chip, "sample", 4), near)
     grad_in, mark = far_input(spread, g_far, near)
     mine = slab_sum(line, swap(line, "slab", 2), swap(line, "slab", 1), swap(line, "slab", 3), mark)
     other = swap(mine, "sample", 1)

time: 34.6 us -> 34.3 us (level)
  no operation moved by 1% of the time
where the time goes in v4:
time: 34.3 us; the launch traced here: 34 us
  starting transfers between devices  14 us (41%)
  waiting for transfers between devices  8.2 us (24%)
  Pallas kernels  8.01 us (23%)
  local copies, waits for them, and re-layouts  3.05 us (9%)
  between operations  0.76 us (2%)
    ppermute x11, starting transfers between devices, swap(): return lax.ppermute(block, axis, [(i, i ^ bits) for i in range(count)])  14 us
    ppermute x11, waiting for transfers between devices, swap(): return lax.ppermute(block, axis, [(i, i ^ bits) for i in range(count)])  8.2 us
    pallas_call x1, Pallas kernels, spread_filters(): pl.pallas_call(spread_kernel, out_shape=jax.ShapeDtypeStruct((2, 3, 256,...  2.13 us
    unnamed x8, local copies, waits for them, and re-layouts  2 us
    pallas_call x1, Pallas kernels, filter_partial(): pl.pallas_call(filter_kernel, out_shape=ROWS + (half, half), in_specs=[vm...  1.72 us
    pallas_call x1, Pallas kernels, far_input(): pl.pallas_call(far_input_kernel, out_shape=(jax.ShapeDtypeStruct((32, 4,...  1.6 us
    pallas_call x1, Pallas kernels, finish(): pl.pallas_call(functools.partial(finish_kernel, factor), out_shape=(jax.S...  1.1 us
    dynamic_slice x1, local copies, waits for them, and re-layouts, local_grid(): lax.dynamic_slice_in_dim(g_own, 7 * (1 - row), 9, axis=1)  1.05 us
  transfers between devices with their start and end apart: 11, of which 5 were waited for; matrix products, arithmetic and copies ran while one was open for 0% of the time, Pallas kernels for 15%

profile of v4, /device:TPU:0, one launch (start us, length us, event | category | flops | bytes accessed | tf_op | source)
XLA Modules:
  0.0 34.0 jit_solution(12247995114759012475)
XLA Ops:
  0.6 0.0 copy-start.1
  0.7 1.1 %dynamic-slice_bitcast_fusion = bf16[16,9,8,128]{3,2,1,0:T(8,128)(2,1)S(1)} fusion(bf16[1,16,16,8,128]{4,3,2,1,0:T(8,128)(2,1)} %param.4, s32[]{:T(128)S(6)} %select_n.9), kind=kLoop, calls=%fused_computation | loop fusion | bytes 589828 | tf_op jit(solution)/shard_map/dynamic_slice | solution.py:377
  1.7 3.0 %collective-permute-start = (bf16[16,9,8,128]{3,2,1,0:T(8,128)(2,1)S(1)}, bf16[16,9,8,128]{3,2,1,0:T(8,128)(2,1)S(1)}, u32[]{:S(2)}, u32[]{:S(2)}) collective-permute-start(bf16[16,9,8,128]{3,2,1,0:T(8,128)(2,1)S(1)} %dynamic-slice_bitcast_fusion), channel_id=1, source_target_pairs={{0,16},{8,24},{16,0},{24,8},{1,17},{9,25},{17,1},{25,9},{2,18},{10... | collective-permute-start | bytes 884744 | tf_op jit(solution)/shard_map/ppermute | solution.py:334
  4.7 1.5 %collective-permute-start.1 = (bf16[32,4,8,128]{3,2,1,0:T(8,128)(2,1)}, bf16[32,4,8,128]{3,2,1,0:T(8,128)(2,1)S(1)}, u32[]{:S(2)}, u32[]{:S(2)}) collective-permute-start(bf16[32,4,8,128]{3,2,1,0:T(8,128)(2,1)} %bitcast.11), channel_id=1, source_target_pairs={{0,8},{8,0},{16,24},{24,16},{1,9},{9,1},{17,25},{25,17},{2,10},{10... | collective-permute-start | bytes 786440 | tf_op jit(solution)/shard_map/ppermute | solution.py:334
  6.2 0.0 copy-start
  6.2 1.0 %copy-done = bf16[1,16,16,8,128]{4,3,2,1,0:T(8,128)(2,1)S(1)} copy-done((bf16[1,16,16,8,128]{4,3,2,1,0:T(8,128)(2,1)S(1)}, bf16[1,16,16,8,128]{4,3,2,1,0:T(8,128)(2,1)}, u32[]{:S(2)}) %copy-start) | copy-done | bytes 524312
  7.3 0.0 copy-start.2
  7.3 0.9 %copy-done.2 = bf16[1,32,4,8,128]{4,3,2,1,0:T(8,128)(2,1)S(1)} copy-done((bf16[1,32,4,8,128]{4,3,2,1,0:T(8,128)(2,1)S(1)}, bf16[1,32,4,8,128]{4,3,2,1,0:T(8,128)(2,1)}, u32[]{:S(2)}) %copy-start.2) | copy-done | bytes 262168
  8.2 0.5 %near_rows.1 = (bf16[8,32,1280]{2,1,0:T(8,128)(2,1)S(1)}, bf16[10,128,1024]{2,1,0:T(8,128)(2,1)S(1)}, f32[16,128]{1,0:T(8,128)S(1)}) custom-call(bf16[16,16,8,128]{3,2,1,0:T(8,128)(2,1)S(1)} %bitcast.8, bf16[32,4,8,128]{3,2,1,0:T(8,128)(2,1)S(1)} %bitcast.12), custom_call_target="tpu_custom_call" | custom-call | flops 268435456 | bytes 2097152 | tf_op jit(solution)/shard_map/near_rows/pallas_call | solution.py:112
  8.7 4.0 %collective-permute-done.1.a_nbr = bf16[32,4,8,128]{3,2,1,0:T(8,128)(2,1)S(1)} collective-permute-done((bf16[32,4,8,128]{3,2,1,0:T(8,128)(2,1)}, bf16[32,4,8,128]{3,2,1,0:T(8,128)(2,1)S(1)}, u32[]{:S(2)}, u32[]{:S(2)}) %collective-permute-start.1) | collective-permute-done | bytes 262176 | tf_op jit(solution)/shard_map/ppermute | solution.py:334
  12.7 0.0 collective-permute-done.g_nbr
  12.7 1.7 %filter_partial.1 = (bf16[8,32,1280]{2,1,0:T(8,128)(2,1)S(1)}, bf16[10,128,1024]{2,1,0:T(8,128)(2,1)S(1)}, f32[112,128]{1,0:T(8,128)S(1)}, f32[112,128]{1,0:T(8,128)S(1)}) custom-call(bf16[8,32,1280]{2,1,0:T(8,128)(2,1)S(1)} %get-tuple-element.12.a_in, ...), custom_call_target="tpu_custom_call", output_to_operand_aliasing={{0}: (0, {}), {1}: (1, {})} | custom-call | flops 566231040 | bytes 2097152 | tf_op jit(solution)/shard_map/filter_partial/pallas_call | solution.py:157
  14.5 0.0 copy-start.3
  14.5 0.1 collective-permute-start.2
  14.5 0.0 copy-done.1
  14.6 1.5 %collective-permute-start.3 = (bf16[32,6,8,128]{3,2,1,0:T(8,128)(2,1)S(1)}, bf16[32,6,8,128]{3,2,1,0:T(8,128)(2,1)S(1)}, u32[]{:S(2)}, u32[]{:S(2)}) collective-permute-start(bf16[32,6,8,128]{3,2,1,0:T(8,128)(2,1)S(1)} %pass_on.1), channel_id=1, source_target_pairs={{0,8},{8,0},{16,24},{24,16},{1,9},{9,1},{17,25},{25,17},{2,10},{10... | collective-permute-start | bytes 1179656 | tf_op jit(solution)/shard_map/ppermute | solution.py:334
  16.2 0.0 collective-permute-done.2
  16.2 2.7 %collective-permute-start.6 = (f32[112,128]{1,0:T(8,128)S(1)}, f32[112,128]{1,0:T(8,128)S(1)}, u32[]{:S(2)}, u32[]{:S(2)}) collective-permute-start(f32[112,128]{1,0:T(8,128)S(1)} %add.8.after.chip), channel_id=1, source_target_pairs={{0,4},{1,5},{2,6},{3,7},{4,0},{5,1},{6,2},{7,3},{8,12},{9,13},{10,... | collective-permute-start | bytes 172040 | tf_op jit(solution)/shard_map/ppermute | solution.py:334
  18.8 1.3 %collective-permute-start.5 = (f32[112,128]{1,0:T(8,128)S(1)}, f32[112,128]{1,0:T(8,128)S(1)}, u32[]{:S(2)}, u32[]{:S(2)}) collective-permute-start(f32[112,128]{1,0:T(8,128)S(1)} %add.8.after.chip), channel_id=1, source_target_pairs={{0,6},{1,7},{2,4},{3,5},{4,2},{5,3},{6,0},{7,1},{8,14},{9,15},{10,... | collective-permute-start | bytes 172040 | tf_op jit(solution)/shard_map/ppermute | solution.py:334
  20.2 0.2 collective-permute-start.4
  20.4 0.0 copy-done.3
  20.4 2.1 %spread_filters.1.spread = bf16[2,3,256,768]{3,2,1,0:T(8,128)(2,1)S(1)} custom-call(bf16[27,32,64]{2,1,0:T(8,128)(2,1)S(1)} %bitcast.13, f32[112,128]{1,0:T(8,128)S(1)} %add.8.after.chip), custom_call_target="tpu_custom_call" | custom-call | flops 8589934592 | bytes 33554432 | tf_op jit(solution)/shard_map/spread_filters/pallas_call | solution.py:256
  22.6 0.9 %near_input.1.near.after = f32[256,512]{1,0:T(8,128)S(1)} custom-call(bf16[2,3,256,768]{3,2,1,0:T(8,128)(2,1)S(1)} %spread_filters.1.spread, bf16[16,16,8,128]{3,2,1,0:T(8,128)(2,1)S(1)} %bitcast.10, bf16[16,9,8,128]{3,2,1,0:T(8,128)(2,1)S(1)} %collective-permute-done.g_nbr), custom_call_target="tpu_custom_call" | custom-call | flops 8589934592 | bytes 33554432 | tf_op jit(solution)/shard_map/near_input/pallas_call | solution.py:298
  23.4 0.0 collective-permute-done.6.four
  23.5 1.6 %collective-permute-done.5.six = f32[112,128]{1,0:T(8,128)S(1)} collective-permute-done((f32[112,128]{1,0:T(8,128)S(1)}, f32[112,128]{1,0:T(8,128)S(1)}, u32[]{:S(2)}, u32[]{:S(2)}) %collective-permute-start.5) | collective-permute-done | bytes 57376 | tf_op jit(solution)/shard_map/ppermute | solution.py:334
  25.0 0.0 collective-permute-done.4.two
  25.0 1.3 %collective-permute-start.9 = (f32[112,128]{1,0:T(8,128)S(1)}, f32[112,128]{1,0:T(8,128)S(1)}, u32[]{:S(2)}, u32[]{:S(2)}) collective-permute-start(f32[112,128]{1,0:T(8,128)S(1)} %line_sum.1.line), channel_id=1, source_target_pairs={{0,24},{8,16},{16,8},{24,0},{1,25},{9,17},{17,9},{25,1},{2,26},{10... | collective-permute-start | bytes 172040 | tf_op jit(solution)/shard_map/ppermute | solution.py:334
  26.4 1.0 %collective-permute-start.8 = (f32[112,128]{1,0:T(8,128)S(1)}, f32[112,128]{1,0:T(8,128)S(1)}, u32[]{:S(2)}, u32[]{:S(2)}) collective-permute-start(f32[112,128]{1,0:T(8,128)S(1)} %line_sum.1.line), channel_id=1, source_target_pairs={{0,8},{8,0},{16,24},{24,16},{1,9},{9,1},{17,25},{25,17},{2,10},{10... | collective-permute-start | bytes 172040 | tf_op jit(solution)/shard_map/ppermute | solution.py:334
  27.4 1.2 %collective-permute-start.7 = (f32[112,128]{1,0:T(8,128)S(1)}, f32[112,128]{1,0:T(8,128)S(1)}, u32[]{:S(2)}, u32[]{:S(2)}) collective-permute-start(f32[112,128]{1,0:T(8,128)S(1)} %line_sum.1.line), channel_id=1, source_target_pairs={{0,16},{8,24},{16,0},{24,8},{1,17},{9,25},{17,1},{25,9},{2,18},{10... | collective-permute-start | bytes 172040 | tf_op jit(solution)/shard_map/ppermute | solution.py:334
  28.6 0.0 collective-permute-done.3.g_far
  28.6 1.6 %far_input.1 = (bf16[32,4,8,128]{3,2,1,0:T(8,128)(2,1)}, f32[8,128]{1,0:T(8,128)S(1)}) custom-call(bf16[2,3,256,768]{3,2,1,0:T(8,128)(2,1)S(1)} %spread_filters.1.spread, bf16[32,6,8,128]{3,2,1,0:T(8,128)(2,1)S(1)} %collective-permute-done.3.g_far, f32[256,512]{1,0:T(8,128)S(1)} %near_input.1.near.after), custom_call_target="tpu_custom_call" | custom-call | flops 301989888 | bytes 4194304 | tf_op jit(solution)/shard_map/far_input/pallas_call | solution.py:320
  30.2 0.0 collective-permute-done.9.diagonal
  30.2 0.4 %collective-permute-done.8.beside = f32[112,128]{1,0:T(8,128)S(1)} collective-permute-done((f32[112,128]{1,0:T(8,128)S(1)}, f32[112,128]{1,0:T(8,128)S(1)}, u32[]{:S(2)}, u32[]{:S(2)}) %collective-permute-start.8) | collective-permute-done | bytes 57376 | tf_op jit(solution)/shard_map/ppermute | solution.py:334
  30.6 1.0 %collective-permute-done.7.across = f32[112,128]{1,0:T(8,128)S(1)} collective-permute-done((f32[112,128]{1,0:T(8,128)S(1)}, f32[112,128]{1,0:T(8,128)S(1)}, u32[]{:S(2)}, u32[]{:S(2)}) %collective-permute-start.7) | collective-permute-done | bytes 57376 | tf_op jit(solution)/shard_map/ppermute | solution.py:334
  31.6 0.1 collective-permute-start.10
  31.6 1.3 %collective-permute-done.10.other = f32[2,112,128]{2,1,0:T(8,128)S(1)} collective-permute-done((f32[2,112,128]{2,1,0:T(8,128)S(1)}, f32[2,112,128]{2,1,0:T(8,128)S(1)}, u32[]{:S(2)}, u32[]{:S(2)}) %collective-permute-start.10) | collective-permute-done | bytes 114720 | tf_op jit(solution)/shard_map/ppermute | solution.py:334
  32.9 1.1 %filter_finish.1 = (f32[27,32,64]{2,1,0:T(8,128)}, f32[1,64]{1,0:T(1,128)}) custom-call(f32[2,112,128]{2,1,0:T(8,128)S(1)} %slab_sum.1.mine, f32[2,112,128]{2,1,0:T(8,128)S(1)} %collective-permute-done.10.other), custom_call_target="tpu_custom_call" | custom-call | flops 262144 | bytes 1048576 | tf_op jit(solution)/shard_map/filter_finish/pallas_call | solution.py:220
  (4 shorter events, 0.1 us)
Async XLA Ops:
  0.6 13.9 %copy-start.1 = (bf16[1,16,16,8,128]{4,3,2,1,0:T(8,128)(2,1)S(1)}, bf16[1,16,16,8,128]{4,3,2,1,0:T(8,128)(2,1)}, u32[]{:S(2)}) copy-start(bf16[1,16,16,8,128]{4,3,2,1,0:T(8,128)(2,1)} %param.4) | copy-start | bytes 1572868
  1.7 11.0 %collective-permute-start = (bf16[16,9,8,128]{3,2,1,0:T(8,128)(2,1)S(1)}, bf16[16,9,8,128]{3,2,1,0:T(8,128)(2,1)S(1)}, u32[]{:S(2)}, u32[]{:S(2)}) collective-permute-start(bf16[16,9,8,128]{3,2,1,0:T(8,128)(2,1)S(1)} %dynamic-slice_bitcast_fusion), channel_id=1, source_target_pairs={{0,16},{8,24},{16,0},{24,8},{1,17},{9,25},{17,1},{25,9},{2,18},{10... | collective-permute-start | bytes 884744 | tf_op jit(solution)/shard_map/ppermute | solution.py:334
  4.7 8.0 %collective-permute-start.1 = (bf16[32,4,8,128]{3,2,1,0:T(8,128)(2,1)}, bf16[32,4,8,128]{3,2,1,0:T(8,128)(2,1)S(1)}, u32[]{:S(2)}, u32[]{:S(2)}) collective-permute-start(bf16[32,4,8,128]{3,2,1,0:T(8,128)(2,1)} %bitcast.11), channel_id=1, source_target_pairs={{0,8},{8,0},{16,24},{24,16},{1,9},{9,1},{17,25},{25,17},{2,10},{10... | collective-permute-start | bytes 786440 | tf_op jit(solution)/shard_map/ppermute | solution.py:334
  6.2 1.0 %copy-start = (bf16[1,16,16,8,128]{4,3,2,1,0:T(8,128)(2,1)S(1)}, bf16[1,16,16,8,128]{4,3,2,1,0:T(8,128)(2,1)}, u32[]{:S(2)}) copy-start(bf16[1,16,16,8,128]{4,3,2,1,0:T(8,128)(2,1)} %param.4) | copy-start | bytes 1572868
  7.3 0.9 %copy-start.2 = (bf16[1,32,4,8,128]{4,3,2,1,0:T(8,128)(2,1)S(1)}, bf16[1,32,4,8,128]{4,3,2,1,0:T(8,128)(2,1)}, u32[]{:S(2)}) copy-start(bf16[1,32,4,8,128]{4,3,2,1,0:T(8,128)(2,1)} %param.3) | copy-start | bytes 786436
  14.5 6.0 %copy-start.3 = (bf16[27,64,32]{1,2,0:T(8,128)(2,1)S(1)}, bf16[27,64,32]{1,2,0:T(8,128)(2,1)}, u32[]{:S(2)}) copy-start(bf16[27,64,32]{1,2,0:T(8,128)(2,1)} %param.5) | copy-start | bytes 331780
  14.5 1.7 %collective-permute-start.2 = (f32[112,128]{1,0:T(8,128)S(1)}, f32[112,128]{1,0:T(8,128)S(1)}, u32[]{:S(2)}, u32[]{:S(2)}) collective-permute-start(f32[112,128]{1,0:T(8,128)S(1)} %get-tuple-element.16), channel_id=1, source_target_pairs={{0,1},{1,0},{2,3},{3,2},{4,5},{5,4},{6,7},{7,6},{8,9},{9,8},{10,11... | collective-permute-start | bytes 172040 | tf_op jit(solution)/shard_map/ppermute | solution.py:334
  14.6 14.0 %collective-permute-start.3 = (bf16[32,6,8,128]{3,2,1,0:T(8,128)(2,1)S(1)}, bf16[32,6,8,128]{3,2,1,0:T(8,128)(2,1)S(1)}, u32[]{:S(2)}, u32[]{:S(2)}) collective-permute-start(bf16[32,6,8,128]{3,2,1,0:T(8,128)(2,1)S(1)} %pass_on.1), channel_id=1, source_target_pairs={{0,8},{8,0},{16,24},{24,16},{1,9},{9,1},{17,25},{25,17},{2,10},{10... | collective-permute-start | bytes 1179656 | tf_op jit(solution)/shard_map/ppermute | solution.py:334
  16.2 7.3 %collective-permute-start.6 = (f32[112,128]{1,0:T(8,128)S(1)}, f32[112,128]{1,0:T(8,128)S(1)}, u32[]{:S(2)}, u32[]{:S(2)}) collective-permute-start(f32[112,128]{1,0:T(8,128)S(1)} %add.8.after.chip), channel_id=1, source_target_pairs={{0,4},{1,5},{2,6},{3,7},{4,0},{5,1},{6,2},{7,3},{8,12},{9,13},{10,... | collective-permute-start | bytes 172040 | tf_op jit(solution)/shard_map/ppermute | solution.py:334
  18.8 6.2 %collective-permute-start.5 = (f32[112,128]{1,0:T(8,128)S(1)}, f32[112,128]{1,0:T(8,128)S(1)}, u32[]{:S(2)}, u32[]{:S(2)}) collective-permute-start(f32[112,128]{1,0:T(8,128)S(1)} %add.8.after.chip), channel_id=1, source_target_pairs={{0,6},{1,7},{2,4},{3,5},{4,2},{5,3},{6,0},{7,1},{8,14},{9,15},{10,... | collective-permute-start | bytes 172040 | tf_op jit(solution)/shard_map/ppermute | solution.py:334
  20.2 4.9 %collective-permute-start.4 = (f32[112,128]{1,0:T(8,128)S(1)}, f32[112,128]{1,0:T(8,128)S(1)}, u32[]{:S(2)}, u32[]{:S(2)}) collective-permute-start(f32[112,128]{1,0:T(8,128)S(1)} %add.8.after.chip), channel_id=1, source_target_pairs={{0,2},{1,3},{2,0},{3,1},{4,6},{5,7},{6,4},{7,5},{8,10},{9,11},{10,... | collective-permute-start | bytes 172040 | tf_op jit(solution)/shard_map/ppermute | solution.py:334
  25.0 5.2 %collective-permute-start.9 = (f32[112,128]{1,0:T(8,128)S(1)}, f32[112,128]{1,0:T(8,128)S(1)}, u32[]{:S(2)}, u32[]{:S(2)}) collective-permute-start(f32[112,128]{1,0:T(8,128)S(1)} %line_sum.1.line), channel_id=1, source_target_pairs={{0,24},{8,16},{16,8},{24,0},{1,25},{9,17},{17,9},{25,1},{2,26},{10... | collective-permute-start | bytes 172040 | tf_op jit(solution)/shard_map/ppermute | solution.py:334
  26.4 4.2 %collective-permute-start.8 = (f32[112,128]{1,0:T(8,128)S(1)}, f32[112,128]{1,0:T(8,128)S(1)}, u32[]{:S(2)}, u32[]{:S(2)}) collective-permute-start(f32[112,128]{1,0:T(8,128)S(1)} %line_sum.1.line), channel_id=1, source_target_pairs={{0,8},{8,0},{16,24},{24,16},{1,9},{9,1},{17,25},{25,17},{2,10},{10... | collective-permute-start | bytes 172040 | tf_op jit(solution)/shard_map/ppermute | solution.py:334
  27.4 4.2 %collective-permute-start.7 = (f32[112,128]{1,0:T(8,128)S(1)}, f32[112,128]{1,0:T(8,128)S(1)}, u32[]{:S(2)}, u32[]{:S(2)}) collective-permute-start(f32[112,128]{1,0:T(8,128)S(1)} %line_sum.1.line), channel_id=1, source_target_pairs={{0,16},{8,24},{16,0},{24,8},{1,17},{9,25},{17,1},{25,9},{2,18},{10... | collective-permute-start | bytes 172040 | tf_op jit(solution)/shard_map/ppermute | solution.py:334
  31.6 1.4 %collective-permute-start.10 = (f32[2,112,128]{2,1,0:T(8,128)S(1)}, f32[2,112,128]{2,1,0:T(8,128)S(1)}, u32[]{:S(2)}, u32[]{:S(2)}) collective-permute-start(f32[2,112,128]{2,1,0:T(8,128)S(1)} %slab_sum.1.mine), channel_id=1, source_target_pairs={{0,1},{1,0},{2,3},{3,2},{4,5},{5,4},{6,7},{7,6},{8,9},{9,8},{10,11... | collective-permute-start | bytes 344072 | tf_op jit(solution)/shard_map/ppermute | solution.py:334

commit v5 on v4

--- a/solution.py
+++ b/solution.py
@@ -120,8 +120,7 @@
     )(g_own, a_own)
 
 
-def filter_kernel(a_in, g_in, sums, g_nbr, a_nbr, abuf, gbuf, keep, send):
-    row, col, core = grid_place()
+def filter_body(row, col, core, sums, g_nbr, a_nbr, abuf, gbuf, keep, send):
     act_rows(a_nbr, act_put(abuf, 4 - 4 * col))
     far_sums = cot_rows(g_nbr, 0, row, cot_put(gbuf, row, 1 - row))
     parts = []
@@ -152,18 +151,27 @@
     send[...] = jnp.where(core == 0, high, low)
 
 
-def filter_partial(a_rows, g_rows, sums, g_nbr, a_nbr):
+def filter_kernel(a_in, g_in, sums, g_nbr, a_nbr, after, *outs):
+    row, col, core = grid_place()
+    for r in range(2):
+        for c in range(2):
+            pl.when((row == r) & (col == c))(
+                functools.partial(filter_body, r, c, core, sums, g_nbr, a_nbr, *outs)
+            )
+
+
+def filter_partial(a_rows, g_rows, sums, g_nbr, a_nbr, after):
     half = jax.ShapeDtypeStruct((112, 128), F32)
     return pl.pallas_call(
         filter_kernel,
         out_shape=ROWS + (half, half),
-        in_specs=[vmem()] * 5,
+        in_specs=[vmem()] * 5 + [anywhere()],
         out_specs=(vmem(),) * 4,
         input_output_aliases={0: 0, 1: 1},
         compiler_params=pltpu.CompilerParams(vmem_limit_bytes=12 * 2**20),
         cost_estimate=pl.CostEstimate(flops=2 * 10 * 288 * 96 * 1024, bytes_accessed=2**21, transcendentals=0),
         name="filter_partial",
-    )(a_rows, g_rows, sums, g_nbr, a_nbr)[2:]
+    )(a_rows, g_rows, sums, g_nbr, a_nbr, after)[2:]
 
 
 def pass_kernel(g_own, g_nbr, after, out):
@@ -259,7 +267,7 @@
         in_specs=[vmem(), anywhere()],
         out_specs=vmem(),
         compiler_params=pltpu.CompilerParams(vmem_limit_bytes=8 * 2**20),
-        cost_estimate=pl.CostEstimate(flops=2**33, bytes_accessed=2**25, transcendentals=0),
+        cost_estimate=pl.CostEstimate(flops=2 * 27 * 256 * 64 * 512, bytes_accessed=2**21, transcendentals=0),
         name="spread_filters",
     )(weight, after)
 
@@ -334,11 +342,11 @@
     return lax.ppermute(block, axis, [(i, i ^ bits) for i in range(count)])
 
 
-def line_kernel(chip, two, six, four, after, out):
-    out[...] = (chip[...] + two[...]) + (four[...] + six[...])
-
-
-def line_sum(chip, two, six, four, after):
+def line_kernel(chip, one_off, two_off, both_off, after, out):
+    out[...] = (chip[...] + one_off[...]) + (two_off[...] + both_off[...])
+
+
+def line_sum(chip, one_off, two_off, both_off, after):
     return pl.pallas_call(
         line_kernel,
         out_shape=jax.ShapeDtypeStruct(chip.shape, F32),
@@ -347,24 +355,30 @@
         compiler_params=pltpu.CompilerParams(vmem_limit_bytes=2**20),
         cost_estimate=pl.CostEstimate(flops=2**16, bytes_accessed=2**18, transcendentals=0),
         name="line_sum",
-    )(chip, two, six, four, after)
-
-
-def slab_kernel(line, across, beside, diagonal, after, out):
+    )(chip, one_off, two_off, both_off, after)
+
+
+def last_kernel(line, beside, across, diagonal, after, out):
     out[0] = line[...] + across[...]
     out[1] = beside[...] + diagonal[...]
 
 
-def slab_sum(line, across, beside, diagonal, after):
-    return pl.pallas_call(
-        slab_kernel,
+def last_sum(line, beside, across, diagonal, after):
+    return pl.pallas_call(
+        last_kernel,
         out_shape=jax.ShapeDtypeStruct((2,) + line.shape, F32),
         in_specs=[vmem()] * 4 + [anywhere()],
         out_specs=vmem(),
         compiler_params=pltpu.CompilerParams(vmem_limit_bytes=2**20),
         cost_estimate=pl.CostEstimate(flops=2**16, bytes_accessed=2**18, transcendentals=0),
-        name="slab_sum",
-    )(line, across, beside, diagonal, after)
+        name="last_sum",
+    )(line, beside, across, diagonal, after)
+
+
+def swap_at(block, slab_bits, sample_bits):
+    count, samples = lax.axis_size(("slab", "sample")), lax.axis_size("sample")
+    pairs = [(i, i ^ (samples * slab_bits + sample_bits)) for i in range(count)]
+    return lax.ppermute(block, ("slab", "sample"), pairs)
 
 
 def local_grid(activations, grad_out, weight):
@@ -376,14 +390,14 @@
     a_nbr = swap(act, "slab", 1)
     g_nbr = swap(lax.dynamic_slice_in_dim(g_own, 7 * (1 - row), 9, axis=1), "slab", 2)
     a_rows, g_rows, sums = near_rows(g_own, act)
-    keep, send = filter_partial(a_rows, g_rows, sums, g_nbr, a_nbr)
+    spread = spread_filters(jnp.swapaxes(weight, 1, 2), sums)
+    keep, send = filter_partial(a_rows, g_rows, sums, g_nbr, a_nbr, spread)
     chip = keep + swap(send, "sample", 1)
     g_far = swap(pass_on(g_own, g_nbr, keep), "slab", 1)
-    spread = spread_filters(jnp.swapaxes(weight, 1, 2), chip)
     near = near_input(spread, g_own, g_nbr)
-    line = line_sum(chip, swap(chip, "sample", 2), swap(chip, "sample", 6), swap(chip, "sample", 4), near)
+    line = line_sum(chip, swap_at(chip, 2, 0), swap_at(chip, 0, 2), swap_at(chip, 2, 2), near)
     grad_in, mark = far_input(spread, g_far, near)
-    mine = slab_sum(line, swap(line, "slab", 2), swap(line, "slab", 1), swap(line, "slab", 3), mark)
+    mine = last_sum(line, swap_at(line, 1, 0), swap_at(line, 0, 4), swap_at(line, 1, 4), mark)
     other = swap(mine, "sample", 1)
     cells = 8 * 128 * 4 * lax.axis_size("slab") * lax.axis_size("sample")
     grad_weight, grad_bias = finish(mine, other, 1.0 / math.sqrt(cells))

time: 34.3 us -> 33.5 us (0.977)
  waiting for transfers between devices: 8.2 us -> 6.54 us
  local copies, waits for them, and re-layouts: 3.05 us -> 3.92 us
    ppermute x0 -> x6, starting transfers between devices: none -> 8.01 us  [swap_at(): return lax.ppermute(block, ('slab', 'sample'), pairs)]
    ppermute x11 -> x5, starting transfers between devices: 14 us -> 6.21 us  [swap(): return lax.ppermute(block, axis, [(i, i ^ bits) for i in range(count)])]
    ppermute x11 -> x5, waiting for transfers between devices: 8.2 us -> 2.22 us  [swap(): return lax.ppermute(block, axis, [(i, i ^ bits) for i in range(count)])]
    ppermute x0 -> x6, waiting for transfers between devices: none -> 4.32 us  [swap_at(): return lax.ppermute(block, ('slab', 'sample'), pairs)]
    unnamed x8, local copies, waits for them, and re-layouts: 2 us -> 2.93 us
  transfers between devices with their start and end apart: 11 -> 11, of which waited for: 5 -> 7; matrix products, arithmetic and copies ran while one was open for 0% -> 0% of each run, Pallas kernels for 15% -> 15%
where the time goes in v5:
time: 33.5 us; the launch traced here: 33.2 us
  starting transfers between devices  14.2 us (42%)
  Pallas kernels  7.79 us (23%)
  waiting for transfers between devices  6.54 us (20%)
  local copies, waits for them, and re-layouts  3.92 us (12%)
  between operations  0.74 us (2%)
    ppermute x6, starting transfers between devices, swap_at(): return lax.ppermute(block, ('slab', 'sample'), pairs)  8.01 us
    ppermute x5, starting transfers between devices, swap(): return lax.ppermute(block, axis, [(i, i ^ bits) for i in range(count)])  6.21 us
    ppermute x6, waiting for transfers between devices, swap_at(): return lax.ppermute(block, ('slab', 'sample'), pairs)  4.32 us
    unnamed x8, local copies, waits for them, and re-layouts  2.93 us
    ppermute x5, waiting for transfers between devices, swap(): return lax.ppermute(block, axis, [(i, i ^ bits) for i in range(count)])  2.22 us
    pallas_call x1, Pallas kernels, spread_filters(): pl.pallas_call(spread_kernel, out_shape=jax.ShapeDtypeStruct((2, 3, 256,...  2.13 us
    pallas_call x1, Pallas kernels, far_input(): pl.pallas_call(far_input_kernel, out_shape=(jax.ShapeDtypeStruct((32, 4,...  1.59 us
    pallas_call x1, Pallas kernels, filter_partial(): pl.pallas_call(filter_kernel, out_shape=ROWS + (half, half), in_specs=[vm...  1.53 us
  transfers between devices with their start and end apart: 11, of which 7 were waited for; matrix products, arithmetic and copies ran while one was open for 0% of the time, Pallas kernels for 15%

profile of v5, /device:TPU:0, one launch (start us, length us, event | category | flops | bytes accessed | tf_op | source)
XLA Modules:
  0.0 33.2 jit_solution(7049386931164385890)
XLA Ops:
  0.6 1.0 %dynamic-slice_bitcast_fusion = bf16[16,9,8,128]{3,2,1,0:T(8,128)(2,1)S(1)} fusion(bf16[1,16,16,8,128]{4,3,2,1,0:T(8,128)(2,1)} %param.4, s32[]{:T(128)S(6)} %select_n.9), kind=kLoop, calls=%fused_computation | loop fusion | bytes 589828 | tf_op jit(solution)/shard_map/dynamic_slice | solution.py:391
  1.6 3.0 %collective-permute-start = (bf16[16,9,8,128]{3,2,1,0:T(8,128)(2,1)S(1)}, bf16[16,9,8,128]{3,2,1,0:T(8,128)(2,1)S(1)}, u32[]{:S(2)}, u32[]{:S(2)}) collective-permute-start(bf16[16,9,8,128]{3,2,1,0:T(8,128)(2,1)S(1)} %dynamic-slice_bitcast_fusion), channel_id=1, source_target_pairs={{0,16},{8,24},{16,0},{24,8},{1,17},{9,25},{17,1},{25,9},{2,18},{10... | collective-permute-start | bytes 884744 | tf_op jit(solution)/shard_map/ppermute | solution.py:342
  4.7 1.5 %collective-permute-start.1 = (bf16[32,4,8,128]{3,2,1,0:T(8,128)(2,1)}, bf16[32,4,8,128]{3,2,1,0:T(8,128)(2,1)S(1)}, u32[]{:S(2)}, u32[]{:S(2)}) collective-permute-start(bf16[32,4,8,128]{3,2,1,0:T(8,128)(2,1)} %bitcast.12), channel_id=1, source_target_pairs={{0,8},{8,0},{16,24},{24,16},{1,9},{9,1},{17,25},{25,17},{2,10},{10... | collective-permute-start | bytes 786440 | tf_op jit(solution)/shard_map/ppermute | solution.py:342
  6.2 0.0 copy-start.1
  6.2 1.0 %copy-done.1 = bf16[1,16,16,8,128]{4,3,2,1,0:T(8,128)(2,1)S(1)} copy-done((bf16[1,16,16,8,128]{4,3,2,1,0:T(8,128)(2,1)S(1)}, bf16[1,16,16,8,128]{4,3,2,1,0:T(8,128)(2,1)}, u32[]{:S(2)}) %copy-start.1) | copy-done | bytes 524312
  7.2 0.0 copy-start.3
  7.2 0.9 %copy-done.3 = bf16[1,32,4,8,128]{4,3,2,1,0:T(8,128)(2,1)S(1)} copy-done((bf16[1,32,4,8,128]{4,3,2,1,0:T(8,128)(2,1)S(1)}, bf16[1,32,4,8,128]{4,3,2,1,0:T(8,128)(2,1)}, u32[]{:S(2)}) %copy-start.3) | copy-done | bytes 262168
  8.2 0.5 %near_rows.1 = (bf16[8,32,1280]{2,1,0:T(8,128)(2,1)S(1)}, bf16[10,128,1024]{2,1,0:T(8,128)(2,1)S(1)}, f32[16,128]{1,0:T(8,128)S(1)}) custom-call(bf16[16,16,8,128]{3,2,1,0:T(8,128)(2,1)S(1)} %bitcast.9, bf16[32,4,8,128]{3,2,1,0:T(8,128)(2,1)S(1)} %bitcast.13), custom_call_target="tpu_custom_call" | custom-call | flops 268435456 | bytes 2097152 | tf_op jit(solution)/shard_map/near_rows/pallas_call | solution.py:112
  8.7 0.0 copy-start
  8.7 0.9 %copy-done = bf16[27,64,32]{1,2,0:T(8,128)(2,1)S(1)} copy-done((bf16[27,64,32]{1,2,0:T(8,128)(2,1)S(1)}, bf16[27,64,32]{1,2,0:T(8,128)(2,1)}, u32[]{:S(2)}) %copy-start) | copy-done | bytes 110616
  9.6 2.1 %spread_filters.1.after.spread = bf16[2,3,256,768]{3,2,1,0:T(8,128)(2,1)S(1)} custom-call(bf16[27,32,64]{2,1,0:T(8,128)(2,1)S(1)} %bitcast.8, f32[16,128]{1,0:T(8,128)S(1)} %get-tuple-element.12.after.sums), custom_call_target="tpu_custom_call" | custom-call | flops 452984832 | bytes 2097152 | tf_op jit(solution)/shard_map/spread_filters/pallas_call | solution.py:264
  11.8 0.9 %collective-permute-done.1.a_nbr = bf16[32,4,8,128]{3,2,1,0:T(8,128)(2,1)S(1)} collective-permute-done((bf16[32,4,8,128]{3,2,1,0:T(8,128)(2,1)}, bf16[32,4,8,128]{3,2,1,0:T(8,128)(2,1)S(1)}, u32[]{:S(2)}, u32[]{:S(2)}) %collective-permute-start.1) | collective-permute-done | bytes 262176 | tf_op jit(solution)/shard_map/ppermute | solution.py:342
  12.7 0.0 collective-permute-done.g_nbr
  12.7 0.0 copy-start.2
  12.7 1.5 %filter_partial.1 = (bf16[8,32,1280]{2,1,0:T(8,128)(2,1)S(1)}, bf16[10,128,1024]{2,1,0:T(8,128)(2,1)S(1)}, f32[112,128]{1,0:T(8,128)S(1)}, f32[112,128]{1,0:T(8,128)S(1)}) custom-call(bf16[8,32,1280]{2,1,0:T(8,128)(2,1)S(1)} %get-tuple-element.13.a_in, ...), custom_call_target="tpu_custom_call", output_to_operand_aliasing={{0}: (0, {}), {1}: (1, {})} | custom-call | flops 566231040 | bytes 2097152 | tf_op jit(solution)/shard_map/filter_partial/pallas_call | solution.py:165
  14.2 0.1 collective-permute-start.3
  14.3 0.0 copy-done.2
  14.3 0.1 pass_on.1
  14.3 1.5 %collective-permute-start.2 = (bf16[32,6,8,128]{3,2,1,0:T(8,128)(2,1)S(1)}, bf16[32,6,8,128]{3,2,1,0:T(8,128)(2,1)S(1)}, u32[]{:S(2)}, u32[]{:S(2)}) collective-permute-start(bf16[32,6,8,128]{3,2,1,0:T(8,128)(2,1)S(1)} %pass_on.1), channel_id=1, source_target_pairs={{0,8},{8,0},{16,24},{24,16},{1,9},{9,1},{17,25},{25,17},{2,10},{10... | collective-permute-start | bytes 1179656 | tf_op jit(solution)/shard_map/ppermute | solution.py:342
  15.9 0.0 collective-permute-done.3
  15.9 1.9 %collective-permute-start.6 = (f32[112,128]{1,0:T(8,128)S(1)}, f32[112,128]{1,0:T(8,128)S(1)}, u32[]{:S(2)}, u32[]{:S(2)}) collective-permute-start(f32[112,128]{1,0:T(8,128)S(1)} %add.8.chip), channel_id=1, source_target_pairs={{0,18},{1,19},{2,16},{3,17},{4,22},{5,23},{6,20},{7,21},{8,26},{9,... | collective-permute-start | bytes 172040 | tf_op jit(solution)/shard_map/ppermute | solution.py:381
  17.8 0.5 %collective-permute-start.5 = (f32[112,128]{1,0:T(8,128)S(1)}, f32[112,128]{1,0:T(8,128)S(1)}, u32[]{:S(2)}, u32[]{:S(2)}) collective-permute-start(f32[112,128]{1,0:T(8,128)S(1)} %add.8.chip), channel_id=1, source_target_pairs={{0,2},{1,3},{2,0},{3,1},{4,6},{5,7},{6,4},{7,5},{8,10},{9,11},{10,... | collective-permute-start | bytes 172040 | tf_op jit(solution)/shard_map/ppermute | solution.py:381
  18.2 1.2 %collective-permute-start.4 = (f32[112,128]{1,0:T(8,128)S(1)}, f32[112,128]{1,0:T(8,128)S(1)}, u32[]{:S(2)}, u32[]{:S(2)}) collective-permute-start(f32[112,128]{1,0:T(8,128)S(1)} %add.8.chip), channel_id=1, source_target_pairs={{0,16},{1,17},{2,18},{3,19},{4,20},{5,21},{6,22},{7,23},{8,24},{9,... | collective-permute-start | bytes 172040 | tf_op jit(solution)/shard_map/ppermute | solution.py:381
  19.5 0.8 %near_input.1.near.after = f32[256,512]{1,0:T(8,128)S(1)} custom-call(bf16[2,3,256,768]{3,2,1,0:T(8,128)(2,1)S(1)} %spread_filters.1.after.spread, bf16[16,16,8,128]{3,2,1,0:T(8,128)(2,1)S(1)} %bitcast.11, bf16[16,9,8,128]{3,2,1,0:T(8,128)(2,1)S(1)} %collective-permute-done.g_nbr), custom_call_target="tpu_custom_call" | custom-call | flops 8589934592 | bytes 33554432 | tf_op jit(solution)/shard_map/near_input/pallas_call | solution.py:306
  20.3 0.9 %collective-permute-done.6.both_off = f32[112,128]{1,0:T(8,128)S(1)} collective-permute-done((f32[112,128]{1,0:T(8,128)S(1)}, f32[112,128]{1,0:T(8,128)S(1)}, u32[]{:S(2)}, u32[]{:S(2)}) %collective-permute-start.6) | collective-permute-done | bytes 57376 | tf_op jit(solution)/shard_map/ppermute | solution.py:381
  21.2 0.8 %collective-permute-done.5.two_off = f32[112,128]{1,0:T(8,128)S(1)} collective-permute-done((f32[112,128]{1,0:T(8,128)S(1)}, f32[112,128]{1,0:T(8,128)S(1)}, u32[]{:S(2)}, u32[]{:S(2)}) %collective-permute-start.5) | collective-permute-done | bytes 57376 | tf_op jit(solution)/shard_map/ppermute | solution.py:381
  22.0 0.5 %collective-permute-done.4.one_off = f32[112,128]{1,0:T(8,128)S(1)} collective-permute-done((f32[112,128]{1,0:T(8,128)S(1)}, f32[112,128]{1,0:T(8,128)S(1)}, u32[]{:S(2)}, u32[]{:S(2)}) %collective-permute-start.4) | collective-permute-done | bytes 57376 | tf_op jit(solution)/shard_map/ppermute | solution.py:381
  22.4 3.2 %collective-permute-start.9 = (f32[112,128]{1,0:T(8,128)S(1)}, f32[112,128]{1,0:T(8,128)S(1)}, u32[]{:S(2)}, u32[]{:S(2)}) collective-permute-start(f32[112,128]{1,0:T(8,128)S(1)} %line_sum.1.line), channel_id=1, source_target_pairs={{0,12},{1,13},{2,14},{3,15},{4,8},{5,9},{6,10},{7,11},{8,4},{9,5},... | collective-permute-start | bytes 172040 | tf_op jit(solution)/shard_map/ppermute | solution.py:381
  25.6 0.3 %collective-permute-start.8 = (f32[112,128]{1,0:T(8,128)S(1)}, f32[112,128]{1,0:T(8,128)S(1)}, u32[]{:S(2)}, u32[]{:S(2)}) collective-permute-start(f32[112,128]{1,0:T(8,128)S(1)} %line_sum.1.line), channel_id=1, source_target_pairs={{0,4},{1,5},{2,6},{3,7},{4,0},{5,1},{6,2},{7,3},{8,12},{9,13},{10,... | collective-permute-start | bytes 172040 | tf_op jit(solution)/shard_map/ppermute | solution.py:381
  26.0 0.9 %collective-permute-start.7 = (f32[112,128]{1,0:T(8,128)S(1)}, f32[112,128]{1,0:T(8,128)S(1)}, u32[]{:S(2)}, u32[]{:S(2)}) collective-permute-start(f32[112,128]{1,0:T(8,128)S(1)} %line_sum.1.line), channel_id=1, source_target_pairs={{0,8},{1,9},{2,10},{3,11},{4,12},{5,13},{6,14},{7,15},{8,0},{9,1},... | collective-permute-start | bytes 172040 | tf_op jit(solution)/shard_map/ppermute | solution.py:381
  26.9 0.0 collective-permute-done.2.g_far
  26.9 1.6 %far_input.1 = (bf16[32,4,8,128]{3,2,1,0:T(8,128)(2,1)}, f32[8,128]{1,0:T(8,128)S(1)}) custom-call(bf16[2,3,256,768]{3,2,1,0:T(8,128)(2,1)S(1)} %spread_filters.1.after.spread, bf16[32,6,8,128]{3,2,1,0:T(8,128)(2,1)S(1)} %collective-permute-done.2.g_far, f32[256,512]{1,0:T(8,128)S(1)} %near_input.1.near.after), custom_call_target="tpu_custom_call" | custom-call | flops 301989888 | bytes 4194304 | tf_op jit(solution)/shard_map/far_input/pallas_call | solution.py:328
  28.5 0.1 collective-permute-done.9.diagonal
  28.5 2.2 %collective-permute-done.8.across = f32[112,128]{1,0:T(8,128)S(1)} collective-permute-done((f32[112,128]{1,0:T(8,128)S(1)}, f32[112,128]{1,0:T(8,128)S(1)}, u32[]{:S(2)}, u32[]{:S(2)}) %collective-permute-start.8) | collective-permute-done | bytes 57376 | tf_op jit(solution)/shard_map/ppermute | solution.py:381
  30.7 0.0 collective-permute-done.7.beside
  30.7 0.1 collective-permute-start.10
  30.8 1.3 %collective-permute-done.10.other = f32[2,112,128]{2,1,0:T(8,128)S(1)} collective-permute-done((f32[2,112,128]{2,1,0:T(8,128)S(1)}, f32[2,112,128]{2,1,0:T(8,128)S(1)}, u32[]{:S(2)}, u32[]{:S(2)}) %collective-permute-start.10) | collective-permute-done | bytes 114720 | tf_op jit(solution)/shard_map/ppermute | solution.py:342
  32.1 1.1 %filter_finish.1 = (f32[27,32,64]{2,1,0:T(8,128)}, f32[1,64]{1,0:T(1,128)}) custom-call(f32[2,112,128]{2,1,0:T(8,128)S(1)} %last_sum.1.mine, f32[2,112,128]{2,1,0:T(8,128)S(1)} %collective-permute-done.10.other), custom_call_target="tpu_custom_call" | custom-call | flops 262144 | bytes 1048576 | tf_op jit(solution)/shard_map/filter_finish/pallas_call | solution.py:228
  (3 shorter events, 0.0 us)
Async XLA Ops:
  1.6 11.0 %collective-permute-start = (bf16[16,9,8,128]{3,2,1,0:T(8,128)(2,1)S(1)}, bf16[16,9,8,128]{3,2,1,0:T(8,128)(2,1)S(1)}, u32[]{:S(2)}, u32[]{:S(2)}) collective-permute-start(bf16[16,9,8,128]{3,2,1,0:T(8,128)(2,1)S(1)} %dynamic-slice_bitcast_fusion), channel_id=1, source_target_pairs={{0,16},{8,24},{16,0},{24,8},{1,17},{9,25},{17,1},{25,9},{2,18},{10... | collective-permute-start | bytes 884744 | tf_op jit(solution)/shard_map/ppermute | solution.py:342
  4.7 8.0 %collective-permute-start.1 = (bf16[32,4,8,128]{3,2,1,0:T(8,128)(2,1)}, bf16[32,4,8,128]{3,2,1,0:T(8,128)(2,1)S(1)}, u32[]{:S(2)}, u32[]{:S(2)}) collective-permute-start(bf16[32,4,8,128]{3,2,1,0:T(8,128)(2,1)} %bitcast.12), channel_id=1, source_target_pairs={{0,8},{8,0},{16,24},{24,16},{1,9},{9,1},{17,25},{25,17},{2,10},{10... | collective-permute-start | bytes 786440 | tf_op jit(solution)/shard_map/ppermute | solution.py:342
  6.2 1.0 %copy-start.1 = (bf16[1,16,16,8,128]{4,3,2,1,0:T(8,128)(2,1)S(1)}, bf16[1,16,16,8,128]{4,3,2,1,0:T(8,128)(2,1)}, u32[]{:S(2)}) copy-start(bf16[1,16,16,8,128]{4,3,2,1,0:T(8,128)(2,1)} %param.4) | copy-start | bytes 1572868
  7.2 0.9 %copy-start.3 = (bf16[1,32,4,8,128]{4,3,2,1,0:T(8,128)(2,1)S(1)}, bf16[1,32,4,8,128]{4,3,2,1,0:T(8,128)(2,1)}, u32[]{:S(2)}) copy-start(bf16[1,32,4,8,128]{4,3,2,1,0:T(8,128)(2,1)} %param.3) | copy-start | bytes 786436
  8.7 0.9 %copy-start = (bf16[27,64,32]{1,2,0:T(8,128)(2,1)S(1)}, bf16[27,64,32]{1,2,0:T(8,128)(2,1)}, u32[]{:S(2)}) copy-start(bf16[27,64,32]{1,2,0:T(8,128)(2,1)} %param.5) | copy-start | bytes 331780
  12.7 1.6 %copy-start.2 = (bf16[1,16,16,8,128]{4,3,2,1,0:T(8,128)(2,1)S(1)}, bf16[1,16,16,8,128]{4,3,2,1,0:T(8,128)(2,1)}, u32[]{:S(2)}) copy-start(bf16[1,16,16,8,128]{4,3,2,1,0:T(8,128)(2,1)} %param.4) | copy-start | bytes 1572868
  14.2 1.7 %collective-permute-start.3 = (f32[112,128]{1,0:T(8,128)S(1)}, f32[112,128]{1,0:T(8,128)S(1)}, u32[]{:S(2)}, u32[]{:S(2)}) collective-permute-start(f32[112,128]{1,0:T(8,128)S(1)} %get-tuple-element.17), channel_id=1, source_target_pairs={{0,1},{1,0},{2,3},{3,2},{4,5},{5,4},{6,7},{7,6},{8,9},{9,8},{10,11... | collective-permute-start | bytes 172040 | tf_op jit(solution)/shard_map/ppermute | solution.py:342
  14.3 12.5 %collective-permute-start.2 = (bf16[32,6,8,128]{3,2,1,0:T(8,128)(2,1)S(1)}, bf16[32,6,8,128]{3,2,1,0:T(8,128)(2,1)S(1)}, u32[]{:S(2)}, u32[]{:S(2)}) collective-permute-start(bf16[32,6,8,128]{3,2,1,0:T(8,128)(2,1)S(1)} %pass_on.1), channel_id=1, source_target_pairs={{0,8},{8,0},{16,24},{24,16},{1,9},{9,1},{17,25},{25,17},{2,10},{10... | collective-permute-start | bytes 1179656 | tf_op jit(solution)/shard_map/ppermute | solution.py:342
  15.9 5.3 %collective-permute-start.6 = (f32[112,128]{1,0:T(8,128)S(1)}, f32[112,128]{1,0:T(8,128)S(1)}, u32[]{:S(2)}, u32[]{:S(2)}) collective-permute-start(f32[112,128]{1,0:T(8,128)S(1)} %add.8.chip), channel_id=1, source_target_pairs={{0,18},{1,19},{2,16},{3,17},{4,22},{5,23},{6,20},{7,21},{8,26},{9,... | collective-permute-start | bytes 172040 | tf_op jit(solution)/shard_map/ppermute | solution.py:381
  17.8 4.2 %collective-permute-start.5 = (f32[112,128]{1,0:T(8,128)S(1)}, f32[112,128]{1,0:T(8,128)S(1)}, u32[]{:S(2)}, u32[]{:S(2)}) collective-permute-start(f32[112,128]{1,0:T(8,128)S(1)} %add.8.chip), channel_id=1, source_target_pairs={{0,2},{1,3},{2,0},{3,1},{4,6},{5,7},{6,4},{7,5},{8,10},{9,11},{10,... | collective-permute-start | bytes 172040 | tf_op jit(solution)/shard_map/ppermute | solution.py:381
  18.2 4.2 %collective-permute-start.4 = (f32[112,128]{1,0:T(8,128)S(1)}, f32[112,128]{1,0:T(8,128)S(1)}, u32[]{:S(2)}, u32[]{:S(2)}) collective-permute-start(f32[112,128]{1,0:T(8,128)S(1)} %add.8.chip), channel_id=1, source_target_pairs={{0,16},{1,17},{2,18},{3,19},{4,20},{5,21},{6,22},{7,23},{8,24},{9,... | collective-permute-start | bytes 172040 | tf_op jit(solution)/shard_map/ppermute | solution.py:381
  22.4 6.1 %collective-permute-start.9 = (f32[112,128]{1,0:T(8,128)S(1)}, f32[112,128]{1,0:T(8,128)S(1)}, u32[]{:S(2)}, u32[]{:S(2)}) collective-permute-start(f32[112,128]{1,0:T(8,128)S(1)} %line_sum.1.line), channel_id=1, source_target_pairs={{0,12},{1,13},{2,14},{3,15},{4,8},{5,9},{6,10},{7,11},{8,4},{9,5},... | collective-permute-start | bytes 172040 | tf_op jit(solution)/shard_map/ppermute | solution.py:381
  25.6 5.1 %collective-permute-start.8 = (f32[112,128]{1,0:T(8,128)S(1)}, f32[112,128]{1,0:T(8,128)S(1)}, u32[]{:S(2)}, u32[]{:S(2)}) collective-permute-start(f32[112,128]{1,0:T(8,128)S(1)} %line_sum.1.line), channel_id=1, source_target_pairs={{0,4},{1,5},{2,6},{3,7},{4,0},{5,1},{6,2},{7,3},{8,12},{9,13},{10,... | collective-permute-start | bytes 172040 | tf_op jit(solution)/shard_map/ppermute | solution.py:381
  26.0 4.7 %collective-permute-start.7 = (f32[112,128]{1,0:T(8,128)S(1)}, f32[112,128]{1,0:T(8,128)S(1)}, u32[]{:S(2)}, u32[]{:S(2)}) collective-permute-start(f32[112,128]{1,0:T(8,128)S(1)} %line_sum.1.line), channel_id=1, source_target_pairs={{0,8},{1,9},{2,10},{3,11},{4,12},{5,13},{6,14},{7,15},{8,0},{9,1},... | collective-permute-start | bytes 172040 | tf_op jit(solution)/shard_map/ppermute | solution.py:381
  30.7 1.4 %collective-permute-start.10 = (f32[2,112,128]{2,1,0:T(8,128)S(1)}, f32[2,112,128]{2,1,0:T(8,128)S(1)}, u32[]{:S(2)}, u32[]{:S(2)}) collective-permute-start(f32[2,112,128]{2,1,0:T(8,128)S(1)} %last_sum.1.mine), channel_id=1, source_target_pairs={{0,1},{1,0},{2,3},{3,2},{4,5},{5,4},{6,7},{7,6},{8,9},{9,8},{10,11... | collective-permute-start | bytes 344072 | tf_op jit(solution)/shard_map/ppermute | solution.py:342

commit v6 on v5

--- a/solution.py
+++ b/solution.py
@@ -174,23 +174,26 @@
     )(a_rows, g_rows, sums, g_nbr, a_nbr, after)[2:]
 
 
-def pass_kernel(g_own, g_nbr, after, out):
+PASS = jax.ShapeDtypeStruct((16, 6, 8, 128), BF16)
+
+
+def pass_kernel(near, g, after, out):
     row, col, _ = grid_place()
+    first = 3 * (1 - col) + (7 * row if near else 0)
     for plane in range(6):
-        out[0:16, plane] = g_own[:, 7 * row + 3 * (1 - col) + plane]
-        out[16:32, plane] = g_nbr[:, 3 * (1 - col) + plane]
-
-
-def pass_on(g_own, g_nbr, after):
-    return pl.pallas_call(
-        pass_kernel,
-        out_shape=jax.ShapeDtypeStruct((32, 6, 8, 128), BF16),
-        in_specs=[vmem(), vmem(), anywhere()],
+        out[:, plane] = g[:, first + plane]
+
+
+def pass_on(g, after, near):
+    return pl.pallas_call(
+        functools.partial(pass_kernel, near),
+        out_shape=PASS,
+        in_specs=[vmem(), anywhere()],
         out_specs=vmem(),
         compiler_params=pltpu.CompilerParams(vmem_limit_bytes=4 * 2**20),
         cost_estimate=pl.CostEstimate(flops=2**30, bytes_accessed=2**23, transcendentals=0),
-        name="pass_on",
-    )(g_own, g_nbr, after)
+        name="pass_near" if near else "pass_on",
+    )(g, after)
 
 
 def finish_kernel(factor, mine, other, weight_out, bias_out):
@@ -315,26 +318,26 @@
     )(spread, g_own, g_nbr)
 
 
-def far_input_kernel(spread, g_far, near, out, mark, stack):
+def far_input_kernel(spread, g_x, g_diag, near, out, mark, stack):
     row, col, _ = grid_place()
-    stack_planes(row + col, [(g_far, 0, 0)], stack)
+    stack_planes(row + col, [(g_x, 0, 0), (g_diag, 0, 128)], stack)
     total = (banded(spread, 1, stack) + near[...]).astype(BF16)
     for z in range(4):
         out[:, z] = total[:, 128 * z : 128 * z + 128].reshape(32, 8, 128)
     mark[...] = jnp.zeros((8, 128), F32)
 
 
-def far_input(spread, g_far, near):
+def far_input(spread, g_x, g_diag, near):
     return pl.pallas_call(
         far_input_kernel,
         out_shape=(jax.ShapeDtypeStruct((32, 4, 8, 128), BF16), jax.ShapeDtypeStruct((8, 128), F32)),
-        in_specs=[vmem()] * 3,
+        in_specs=[vmem()] * 4,
         out_specs=(vmem(), vmem()),
         scratch_shapes=[pltpu.VMEM((768, 512), BF16)],
         compiler_params=pltpu.CompilerParams(vmem_limit_bytes=10 * 2**20),
         cost_estimate=pl.CostEstimate(flops=9 * 256 * 256 * 512, bytes_accessed=2**22, transcendentals=0),
         name="far_input",
-    )(spread, g_far, near)
+    )(spread, g_x, g_diag, near)
 
 
 def swap(block, axis, bits):
@@ -391,12 +394,13 @@
     g_nbr = swap(lax.dynamic_slice_in_dim(g_own, 7 * (1 - row), 9, axis=1), "slab", 2)
     a_rows, g_rows, sums = near_rows(g_own, act)
     spread = spread_filters(jnp.swapaxes(weight, 1, 2), sums)
+    g_x = swap(pass_on(g_own, spread, True), "slab", 1)
     keep, send = filter_partial(a_rows, g_rows, sums, g_nbr, a_nbr, spread)
     chip = keep + swap(send, "sample", 1)
-    g_far = swap(pass_on(g_own, g_nbr, keep), "slab", 1)
+    g_diag = swap(pass_on(g_nbr, keep, False), "slab", 1)
     near = near_input(spread, g_own, g_nbr)
     line = line_sum(chip, swap_at(chip, 2, 0), swap_at(chip, 0, 2), swap_at(chip, 2, 2), near)
-    grad_in, mark = far_input(spread, g_far, near)
+    grad_in, mark = far_input(spread, g_x, g_diag, near)
     mine = last_sum(line, swap_at(line, 1, 0), swap_at(line, 0, 4), swap_at(line, 1, 4), mark)
     other = swap(mine, "sample", 1)
     cells = 8 * 128 * 4 * lax.axis_size("slab") * lax.axis_size("sample")

time: 33.5 us -> 33.5 us (level)
  waiting for transfers between devices: 6.54 us -> 5.93 us
  starting transfers between devices: 14.2 us -> 14.8 us
    ppermute x5 -> x6, waiting for transfers between devices: 2.22 us -> 1.59 us  [swap(): return lax.ppermute(block, axis, [(i, i ^ bits) for i in range(count)])]
    ppermute x5 -> x6, starting transfers between devices: 6.21 us -> 6.8 us  [swap(): return lax.ppermute(block, axis, [(i, i ^ bits) for i in range(count)])]
  transfers between devices with their start and end apart: 11 -> 12, of which waited for: 7 -> 7; matrix products, arithmetic and copies ran while one was open for 0% -> 0% of each run, Pallas kernels for 15% -> 20%
where the time goes in v6:
time: 33.5 us; the launch traced here: 33.2 us
  starting transfers between devices  14.8 us (44%)
  Pallas kernels  7.8 us (23%)
  waiting for transfers between devices  5.93 us (18%)
  local copies, waits for them, and re-layouts  3.92 us (12%)
  between operations  0.75 us (2%)
    ppermute x6, starting transfers between devices, swap_at(): return lax.ppermute(block, ('slab', 'sample'), pairs)  8.01 us
    ppermute x6, starting transfers between devices, swap(): return lax.ppermute(block, axis, [(i, i ^ bits) for i in range(count)])  6.8 us
    ppermute x6, waiting for transfers between devices, swap_at(): return lax.ppermute(block, ('slab', 'sample'), pairs)  4.34 us
    unnamed x8, local copies, waits for them, and re-layouts  2.93 us
    pallas_call x1, Pallas kernels, spread_filters(): pl.pallas_call(spread_kernel, out_shape=jax.ShapeDtypeStruct((2, 3, 256,...  2.13 us
    ppermute x6, waiting for transfers between devices, swap(): return lax.ppermute(block, axis, [(i, i ^ bits) for i in range(count)])  1.59 us
    pallas_call x1, Pallas kernels, far_input(): pl.pallas_call(far_input_kernel, out_shape=(jax.ShapeDtypeStruct((32, 4,...  1.58 us
    pallas_call x1, Pallas kernels, filter_partial(): pl.pallas_call(filter_kernel, out_shape=ROWS + (half, half), in_specs=[vm...  1.53 us
  transfers between devices with their start and end apart: 12, of which 7 were waited for; matrix products, arithmetic and copies ran while one was open for 0% of the time, Pallas kernels for 20%

profile of v6, /device:TPU:0, one launch (start us, length us, event | category | flops | bytes accessed | tf_op | source)
XLA Modules:
  0.0 33.2 jit_solution(9728477283192505878)
XLA Ops:
  0.6 1.0 %dynamic-slice_bitcast_fusion = bf16[16,9,8,128]{3,2,1,0:T(8,128)(2,1)S(1)} fusion(bf16[1,16,16,8,128]{4,3,2,1,0:T(8,128)(2,1)} %param.4, s32[]{:T(128)S(6)} %select_n.9), kind=kLoop, calls=%fused_computation | loop fusion | bytes 589828 | tf_op jit(solution)/shard_map/dynamic_slice | solution.py:394
  1.6 3.0 %collective-permute-start.1 = (bf16[16,9,8,128]{3,2,1,0:T(8,128)(2,1)S(1)}, bf16[16,9,8,128]{3,2,1,0:T(8,128)(2,1)S(1)}, u32[]{:S(2)}, u32[]{:S(2)}) collective-permute-start(bf16[16,9,8,128]{3,2,1,0:T(8,128)(2,1)S(1)} %dynamic-slice_bitcast_fusion), channel_id=1, source_target_pairs={{0,16},{8,24},{16,0},{24,8},{1,17},{9,25},{17,1},{25,9},{2,18},{10... | collective-permute-start | bytes 884744 | tf_op jit(solution)/shard_map/ppermute | solution.py:345
  4.7 1.5 %collective-permute-start.2 = (bf16[32,4,8,128]{3,2,1,0:T(8,128)(2,1)}, bf16[32,4,8,128]{3,2,1,0:T(8,128)(2,1)S(1)}, u32[]{:S(2)}, u32[]{:S(2)}) collective-permute-start(bf16[32,4,8,128]{3,2,1,0:T(8,128)(2,1)} %bitcast.12), channel_id=1, source_target_pairs={{0,8},{8,0},{16,24},{24,16},{1,9},{9,1},{17,25},{25,17},{2,10},{10... | collective-permute-start | bytes 786440 | tf_op jit(solution)/shard_map/ppermute | solution.py:345
  6.2 0.0 copy-start.1
  6.2 1.0 %copy-done.1 = bf16[1,16,16,8,128]{4,3,2,1,0:T(8,128)(2,1)S(1)} copy-done((bf16[1,16,16,8,128]{4,3,2,1,0:T(8,128)(2,1)S(1)}, bf16[1,16,16,8,128]{4,3,2,1,0:T(8,128)(2,1)}, u32[]{:S(2)}) %copy-start.1) | copy-done | bytes 524312
  7.2 0.0 copy-start.3
  7.2 0.9 %copy-done.3 = bf16[1,32,4,8,128]{4,3,2,1,0:T(8,128)(2,1)S(1)} copy-done((bf16[1,32,4,8,128]{4,3,2,1,0:T(8,128)(2,1)S(1)}, bf16[1,32,4,8,128]{4,3,2,1,0:T(8,128)(2,1)}, u32[]{:S(2)}) %copy-start.3) | copy-done | bytes 262168
  8.2 0.5 %near_rows.1 = (bf16[8,32,1280]{2,1,0:T(8,128)(2,1)S(1)}, bf16[10,128,1024]{2,1,0:T(8,128)(2,1)S(1)}, f32[16,128]{1,0:T(8,128)S(1)}) custom-call(bf16[16,16,8,128]{3,2,1,0:T(8,128)(2,1)S(1)} %bitcast.9, bf16[32,4,8,128]{3,2,1,0:T(8,128)(2,1)S(1)} %bitcast.13), custom_call_target="tpu_custom_call" | custom-call | flops 268435456 | bytes 2097152 | tf_op jit(solution)/shard_map/near_rows/pallas_call | solution.py:112
  8.7 0.0 copy-start
  8.7 0.9 %copy-done = bf16[27,64,32]{1,2,0:T(8,128)(2,1)S(1)} copy-done((bf16[27,64,32]{1,2,0:T(8,128)(2,1)S(1)}, bf16[27,64,32]{1,2,0:T(8,128)(2,1)}, u32[]{:S(2)}) %copy-start) | copy-done | bytes 110616
  9.6 2.1 %spread_filters.1.after.spread = bf16[2,3,256,768]{3,2,1,0:T(8,128)(2,1)S(1)} custom-call(bf16[27,32,64]{2,1,0:T(8,128)(2,1)S(1)} %bitcast.8, f32[16,128]{1,0:T(8,128)S(1)} %get-tuple-element.12.after.sums), custom_call_target="tpu_custom_call" | custom-call | flops 452984832 | bytes 2097152 | tf_op jit(solution)/shard_map/spread_filters/pallas_call | solution.py:267
  11.8 0.6 %collective-permute-start = (bf16[16,6,8,128]{3,2,1,0:T(8,128)(2,1)S(1)}, bf16[16,6,8,128]{3,2,1,0:T(8,128)(2,1)S(1)}, u32[]{:S(2)}, u32[]{:S(2)}) collective-permute-start(bf16[16,6,8,128]{3,2,1,0:T(8,128)(2,1)S(1)} %pass_near.1), channel_id=1, source_target_pairs={{0,8},{8,0},{16,24},{24,16},{1,9},{9,1},{17,25},{25,17},{2,10},{10... | collective-permute-start | bytes 589832 | tf_op jit(solution)/shard_map/ppermute | solution.py:345
  12.4 0.3 collective-permute-done.2.a_nbr
  12.7 0.0 collective-permute-done.1.g_nbr.g
  12.7 1.5 %filter_partial.1 = (bf16[8,32,1280]{2,1,0:T(8,128)(2,1)S(1)}, bf16[10,128,1024]{2,1,0:T(8,128)(2,1)S(1)}, f32[112,128]{1,0:T(8,128)S(1)}, f32[112,128]{1,0:T(8,128)S(1)}) custom-call(bf16[8,32,1280]{2,1,0:T(8,128)(2,1)S(1)} %get-tuple-element.13.a_in, ...), custom_call_target="tpu_custom_call", output_to_operand_aliasing={{0}: (0, {}), {1}: (1, {})} | custom-call | flops 566231040 | bytes 2097152 | tf_op jit(solution)/shard_map/filter_partial/pallas_call | solution.py:165
  14.2 0.0 copy-start.2
  14.2 0.1 collective-permute-start.4
  14.3 1.5 %collective-permute-start.3 = (bf16[16,6,8,128]{3,2,1,0:T(8,128)(2,1)S(1)}, bf16[16,6,8,128]{3,2,1,0:T(8,128)(2,1)S(1)}, u32[]{:S(2)}, u32[]{:S(2)}) collective-permute-start(bf16[16,6,8,128]{3,2,1,0:T(8,128)(2,1)S(1)} %pass_on.1), channel_id=1, source_target_pairs={{0,8},{8,0},{16,24},{24,16},{1,9},{9,1},{17,25},{25,17},{2,10},{10... | collective-permute-start | bytes 589832 | tf_op jit(solution)/shard_map/ppermute | solution.py:345
  15.9 0.0 collective-permute-done.4
  15.9 1.9 %collective-permute-start.7 = (f32[112,128]{1,0:T(8,128)S(1)}, f32[112,128]{1,0:T(8,128)S(1)}, u32[]{:S(2)}, u32[]{:S(2)}) collective-permute-start(f32[112,128]{1,0:T(8,128)S(1)} %add.8.chip), channel_id=1, source_target_pairs={{0,18},{1,19},{2,16},{3,17},{4,22},{5,23},{6,20},{7,21},{8,26},{9,... | collective-permute-start | bytes 172040 | tf_op jit(solution)/shard_map/ppermute | solution.py:384
  17.8 0.5 %collective-permute-start.6 = (f32[112,128]{1,0:T(8,128)S(1)}, f32[112,128]{1,0:T(8,128)S(1)}, u32[]{:S(2)}, u32[]{:S(2)}) collective-permute-start(f32[112,128]{1,0:T(8,128)S(1)} %add.8.chip), channel_id=1, source_target_pairs={{0,2},{1,3},{2,0},{3,1},{4,6},{5,7},{6,4},{7,5},{8,10},{9,11},{10,... | collective-permute-start | bytes 172040 | tf_op jit(solution)/shard_map/ppermute | solution.py:384
  18.2 1.2 %collective-permute-start.5 = (f32[112,128]{1,0:T(8,128)S(1)}, f32[112,128]{1,0:T(8,128)S(1)}, u32[]{:S(2)}, u32[]{:S(2)}) collective-permute-start(f32[112,128]{1,0:T(8,128)S(1)} %add.8.chip), channel_id=1, source_target_pairs={{0,16},{1,17},{2,18},{3,19},{4,20},{5,21},{6,22},{7,23},{8,24},{9,... | collective-permute-start | bytes 172040 | tf_op jit(solution)/shard_map/ppermute | solution.py:384
  19.4 0.0 copy-done.2
  19.4 0.9 %near_input.1.near.after = f32[256,512]{1,0:T(8,128)S(1)} custom-call(bf16[2,3,256,768]{3,2,1,0:T(8,128)(2,1)S(1)} %spread_filters.1.after.spread, bf16[16,16,8,128]{3,2,1,0:T(8,128)(2,1)S(1)} %bitcast.11, bf16[16,9,8,128]{3,2,1,0:T(8,128)(2,1)S(1)} %collective-permute-done.1.g_nbr.g), custom_call_target="tpu_custom_call" | custom-call | flops 8589934592 | bytes 33554432 | tf_op jit(solution)/shard_map/near_input/pallas_call | solution.py:309
  20.3 0.9 %collective-permute-done.7.both_off = f32[112,128]{1,0:T(8,128)S(1)} collective-permute-done((f32[112,128]{1,0:T(8,128)S(1)}, f32[112,128]{1,0:T(8,128)S(1)}, u32[]{:S(2)}, u32[]{:S(2)}) %collective-permute-start.7) | collective-permute-done | bytes 57376 | tf_op jit(solution)/shard_map/ppermute | solution.py:384
  21.2 0.8 %collective-permute-done.6.two_off = f32[112,128]{1,0:T(8,128)S(1)} collective-permute-done((f32[112,128]{1,0:T(8,128)S(1)}, f32[112,128]{1,0:T(8,128)S(1)}, u32[]{:S(2)}, u32[]{:S(2)}) %collective-permute-start.6) | collective-permute-done | bytes 57376 | tf_op jit(solution)/shard_map/ppermute | solution.py:384
  21.9 0.5 %collective-permute-done.5.one_off = f32[112,128]{1,0:T(8,128)S(1)} collective-permute-done((f32[112,128]{1,0:T(8,128)S(1)}, f32[112,128]{1,0:T(8,128)S(1)}, u32[]{:S(2)}, u32[]{:S(2)}) %collective-permute-start.5) | collective-permute-done | bytes 57376 | tf_op jit(solution)/shard_map/ppermute | solution.py:384
  22.4 3.2 %collective-permute-start.10 = (f32[112,128]{1,0:T(8,128)S(1)}, f32[112,128]{1,0:T(8,128)S(1)}, u32[]{:S(2)}, u32[]{:S(2)}) collective-permute-start(f32[112,128]{1,0:T(8,128)S(1)} %line_sum.1.line), channel_id=1, source_target_pairs={{0,12},{1,13},{2,14},{3,15},{4,8},{5,9},{6,10},{7,11},{8,4},{9,5},... | collective-permute-start | bytes 172040 | tf_op jit(solution)/shard_map/ppermute | solution.py:384
  25.6 0.3 %collective-permute-start.9 = (f32[112,128]{1,0:T(8,128)S(1)}, f32[112,128]{1,0:T(8,128)S(1)}, u32[]{:S(2)}, u32[]{:S(2)}) collective-permute-start(f32[112,128]{1,0:T(8,128)S(1)} %line_sum.1.line), channel_id=1, source_target_pairs={{0,4},{1,5},{2,6},{3,7},{4,0},{5,1},{6,2},{7,3},{8,12},{9,13},{10,... | collective-permute-start | bytes 172040 | tf_op jit(solution)/shard_map/ppermute | solution.py:384
  26.0 0.9 %collective-permute-start.8 = (f32[112,128]{1,0:T(8,128)S(1)}, f32[112,128]{1,0:T(8,128)S(1)}, u32[]{:S(2)}, u32[]{:S(2)}) collective-permute-start(f32[112,128]{1,0:T(8,128)S(1)} %line_sum.1.line), channel_id=1, source_target_pairs={{0,8},{1,9},{2,10},{3,11},{4,12},{5,13},{6,14},{7,15},{8,0},{9,1},... | collective-permute-start | bytes 172040 | tf_op jit(solution)/shard_map/ppermute | solution.py:384
  26.9 0.0 collective-permute-done.g_x
  26.9 0.0 collective-permute-done.3.g_diag
  26.9 1.6 %far_input.1 = (bf16[32,4,8,128]{3,2,1,0:T(8,128)(2,1)}, f32[8,128]{1,0:T(8,128)S(1)}) custom-call(bf16[2,3,256,768]{3,2,1,0:T(8,128)(2,1)S(1)} %spread_filters.1.after.spread, bf16[16,6,8,128]{3,2,1,0:T(8,128)(2,1)S(1)} %collective-permute-done.g_x, bf16[16,6,8,128]{3,2,1,0:T(8,128)(2,1)S(1)} %collective-permute-done.3.g_diag, ...), custom_call_target="tpu_custom_call" | custom-call | flops 301989888 | bytes 4194304 | tf_op jit(solution)/shard_map/far_input/pallas_call | solution.py:331
  28.5 0.1 collective-permute-done.10.diagonal
  28.5 2.2 %collective-permute-done.9.across = f32[112,128]{1,0:T(8,128)S(1)} collective-permute-done((f32[112,128]{1,0:T(8,128)S(1)}, f32[112,128]{1,0:T(8,128)S(1)}, u32[]{:S(2)}, u32[]{:S(2)}) %collective-permute-start.9) | collective-permute-done | bytes 57376 | tf_op jit(solution)/shard_map/ppermute | solution.py:384
  30.7 0.0 collective-permute-done.8.beside
  30.7 0.1 collective-permute-start.11
  30.8 1.3 %collective-permute-done.11.other = f32[2,112,128]{2,1,0:T(8,128)S(1)} collective-permute-done((f32[2,112,128]{2,1,0:T(8,128)S(1)}, f32[2,112,128]{2,1,0:T(8,128)S(1)}, u32[]{:S(2)}, u32[]{:S(2)}) %collective-permute-start.11) | collective-permute-done | bytes 114720 | tf_op jit(solution)/shard_map/ppermute | solution.py:345
  32.1 1.1 %filter_finish.1 = (f32[27,32,64]{2,1,0:T(8,128)}, f32[1,64]{1,0:T(1,128)}) custom-call(f32[2,112,128]{2,1,0:T(8,128)S(1)} %last_sum.1.mine, f32[2,112,128]{2,1,0:T(8,128)S(1)} %collective-permute-done.11.other), custom_call_target="tpu_custom_call" | custom-call | flops 262144 | bytes 1048576 | tf_op jit(solution)/shard_map/filter_finish/pallas_call | solution.py:231
  (5 shorter events, 0.1 us)
Async XLA Ops:
  1.6 11.0 %collective-permute-start.1 = (bf16[16,9,8,128]{3,2,1,0:T(8,128)(2,1)S(1)}, bf16[16,9,8,128]{3,2,1,0:T(8,128)(2,1)S(1)}, u32[]{:S(2)}, u32[]{:S(2)}) collective-permute-start(bf16[16,9,8,128]{3,2,1,0:T(8,128)(2,1)S(1)} %dynamic-slice_bitcast_fusion), channel_id=1, source_target_pairs={{0,16},{8,24},{16,0},{24,8},{1,17},{9,25},{17,1},{25,9},{2,18},{10... | collective-permute-start | bytes 884744 | tf_op jit(solution)/shard_map/ppermute | solution.py:345
  4.7 8.0 %collective-permute-start.2 = (bf16[32,4,8,128]{3,2,1,0:T(8,128)(2,1)}, bf16[32,4,8,128]{3,2,1,0:T(8,128)(2,1)S(1)}, u32[]{:S(2)}, u32[]{:S(2)}) collective-permute-start(bf16[32,4,8,128]{3,2,1,0:T(8,128)(2,1)} %bitcast.12), channel_id=1, source_target_pairs={{0,8},{8,0},{16,24},{24,16},{1,9},{9,1},{17,25},{25,17},{2,10},{10... | collective-permute-start | bytes 786440 | tf_op jit(solution)/shard_map/ppermute | solution.py:345
  6.2 1.0 %copy-start.1 = (bf16[1,16,16,8,128]{4,3,2,1,0:T(8,128)(2,1)S(1)}, bf16[1,16,16,8,128]{4,3,2,1,0:T(8,128)(2,1)}, u32[]{:S(2)}) copy-start(bf16[1,16,16,8,128]{4,3,2,1,0:T(8,128)(2,1)} %param.4) | copy-start | bytes 1572868
  7.2 0.9 %copy-start.3 = (bf16[1,32,4,8,128]{4,3,2,1,0:T(8,128)(2,1)S(1)}, bf16[1,32,4,8,128]{4,3,2,1,0:T(8,128)(2,1)}, u32[]{:S(2)}) copy-start(bf16[1,32,4,8,128]{4,3,2,1,0:T(8,128)(2,1)} %param.3) | copy-start | bytes 786436
  8.7 0.9 %copy-start = (bf16[27,64,32]{1,2,0:T(8,128)(2,1)S(1)}, bf16[27,64,32]{1,2,0:T(8,128)(2,1)}, u32[]{:S(2)}) copy-start(bf16[27,64,32]{1,2,0:T(8,128)(2,1)} %param.5) | copy-start | bytes 331780
  11.8 15.1 %collective-permute-start = (bf16[16,6,8,128]{3,2,1,0:T(8,128)(2,1)S(1)}, bf16[16,6,8,128]{3,2,1,0:T(8,128)(2,1)S(1)}, u32[]{:S(2)}, u32[]{:S(2)}) collective-permute-start(bf16[16,6,8,128]{3,2,1,0:T(8,128)(2,1)S(1)} %pass_near.1), channel_id=1, source_target_pairs={{0,8},{8,0},{16,24},{24,16},{1,9},{9,1},{17,25},{25,17},{2,10},{10... | collective-permute-start | bytes 589832 | tf_op jit(solution)/shard_map/ppermute | solution.py:345
  14.2 5.2 %copy-start.2 = (bf16[1,16,16,8,128]{4,3,2,1,0:T(8,128)(2,1)S(1)}, bf16[1,16,16,8,128]{4,3,2,1,0:T(8,128)(2,1)}, u32[]{:S(2)}) copy-start(bf16[1,16,16,8,128]{4,3,2,1,0:T(8,128)(2,1)} %param.4) | copy-start | bytes 1572868
  14.2 1.7 %collective-permute-start.4 = (f32[112,128]{1,0:T(8,128)S(1)}, f32[112,128]{1,0:T(8,128)S(1)}, u32[]{:S(2)}, u32[]{:S(2)}) collective-permute-start(f32[112,128]{1,0:T(8,128)S(1)} %get-tuple-element.17), channel_id=1, source_target_pairs={{0,1},{1,0},{2,3},{3,2},{4,5},{5,4},{6,7},{7,6},{8,9},{9,8},{10,11... | collective-permute-start | bytes 172040 | tf_op jit(solution)/shard_map/ppermute | solution.py:345
  14.3 12.5 %collective-permute-start.3 = (bf16[16,6,8,128]{3,2,1,0:T(8,128)(2,1)S(1)}, bf16[16,6,8,128]{3,2,1,0:T(8,128)(2,1)S(1)}, u32[]{:S(2)}, u32[]{:S(2)}) collective-permute-start(bf16[16,6,8,128]{3,2,1,0:T(8,128)(2,1)S(1)} %pass_on.1), channel_id=1, source_target_pairs={{0,8},{8,0},{16,24},{24,16},{1,9},{9,1},{17,25},{25,17},{2,10},{10... | collective-permute-start | bytes 589832 | tf_op jit(solution)/shard_map/ppermute | solution.py:345
  15.9 5.3 %collective-permute-start.7 = (f32[112,128]{1,0:T(8,128)S(1)}, f32[112,128]{1,0:T(8,128)S(1)}, u32[]{:S(2)}, u32[]{:S(2)}) collective-permute-start(f32[112,128]{1,0:T(8,128)S(1)} %add.8.chip), channel_id=1, source_target_pairs={{0,18},{1,19},{2,16},{3,17},{4,22},{5,23},{6,20},{7,21},{8,26},{9,... | collective-permute-start | bytes 172040 | tf_op jit(solution)/shard_map/ppermute | solution.py:384
  17.8 4.2 %collective-permute-start.6 = (f32[112,128]{1,0:T(8,128)S(1)}, f32[112,128]{1,0:T(8,128)S(1)}, u32[]{:S(2)}, u32[]{:S(2)}) collective-permute-start(f32[112,128]{1,0:T(8,128)S(1)} %add.8.chip), channel_id=1, source_target_pairs={{0,2},{1,3},{2,0},{3,1},{4,6},{5,7},{6,4},{7,5},{8,10},{9,11},{10,... | collective-permute-start | bytes 172040 | tf_op jit(solution)/shard_map/ppermute | solution.py:384
  18.2 4.2 %collective-permute-start.5 = (f32[112,128]{1,0:T(8,128)S(1)}, f32[112,128]{1,0:T(8,128)S(1)}, u32[]{:S(2)}, u32[]{:S(2)}) collective-permute-start(f32[112,128]{1,0:T(8,128)S(1)} %add.8.chip), channel_id=1, source_target_pairs={{0,16},{1,17},{2,18},{3,19},{4,20},{5,21},{6,22},{7,23},{8,24},{9,... | collective-permute-start | bytes 172040 | tf_op jit(solution)/shard_map/ppermute | solution.py:384
  22.4 6.1 %collective-permute-start.10 = (f32[112,128]{1,0:T(8,128)S(1)}, f32[112,128]{1,0:T(8,128)S(1)}, u32[]{:S(2)}, u32[]{:S(2)}) collective-permute-start(f32[112,128]{1,0:T(8,128)S(1)} %line_sum.1.line), channel_id=1, source_target_pairs={{0,12},{1,13},{2,14},{3,15},{4,8},{5,9},{6,10},{7,11},{8,4},{9,5},... | collective-permute-start | bytes 172040 | tf_op jit(solution)/shard_map/ppermute | solution.py:384
  25.6 5.1 %collective-permute-start.9 = (f32[112,128]{1,0:T(8,128)S(1)}, f32[112,128]{1,0:T(8,128)S(1)}, u32[]{:S(2)}, u32[]{:S(2)}) collective-permute-start(f32[112,128]{1,0:T(8,128)S(1)} %line_sum.1.line), channel_id=1, source_target_pairs={{0,4},{1,5},{2,6},{3,7},{4,0},{5,1},{6,2},{7,3},{8,12},{9,13},{10,... | collective-permute-start | bytes 172040 | tf_op jit(solution)/shard_map/ppermute | solution.py:384
  26.0 4.7 %collective-permute-start.8 = (f32[112,128]{1,0:T(8,128)S(1)}, f32[112,128]{1,0:T(8,128)S(1)}, u32[]{:S(2)}, u32[]{:S(2)}) collective-permute-start(f32[112,128]{1,0:T(8,128)S(1)} %line_sum.1.line), channel_id=1, source_target_pairs={{0,8},{1,9},{2,10},{3,11},{4,12},{5,13},{6,14},{7,15},{8,0},{9,1},... | collective-permute-start | bytes 172040 | tf_op jit(solution)/shard_map/ppermute | solution.py:384
  30.7 1.4 %collective-permute-start.11 = (f32[2,112,128]{2,1,0:T(8,128)S(1)}, f32[2,112,128]{2,1,0:T(8,128)S(1)}, u32[]{:S(2)}, u32[]{:S(2)}) collective-permute-start(f32[2,112,128]{2,1,0:T(8,128)S(1)} %last_sum.1.mine), channel_id=1, source_target_pairs={{0,1},{1,0},{2,3},{3,2},{4,5},{5,4},{6,7},{7,6},{8,9},{9,8},{10,11... | collective-permute-start | bytes 344072 | tf_op jit(solution)/shard_map/ppermute | solution.py:345

commit v7 on v5

--- a/solution.py
+++ b/solution.py
@@ -32,10 +32,6 @@
 
 def one(mask):
     return mask.astype(F32).astype(BF16)
-
-
-def turn_planes(turned, shift_rows, store):
-    pass
 
 
 def act_rows(source, put):
@@ -193,15 +189,9 @@
     )(g_own, g_nbr, after)
 
 
-def finish_kernel(factor, mine, other, weight_out, bias_out):
-    _, col, core = grid_place()
-    lane = iota((224, 128), 1)
-    tables = []
-    for x in range(2):
-        which = jnp.where(col == x, 0, 1)
-        a, b = mine[which], other[which]
-        low, high = jnp.where(core == 0, a, b), jnp.where(core == 0, b, a)
-        tables.append(jnp.concatenate([low, high], axis=0) * factor)
+def arranged(factor, col, halves):
+    lane = iota((112, 128), 1)
+    tables = [halves[jnp.where(col == x, 0, 1)] * factor for x in range(2)]
     even = (lane & 16) == 0
     first = jnp.where(even, tables[0], pltpu.roll(tables[1], 16, 1))
     second = jnp.where(even, pltpu.roll(tables[0], 112, 1), tables[1])
@@ -210,6 +200,32 @@
         left = pltpu.roll(first, 128 - 32 * dx, 1) if dx else first
         right = pltpu.roll(second, (160 - 32 * dx) % 128, 1) if dx != 1 else second
         whole.append(jnp.where(lane < 32, left, right))
+    return whole
+
+
+def prepare_kernel(factor, mine, out):
+    _, col, _ = grid_place()
+    for dx, value in enumerate(arranged(factor, col, mine)):
+        out[dx] = value
+
+
+def prepare(mine, factor):
+    return pl.pallas_call(
+        functools.partial(prepare_kernel, factor),
+        out_shape=jax.ShapeDtypeStruct((4, 112, 128), F32),
+        in_specs=[vmem()],
+        out_specs=vmem(),
+        compiler_params=pltpu.CompilerParams(vmem_limit_bytes=2 * 2**20),
+        cost_estimate=pl.CostEstimate(flops=2**18, bytes_accessed=2**19, transcendentals=0),
+        name="prepare",
+    )(mine)
+
+
+def finish_body(core, ready, other, weight_out, bias_out):
+    whole = []
+    for dx in range(4):
+        halves = (ready[dx], other[dx]) if core == 0 else (other[dx], ready[dx])
+        whole.append(jnp.concatenate(halves, axis=0))
     for nine in range(9):
         for dx in range(3):
             k = 3 * nine + dx
@@ -224,7 +240,16 @@
     bias_out[...] = whole[0][216:217, 0:64]
 
 
-def finish(mine, other, factor):
+def finish_kernel(factor, ready, other, weight_out, bias_out):
+    _, col, core = grid_place()
+    for c in range(2):
+
+        @pl.when(core == c)
+        def _(c=c):
+            finish_body(c, ready, arranged(factor, col, other), weight_out, bias_out)
+
+
+def finish(ready, other, factor):
     return pl.pallas_call(
         functools.partial(finish_kernel, factor),
         out_shape=(jax.ShapeDtypeStruct((27, 32, 64), F32), jax.ShapeDtypeStruct((1, 64), F32)),
@@ -233,7 +258,7 @@
         compiler_params=pltpu.CompilerParams(vmem_limit_bytes=4 * 2**20),
         cost_estimate=pl.CostEstimate(flops=2**18, bytes_accessed=2**20, transcendentals=0),
         name="filter_finish",
-    )(mine, other)
+    )(ready, other)
 
 
 def spread_kernel(weight, after, out):
@@ -400,7 +425,8 @@
     mine = last_sum(line, swap_at(line, 1, 0), swap_at(line, 0, 4), swap_at(line, 1, 4), mark)
     other = swap(mine, "sample", 1)
     cells = 8 * 128 * 4 * lax.axis_size("slab") * lax.axis_size("sample")
-    grad_weight, grad_bias = finish(mine, other, 1.0 / math.sqrt(cells))
+    factor = 1.0 / math.sqrt(cells)
+    grad_weight, grad_bias = finish(prepare(mine, factor), other, factor)
     return grad_in[None], jnp.swapaxes(grad_weight, 1, 2), grad_bias.reshape(64)
 
 

time: 33.5 us -> 33.4 us (level)
  transfers between devices with their start and end apart: 11 -> 11, of which waited for: 7 -> 7; matrix products, arithmetic and copies ran while one was open for 0% -> 0% of each run, Pallas kernels for 15% -> 16%
where the time goes in v7:
time: 33.4 us; the launch traced here: 33.1 us
  starting transfers between devices  14.2 us (43%)
  Pallas kernels  7.93 us (24%)
  waiting for transfers between devices  6.28 us (19%)
  local copies, waits for them, and re-layouts  3.92 us (12%)
  between operations  0.75 us (2%)
    ppermute x6, starting transfers between devices, swap_at(): return lax.ppermute(block, ('slab', 'sample'), pairs)  8.01 us
    ppermute x5, starting transfers between devices, swap(): return lax.ppermute(block, axis, [(i, i ^ bits) for i in range(count)])  6.21 us
    ppermute x6, waiting for transfers between devices, swap_at(): return lax.ppermute(block, ('slab', 'sample'), pairs)  4.32 us
    unnamed x8, local copies, waits for them, and re-layouts  2.93 us
    pallas_call x1, Pallas kernels, spread_filters(): pl.pallas_call(spread_kernel, out_shape=jax.ShapeDtypeStruct((2, 3, 256,...  2.13 us
    ppermute x5, waiting for transfers between devices, swap(): return lax.ppermute(block, axis, [(i, i ^ bits) for i in range(count)])  1.96 us
    pallas_call x1, Pallas kernels, far_input(): pl.pallas_call(far_input_kernel, out_shape=(jax.ShapeDtypeStruct((32, 4,...  1.59 us
    pallas_call x1, Pallas kernels, filter_partial(): pl.pallas_call(filter_kernel, out_shape=ROWS + (half, half), in_specs=[vm...  1.53 us
  transfers between devices with their start and end apart: 11, of which 7 were waited for; matrix products, arithmetic and copies ran while one was open for 0% of the time, Pallas kernels for 16%

profile of v7, /device:TPU:0, one launch (start us, length us, event | category | flops | bytes accessed | tf_op | source)
XLA Modules:
  0.0 33.1 jit_solution(11099727720141412686)
XLA Ops:
  0.6 1.0 %dynamic-slice_bitcast_fusion = bf16[16,9,8,128]{3,2,1,0:T(8,128)(2,1)S(1)} fusion(bf16[1,16,16,8,128]{4,3,2,1,0:T(8,128)(2,1)} %param.4, s32[]{:T(128)S(6)} %select_n.9), kind=kLoop, calls=%fused_computation | loop fusion | bytes 589828 | tf_op jit(solution)/shard_map/dynamic_slice | solution.py:416
  1.6 3.0 %collective-permute-start = (bf16[16,9,8,128]{3,2,1,0:T(8,128)(2,1)S(1)}, bf16[16,9,8,128]{3,2,1,0:T(8,128)(2,1)S(1)}, u32[]{:S(2)}, u32[]{:S(2)}) collective-permute-start(bf16[16,9,8,128]{3,2,1,0:T(8,128)(2,1)S(1)} %dynamic-slice_bitcast_fusion), channel_id=1, source_target_pairs={{0,16},{8,24},{16,0},{24,8},{1,17},{9,25},{17,1},{25,9},{2,18},{10... | collective-permute-start | bytes 884744 | tf_op jit(solution)/shard_map/ppermute | solution.py:367
  4.7 1.5 %collective-permute-start.1 = (bf16[32,4,8,128]{3,2,1,0:T(8,128)(2,1)}, bf16[32,4,8,128]{3,2,1,0:T(8,128)(2,1)S(1)}, u32[]{:S(2)}, u32[]{:S(2)}) collective-permute-start(bf16[32,4,8,128]{3,2,1,0:T(8,128)(2,1)} %bitcast.12), channel_id=1, source_target_pairs={{0,8},{8,0},{16,24},{24,16},{1,9},{9,1},{17,25},{25,17},{2,10},{10... | collective-permute-start | bytes 786440 | tf_op jit(solution)/shard_map/ppermute | solution.py:367
  6.2 0.0 copy-start.1
  6.2 1.0 %copy-done.1 = bf16[1,16,16,8,128]{4,3,2,1,0:T(8,128)(2,1)S(1)} copy-done((bf16[1,16,16,8,128]{4,3,2,1,0:T(8,128)(2,1)S(1)}, bf16[1,16,16,8,128]{4,3,2,1,0:T(8,128)(2,1)}, u32[]{:S(2)}) %copy-start.1) | copy-done | bytes 524312
  7.2 0.0 copy-start.3
  7.2 0.9 %copy-done.3 = bf16[1,32,4,8,128]{4,3,2,1,0:T(8,128)(2,1)S(1)} copy-done((bf16[1,32,4,8,128]{4,3,2,1,0:T(8,128)(2,1)S(1)}, bf16[1,32,4,8,128]{4,3,2,1,0:T(8,128)(2,1)}, u32[]{:S(2)}) %copy-start.3) | copy-done | bytes 262168
  8.2 0.5 %near_rows.1 = (bf16[8,32,1280]{2,1,0:T(8,128)(2,1)S(1)}, bf16[10,128,1024]{2,1,0:T(8,128)(2,1)S(1)}, f32[16,128]{1,0:T(8,128)S(1)}) custom-call(bf16[16,16,8,128]{3,2,1,0:T(8,128)(2,1)S(1)} %bitcast.9, bf16[32,4,8,128]{3,2,1,0:T(8,128)(2,1)S(1)} %bitcast.13), custom_call_target="tpu_custom_call" | custom-call | flops 268435456 | bytes 2097152 | tf_op jit(solution)/shard_map/near_rows/pallas_call | solution.py:108
  8.7 0.0 copy-start
  8.7 0.9 %copy-done = bf16[27,64,32]{1,2,0:T(8,128)(2,1)S(1)} copy-done((bf16[27,64,32]{1,2,0:T(8,128)(2,1)S(1)}, bf16[27,64,32]{1,2,0:T(8,128)(2,1)}, u32[]{:S(2)}) %copy-start) | copy-done | bytes 110616
  9.6 2.1 %spread_filters.1.after.spread = bf16[2,3,256,768]{3,2,1,0:T(8,128)(2,1)S(1)} custom-call(bf16[27,32,64]{2,1,0:T(8,128)(2,1)S(1)} %bitcast.8, f32[16,128]{1,0:T(8,128)S(1)} %get-tuple-element.12.after.sums), custom_call_target="tpu_custom_call" | custom-call | flops 452984832 | bytes 2097152 | tf_op jit(solution)/shard_map/spread_filters/pallas_call | solution.py:289
  11.8 0.9 %collective-permute-done.1.a_nbr = bf16[32,4,8,128]{3,2,1,0:T(8,128)(2,1)S(1)} collective-permute-done((bf16[32,4,8,128]{3,2,1,0:T(8,128)(2,1)}, bf16[32,4,8,128]{3,2,1,0:T(8,128)(2,1)S(1)}, u32[]{:S(2)}, u32[]{:S(2)}) %collective-permute-start.1) | collective-permute-done | bytes 262176 | tf_op jit(solution)/shard_map/ppermute | solution.py:367
  12.7 0.0 collective-permute-done.g_nbr
  12.7 0.0 copy-start.2
  12.7 1.5 %filter_partial.1 = (bf16[8,32,1280]{2,1,0:T(8,128)(2,1)S(1)}, bf16[10,128,1024]{2,1,0:T(8,128)(2,1)S(1)}, f32[112,128]{1,0:T(8,128)S(1)}, f32[112,128]{1,0:T(8,128)S(1)}) custom-call(bf16[8,32,1280]{2,1,0:T(8,128)(2,1)S(1)} %get-tuple-element.13.a_in, ...), custom_call_target="tpu_custom_call", output_to_operand_aliasing={{0}: (0, {}), {1}: (1, {})} | custom-call | flops 566231040 | bytes 2097152 | tf_op jit(solution)/shard_map/filter_partial/pallas_call | solution.py:161
  14.2 0.1 collective-permute-start.3
  14.3 0.0 copy-done.2
  14.3 0.1 pass_on.1
  14.3 1.5 %collective-permute-start.2 = (bf16[32,6,8,128]{3,2,1,0:T(8,128)(2,1)S(1)}, bf16[32,6,8,128]{3,2,1,0:T(8,128)(2,1)S(1)}, u32[]{:S(2)}, u32[]{:S(2)}) collective-permute-start(bf16[32,6,8,128]{3,2,1,0:T(8,128)(2,1)S(1)} %pass_on.1), channel_id=1, source_target_pairs={{0,8},{8,0},{16,24},{24,16},{1,9},{9,1},{17,25},{25,17},{2,10},{10... | collective-permute-start | bytes 1179656 | tf_op jit(solution)/shard_map/ppermute | solution.py:367
  15.9 0.0 collective-permute-done.3
  15.9 1.9 %collective-permute-start.6 = (f32[112,128]{1,0:T(8,128)S(1)}, f32[112,128]{1,0:T(8,128)S(1)}, u32[]{:S(2)}, u32[]{:S(2)}) collective-permute-start(f32[112,128]{1,0:T(8,128)S(1)} %add.8.chip), channel_id=1, source_target_pairs={{0,18},{1,19},{2,16},{3,17},{4,22},{5,23},{6,20},{7,21},{8,26},{9,... | collective-permute-start | bytes 172040 | tf_op jit(solution)/shard_map/ppermute | solution.py:406
  17.8 0.5 %collective-permute-start.5 = (f32[112,128]{1,0:T(8,128)S(1)}, f32[112,128]{1,0:T(8,128)S(1)}, u32[]{:S(2)}, u32[]{:S(2)}) collective-permute-start(f32[112,128]{1,0:T(8,128)S(1)} %add.8.chip), channel_id=1, source_target_pairs={{0,2},{1,3},{2,0},{3,1},{4,6},{5,7},{6,4},{7,5},{8,10},{9,11},{10,... | collective-permute-start | bytes 172040 | tf_op jit(solution)/shard_map/ppermute | solution.py:406
  18.2 1.2 %collective-permute-start.4 = (f32[112,128]{1,0:T(8,128)S(1)}, f32[112,128]{1,0:T(8,128)S(1)}, u32[]{:S(2)}, u32[]{:S(2)}) collective-permute-start(f32[112,128]{1,0:T(8,128)S(1)} %add.8.chip), channel_id=1, source_target_pairs={{0,16},{1,17},{2,18},{3,19},{4,20},{5,21},{6,22},{7,23},{8,24},{9,... | collective-permute-start | bytes 172040 | tf_op jit(solution)/shard_map/ppermute | solution.py:406
  19.5 0.8 %near_input.1.near.after = f32[256,512]{1,0:T(8,128)S(1)} custom-call(bf16[2,3,256,768]{3,2,1,0:T(8,128)(2,1)S(1)} %spread_filters.1.after.spread, bf16[16,16,8,128]{3,2,1,0:T(8,128)(2,1)S(1)} %bitcast.11, bf16[16,9,8,128]{3,2,1,0:T(8,128)(2,1)S(1)} %collective-permute-done.g_nbr), custom_call_target="tpu_custom_call" | custom-call | flops 8589934592 | bytes 33554432 | tf_op jit(solution)/shard_map/near_input/pallas_call | solution.py:331
  20.3 0.9 %collective-permute-done.6.both_off = f32[112,128]{1,0:T(8,128)S(1)} collective-permute-done((f32[112,128]{1,0:T(8,128)S(1)}, f32[112,128]{1,0:T(8,128)S(1)}, u32[]{:S(2)}, u32[]{:S(2)}) %collective-permute-start.6) | collective-permute-done | bytes 57376 | tf_op jit(solution)/shard_map/ppermute | solution.py:406
  21.2 0.8 %collective-permute-done.5.two_off = f32[112,128]{1,0:T(8,128)S(1)} collective-permute-done((f32[112,128]{1,0:T(8,128)S(1)}, f32[112,128]{1,0:T(8,128)S(1)}, u32[]{:S(2)}, u32[]{:S(2)}) %collective-permute-start.5) | collective-permute-done | bytes 57376 | tf_op jit(solution)/shard_map/ppermute | solution.py:406
  22.0 0.5 %collective-permute-done.4.one_off = f32[112,128]{1,0:T(8,128)S(1)} collective-permute-done((f32[112,128]{1,0:T(8,128)S(1)}, f32[112,128]{1,0:T(8,128)S(1)}, u32[]{:S(2)}, u32[]{:S(2)}) %collective-permute-start.4) | collective-permute-done | bytes 57376 | tf_op jit(solution)/shard_map/ppermute | solution.py:406
  22.4 3.2 %collective-permute-start.9 = (f32[112,128]{1,0:T(8,128)S(1)}, f32[112,128]{1,0:T(8,128)S(1)}, u32[]{:S(2)}, u32[]{:S(2)}) collective-permute-start(f32[112,128]{1,0:T(8,128)S(1)} %line_sum.1.line), channel_id=1, source_target_pairs={{0,12},{1,13},{2,14},{3,15},{4,8},{5,9},{6,10},{7,11},{8,4},{9,5},... | collective-permute-start | bytes 172040 | tf_op jit(solution)/shard_map/ppermute | solution.py:406
  25.6 0.3 %collective-permute-start.8 = (f32[112,128]{1,0:T(8,128)S(1)}, f32[112,128]{1,0:T(8,128)S(1)}, u32[]{:S(2)}, u32[]{:S(2)}) collective-permute-start(f32[112,128]{1,0:T(8,128)S(1)} %line_sum.1.line), channel_id=1, source_target_pairs={{0,4},{1,5},{2,6},{3,7},{4,0},{5,1},{6,2},{7,3},{8,12},{9,13},{10,... | collective-permute-start | bytes 172040 | tf_op jit(solution)/shard_map/ppermute | solution.py:406
  26.0 0.9 %collective-permute-start.7 = (f32[112,128]{1,0:T(8,128)S(1)}, f32[112,128]{1,0:T(8,128)S(1)}, u32[]{:S(2)}, u32[]{:S(2)}) collective-permute-start(f32[112,128]{1,0:T(8,128)S(1)} %line_sum.1.line), channel_id=1, source_target_pairs={{0,8},{1,9},{2,10},{3,11},{4,12},{5,13},{6,14},{7,15},{8,0},{9,1},... | collective-permute-start | bytes 172040 | tf_op jit(solution)/shard_map/ppermute | solution.py:406
  26.9 0.0 collective-permute-done.2.g_far
  26.9 1.6 %far_input.1 = (bf16[32,4,8,128]{3,2,1,0:T(8,128)(2,1)}, f32[8,128]{1,0:T(8,128)S(1)}) custom-call(bf16[2,3,256,768]{3,2,1,0:T(8,128)(2,1)S(1)} %spread_filters.1.after.spread, bf16[32,6,8,128]{3,2,1,0:T(8,128)(2,1)S(1)} %collective-permute-done.2.g_far, f32[256,512]{1,0:T(8,128)S(1)} %near_input.1.near.after), custom_call_target="tpu_custom_call" | custom-call | flops 301989888 | bytes 4194304 | tf_op jit(solution)/shard_map/far_input/pallas_call | solution.py:353
  28.5 0.1 collective-permute-done.9.diagonal
  28.5 2.2 %collective-permute-done.8.across = f32[112,128]{1,0:T(8,128)S(1)} collective-permute-done((f32[112,128]{1,0:T(8,128)S(1)}, f32[112,128]{1,0:T(8,128)S(1)}, u32[]{:S(2)}, u32[]{:S(2)}) %collective-permute-start.8) | collective-permute-done | bytes 57376 | tf_op jit(solution)/shard_map/ppermute | solution.py:406
  30.7 0.0 collective-permute-done.7.beside
  30.7 0.1 collective-permute-start.10
  30.8 0.2 prepare.1.ready
  31.0 1.1 %collective-permute-done.10.other = f32[2,112,128]{2,1,0:T(8,128)S(1)} collective-permute-done((f32[2,112,128]{2,1,0:T(8,128)S(1)}, f32[2,112,128]{2,1,0:T(8,128)S(1)}, u32[]{:S(2)}, u32[]{:S(2)}) %collective-permute-start.10) | collective-permute-done | bytes 114720 | tf_op jit(solution)/shard_map/ppermute | solution.py:367
  32.1 1.0 %filter_finish.1 = (f32[27,32,64]{2,1,0:T(8,128)}, f32[1,64]{1,0:T(1,128)}) custom-call(f32[4,112,128]{2,1,0:T(8,128)S(1)} %prepare.1.ready, f32[2,112,128]{2,1,0:T(8,128)S(1)} %collective-permute-done.10.other), custom_call_target="tpu_custom_call" | custom-call | flops 262144 | bytes 1048576 | tf_op jit(solution)/shard_map/filter_finish/pallas_call | solution.py:253
  (3 shorter events, 0.0 us)
Async XLA Ops:
  1.6 11.0 %collective-permute-start = (bf16[16,9,8,128]{3,2,1,0:T(8,128)(2,1)S(1)}, bf16[16,9,8,128]{3,2,1,0:T(8,128)(2,1)S(1)}, u32[]{:S(2)}, u32[]{:S(2)}) collective-permute-start(bf16[16,9,8,128]{3,2,1,0:T(8,128)(2,1)S(1)} %dynamic-slice_bitcast_fusion), channel_id=1, source_target_pairs={{0,16},{8,24},{16,0},{24,8},{1,17},{9,25},{17,1},{25,9},{2,18},{10... | collective-permute-start | bytes 884744 | tf_op jit(solution)/shard_map/ppermute | solution.py:367
  4.7 8.0 %collective-permute-start.1 = (bf16[32,4,8,128]{3,2,1,0:T(8,128)(2,1)}, bf16[32,4,8,128]{3,2,1,0:T(8,128)(2,1)S(1)}, u32[]{:S(2)}, u32[]{:S(2)}) collective-permute-start(bf16[32,4,8,128]{3,2,1,0:T(8,128)(2,1)} %bitcast.12), channel_id=1, source_target_pairs={{0,8},{8,0},{16,24},{24,16},{1,9},{9,1},{17,25},{25,17},{2,10},{10... | collective-permute-start | bytes 786440 | tf_op jit(solution)/shard_map/ppermute | solution.py:367
  6.2 1.0 %copy-start.1 = (bf16[1,16,16,8,128]{4,3,2,1,0:T(8,128)(2,1)S(1)}, bf16[1,16,16,8,128]{4,3,2,1,0:T(8,128)(2,1)}, u32[]{:S(2)}) copy-start(bf16[1,16,16,8,128]{4,3,2,1,0:T(8,128)(2,1)} %param.4) | copy-start | bytes 1572868
  7.2 0.9 %copy-start.3 = (bf16[1,32,4,8,128]{4,3,2,1,0:T(8,128)(2,1)S(1)}, bf16[1,32,4,8,128]{4,3,2,1,0:T(8,128)(2,1)}, u32[]{:S(2)}) copy-start(bf16[1,32,4,8,128]{4,3,2,1,0:T(8,128)(2,1)} %param.3) | copy-start | bytes 786436
  8.7 0.9 %copy-start = (bf16[27,64,32]{1,2,0:T(8,128)(2,1)S(1)}, bf16[27,64,32]{1,2,0:T(8,128)(2,1)}, u32[]{:S(2)}) copy-start(bf16[27,64,32]{1,2,0:T(8,128)(2,1)} %param.5) | copy-start | bytes 331780
  12.7 1.6 %copy-start.2 = (bf16[1,16,16,8,128]{4,3,2,1,0:T(8,128)(2,1)S(1)}, bf16[1,16,16,8,128]{4,3,2,1,0:T(8,128)(2,1)}, u32[]{:S(2)}) copy-start(bf16[1,16,16,8,128]{4,3,2,1,0:T(8,128)(2,1)} %param.4) | copy-start | bytes 1572868
  14.2 1.7 %collective-permute-start.3 = (f32[112,128]{1,0:T(8,128)S(1)}, f32[112,128]{1,0:T(8,128)S(1)}, u32[]{:S(2)}, u32[]{:S(2)}) collective-permute-start(f32[112,128]{1,0:T(8,128)S(1)} %get-tuple-element.17), channel_id=1, source_target_pairs={{0,1},{1,0},{2,3},{3,2},{4,5},{5,4},{6,7},{7,6},{8,9},{9,8},{10,11... | collective-permute-start | bytes 172040 | tf_op jit(solution)/shard_map/ppermute | solution.py:367
  14.3 12.5 %collective-permute-start.2 = (bf16[32,6,8,128]{3,2,1,0:T(8,128)(2,1)S(1)}, bf16[32,6,8,128]{3,2,1,0:T(8,128)(2,1)S(1)}, u32[]{:S(2)}, u32[]{:S(2)}) collective-permute-start(bf16[32,6,8,128]{3,2,1,0:T(8,128)(2,1)S(1)} %pass_on.1), channel_id=1, source_target_pairs={{0,8},{8,0},{16,24},{24,16},{1,9},{9,1},{17,25},{25,17},{2,10},{10... | collective-permute-start | bytes 1179656 | tf_op jit(solution)/shard_map/ppermute | solution.py:367
  15.9 5.3 %collective-permute-start.6 = (f32[112,128]{1,0:T(8,128)S(1)}, f32[112,128]{1,0:T(8,128)S(1)}, u32[]{:S(2)}, u32[]{:S(2)}) collective-permute-start(f32[112,128]{1,0:T(8,128)S(1)} %add.8.chip), channel_id=1, source_target_pairs={{0,18},{1,19},{2,16},{3,17},{4,22},{5,23},{6,20},{7,21},{8,26},{9,... | collective-permute-start | bytes 172040 | tf_op jit(solution)/shard_map/ppermute | solution.py:406
  17.8 4.2 %collective-permute-start.5 = (f32[112,128]{1,0:T(8,128)S(1)}, f32[112,128]{1,0:T(8,128)S(1)}, u32[]{:S(2)}, u32[]{:S(2)}) collective-permute-start(f32[112,128]{1,0:T(8,128)S(1)} %add.8.chip), channel_id=1, source_target_pairs={{0,2},{1,3},{2,0},{3,1},{4,6},{5,7},{6,4},{7,5},{8,10},{9,11},{10,... | collective-permute-start | bytes 172040 | tf_op jit(solution)/shard_map/ppermute | solution.py:406
  18.2 4.2 %collective-permute-start.4 = (f32[112,128]{1,0:T(8,128)S(1)}, f32[112,128]{1,0:T(8,128)S(1)}, u32[]{:S(2)}, u32[]{:S(2)}) collective-permute-start(f32[112,128]{1,0:T(8,128)S(1)} %add.8.chip), channel_id=1, source_target_pairs={{0,16},{1,17},{2,18},{3,19},{4,20},{5,21},{6,22},{7,23},{8,24},{9,... | collective-permute-start | bytes 172040 | tf_op jit(solution)/shard_map/ppermute | solution.py:406
  22.4 6.1 %collective-permute-start.9 = (f32[112,128]{1,0:T(8,128)S(1)}, f32[112,128]{1,0:T(8,128)S(1)}, u32[]{:S(2)}, u32[]{:S(2)}) collective-permute-start(f32[112,128]{1,0:T(8,128)S(1)} %line_sum.1.line), channel_id=1, source_target_pairs={{0,12},{1,13},{2,14},{3,15},{4,8},{5,9},{6,10},{7,11},{8,4},{9,5},... | collective-permute-start | bytes 172040 | tf_op jit(solution)/shard_map/ppermute | solution.py:406
  25.6 5.1 %collective-permute-start.8 = (f32[112,128]{1,0:T(8,128)S(1)}, f32[112,128]{1,0:T(8,128)S(1)}, u32[]{:S(2)}, u32[]{:S(2)}) collective-permute-start(f32[112,128]{1,0:T(8,128)S(1)} %line_sum.1.line), channel_id=1, source_target_pairs={{0,4},{1,5},{2,6},{3,7},{4,0},{5,1},{6,2},{7,3},{8,12},{9,13},{10,... | collective-permute-start | bytes 172040 | tf_op jit(solution)/shard_map/ppermute | solution.py:406
  26.0 4.7 %collective-permute-start.7 = (f32[112,128]{1,0:T(8,128)S(1)}, f32[112,128]{1,0:T(8,128)S(1)}, u32[]{:S(2)}, u32[]{:S(2)}) collective-permute-start(f32[112,128]{1,0:T(8,128)S(1)} %line_sum.1.line), channel_id=1, source_target_pairs={{0,8},{1,9},{2,10},{3,11},{4,12},{5,13},{6,14},{7,15},{8,0},{9,1},... | collective-permute-start | bytes 172040 | tf_op jit(solution)/shard_map/ppermute | solution.py:406
  30.7 1.4 %collective-permute-start.10 = (f32[2,112,128]{2,1,0:T(8,128)S(1)}, f32[2,112,128]{2,1,0:T(8,128)S(1)}, u32[]{:S(2)}, u32[]{:S(2)}) collective-permute-start(f32[2,112,128]{2,1,0:T(8,128)S(1)} %last_sum.1.mine), channel_id=1, source_target_pairs={{0,1},{1,0},{2,3},{3,2},{4,5},{5,4},{6,7},{7,6},{8,9},{9,8},{10,11... | collective-permute-start | bytes 344072 | tf_op jit(solution)/shard_map/ppermute | solution.py:367

commit v8 on v7

--- a/solution.py
+++ b/solution.py
@@ -150,10 +150,7 @@
 def filter_kernel(a_in, g_in, sums, g_nbr, a_nbr, after, *outs):
     row, col, core = grid_place()
     for r in range(2):
-        for c in range(2):
-            pl.when((row == r) & (col == c))(
-                functools.partial(filter_body, r, c, core, sums, g_nbr, a_nbr, *outs)
-            )
+        pl.when(row == r)(functools.partial(filter_body, r, col, core, sums, g_nbr, a_nbr, *outs))
 
 
 def filter_partial(a_rows, g_rows, sums, g_nbr, a_nbr, after):

time: 33.4 us -> 33.4 us (level)
  no operation moved by 1% of the time
where the time goes in v8:
time: 33.4 us; the launch traced here: 33.1 us
  starting transfers between devices  14.2 us (43%)
  Pallas kernels  7.91 us (24%)
  waiting for transfers between devices  6.29 us (19%)
  local copies, waits for them, and re-layouts  3.92 us (12%)
  between operations  0.75 us (2%)
    ppermute x6, starting transfers between devices, swap_at(): return lax.ppermute(block, ('slab', 'sample'), pairs)  8.01 us
    ppermute x5, starting transfers between devices, swap(): return lax.ppermute(block, axis, [(i, i ^ bits) for i in range(count)])  6.22 us
    ppermute x6, waiting for transfers between devices, swap_at(): return lax.ppermute(block, ('slab', 'sample'), pairs)  4.33 us
    unnamed x8, local copies, waits for them, and re-layouts  2.93 us
    pallas_call x1, Pallas kernels, spread_filters(): pl.pallas_call(spread_kernel, out_shape=jax.ShapeDtypeStruct((2, 3, 256,...  2.13 us
    ppermute x5, waiting for transfers between devices, swap(): return lax.ppermute(block, axis, [(i, i ^ bits) for i in range(count)])  1.96 us
    pallas_call x1, Pallas kernels, far_input(): pl.pallas_call(far_input_kernel, out_shape=(jax.ShapeDtypeStruct((32, 4,...  1.58 us
    pallas_call x1, Pallas kernels, filter_partial(): pl.pallas_call(filter_kernel, out_shape=ROWS + (half, half), in_specs=[vm...  1.51 us
  transfers between devices with their start and end apart: 11, of which 7 were waited for; matrix products, arithmetic and copies ran while one was open for 0% of the time, Pallas kernels for 16%

profile of v8, /device:TPU:0, one launch (start us, length us, event | category | flops | bytes accessed | tf_op | source)
XLA Modules:
  0.0 33.1 jit_solution(582918042377869394)
XLA Ops:
  0.6 1.0 %dynamic-slice_bitcast_fusion = bf16[16,9,8,128]{3,2,1,0:T(8,128)(2,1)S(1)} fusion(bf16[1,16,16,8,128]{4,3,2,1,0:T(8,128)(2,1)} %param.4, s32[]{:T(128)S(6)} %select_n.9), kind=kLoop, calls=%fused_computation | loop fusion | bytes 589828 | tf_op jit(solution)/shard_map/dynamic_slice | solution.py:413
  1.6 3.0 %collective-permute-start = (bf16[16,9,8,128]{3,2,1,0:T(8,128)(2,1)S(1)}, bf16[16,9,8,128]{3,2,1,0:T(8,128)(2,1)S(1)}, u32[]{:S(2)}, u32[]{:S(2)}) collective-permute-start(bf16[16,9,8,128]{3,2,1,0:T(8,128)(2,1)S(1)} %dynamic-slice_bitcast_fusion), channel_id=1, source_target_pairs={{0,16},{8,24},{16,0},{24,8},{1,17},{9,25},{17,1},{25,9},{2,18},{10... | collective-permute-start | bytes 884744 | tf_op jit(solution)/shard_map/ppermute | solution.py:364
  4.7 1.5 %collective-permute-start.1 = (bf16[32,4,8,128]{3,2,1,0:T(8,128)(2,1)}, bf16[32,4,8,128]{3,2,1,0:T(8,128)(2,1)S(1)}, u32[]{:S(2)}, u32[]{:S(2)}) collective-permute-start(bf16[32,4,8,128]{3,2,1,0:T(8,128)(2,1)} %bitcast.12), channel_id=1, source_target_pairs={{0,8},{8,0},{16,24},{24,16},{1,9},{9,1},{17,25},{25,17},{2,10},{10... | collective-permute-start | bytes 786440 | tf_op jit(solution)/shard_map/ppermute | solution.py:364
  6.2 0.0 copy-start.1
  6.2 1.0 %copy-done.1 = bf16[1,16,16,8,128]{4,3,2,1,0:T(8,128)(2,1)S(1)} copy-done((bf16[1,16,16,8,128]{4,3,2,1,0:T(8,128)(2,1)S(1)}, bf16[1,16,16,8,128]{4,3,2,1,0:T(8,128)(2,1)}, u32[]{:S(2)}) %copy-start.1) | copy-done | bytes 524312
  7.2 0.0 copy-start.3
  7.2 0.9 %copy-done.3 = bf16[1,32,4,8,128]{4,3,2,1,0:T(8,128)(2,1)S(1)} copy-done((bf16[1,32,4,8,128]{4,3,2,1,0:T(8,128)(2,1)S(1)}, bf16[1,32,4,8,128]{4,3,2,1,0:T(8,128)(2,1)}, u32[]{:S(2)}) %copy-start.3) | copy-done | bytes 262168
  8.2 0.5 %near_rows.1 = (bf16[8,32,1280]{2,1,0:T(8,128)(2,1)S(1)}, bf16[10,128,1024]{2,1,0:T(8,128)(2,1)S(1)}, f32[16,128]{1,0:T(8,128)S(1)}) custom-call(bf16[16,16,8,128]{3,2,1,0:T(8,128)(2,1)S(1)} %bitcast.9, bf16[32,4,8,128]{3,2,1,0:T(8,128)(2,1)S(1)} %bitcast.13), custom_call_target="tpu_custom_call" | custom-call | flops 268435456 | bytes 2097152 | tf_op jit(solution)/shard_map/near_rows/pallas_call | solution.py:108
  8.7 0.0 copy-start
  8.7 0.9 %copy-done = bf16[27,64,32]{1,2,0:T(8,128)(2,1)S(1)} copy-done((bf16[27,64,32]{1,2,0:T(8,128)(2,1)S(1)}, bf16[27,64,32]{1,2,0:T(8,128)(2,1)}, u32[]{:S(2)}) %copy-start) | copy-done | bytes 110616
  9.6 2.1 %spread_filters.1.after.spread = bf16[2,3,256,768]{3,2,1,0:T(8,128)(2,1)S(1)} custom-call(bf16[27,32,64]{2,1,0:T(8,128)(2,1)S(1)} %bitcast.8, f32[16,128]{1,0:T(8,128)S(1)} %get-tuple-element.12.after.sums), custom_call_target="tpu_custom_call" | custom-call | flops 452984832 | bytes 2097152 | tf_op jit(solution)/shard_map/spread_filters/pallas_call | solution.py:286
  11.8 0.9 %collective-permute-done.1.a_nbr = bf16[32,4,8,128]{3,2,1,0:T(8,128)(2,1)S(1)} collective-permute-done((bf16[32,4,8,128]{3,2,1,0:T(8,128)(2,1)}, bf16[32,4,8,128]{3,2,1,0:T(8,128)(2,1)S(1)}, u32[]{:S(2)}, u32[]{:S(2)}) %collective-permute-start.1) | collective-permute-done | bytes 262176 | tf_op jit(solution)/shard_map/ppermute | solution.py:364
  12.7 0.0 collective-permute-done.g_nbr
  12.7 0.0 copy-start.2
  12.7 1.5 %filter_partial.1 = (bf16[8,32,1280]{2,1,0:T(8,128)(2,1)S(1)}, bf16[10,128,1024]{2,1,0:T(8,128)(2,1)S(1)}, f32[112,128]{1,0:T(8,128)S(1)}, f32[112,128]{1,0:T(8,128)S(1)}) custom-call(bf16[8,32,1280]{2,1,0:T(8,128)(2,1)S(1)} %get-tuple-element.13.a_in, ...), custom_call_target="tpu_custom_call", output_to_operand_aliasing={{0}: (0, {}), {1}: (1, {})} | custom-call | flops 566231040 | bytes 2097152 | tf_op jit(solution)/shard_map/filter_partial/pallas_call | solution.py:158
  14.2 0.1 collective-permute-start.3
  14.3 0.0 copy-done.2
  14.3 0.1 pass_on.1
  14.3 1.6 %collective-permute-start.2 = (bf16[32,6,8,128]{3,2,1,0:T(8,128)(2,1)S(1)}, bf16[32,6,8,128]{3,2,1,0:T(8,128)(2,1)S(1)}, u32[]{:S(2)}, u32[]{:S(2)}) collective-permute-start(bf16[32,6,8,128]{3,2,1,0:T(8,128)(2,1)S(1)} %pass_on.1), channel_id=1, source_target_pairs={{0,8},{8,0},{16,24},{24,16},{1,9},{9,1},{17,25},{25,17},{2,10},{10... | collective-permute-start | bytes 1179656 | tf_op jit(solution)/shard_map/ppermute | solution.py:364
  15.9 0.0 collective-permute-done.3
  15.9 1.9 %collective-permute-start.6 = (f32[112,128]{1,0:T(8,128)S(1)}, f32[112,128]{1,0:T(8,128)S(1)}, u32[]{:S(2)}, u32[]{:S(2)}) collective-permute-start(f32[112,128]{1,0:T(8,128)S(1)} %add.8.chip), channel_id=1, source_target_pairs={{0,18},{1,19},{2,16},{3,17},{4,22},{5,23},{6,20},{7,21},{8,26},{9,... | collective-permute-start | bytes 172040 | tf_op jit(solution)/shard_map/ppermute | solution.py:403
  17.8 0.4 %collective-permute-start.5 = (f32[112,128]{1,0:T(8,128)S(1)}, f32[112,128]{1,0:T(8,128)S(1)}, u32[]{:S(2)}, u32[]{:S(2)}) collective-permute-start(f32[112,128]{1,0:T(8,128)S(1)} %add.8.chip), channel_id=1, source_target_pairs={{0,2},{1,3},{2,0},{3,1},{4,6},{5,7},{6,4},{7,5},{8,10},{9,11},{10,... | collective-permute-start | bytes 172040 | tf_op jit(solution)/shard_map/ppermute | solution.py:403
  18.2 1.2 %collective-permute-start.4 = (f32[112,128]{1,0:T(8,128)S(1)}, f32[112,128]{1,0:T(8,128)S(1)}, u32[]{:S(2)}, u32[]{:S(2)}) collective-permute-start(f32[112,128]{1,0:T(8,128)S(1)} %add.8.chip), channel_id=1, source_target_pairs={{0,16},{1,17},{2,18},{3,19},{4,20},{5,21},{6,22},{7,23},{8,24},{9,... | collective-permute-start | bytes 172040 | tf_op jit(solution)/shard_map/ppermute | solution.py:403
  19.5 0.8 %near_input.1.near.after = f32[256,512]{1,0:T(8,128)S(1)} custom-call(bf16[2,3,256,768]{3,2,1,0:T(8,128)(2,1)S(1)} %spread_filters.1.after.spread, bf16[16,16,8,128]{3,2,1,0:T(8,128)(2,1)S(1)} %bitcast.11, bf16[16,9,8,128]{3,2,1,0:T(8,128)(2,1)S(1)} %collective-permute-done.g_nbr), custom_call_target="tpu_custom_call" | custom-call | flops 8589934592 | bytes 33554432 | tf_op jit(solution)/shard_map/near_input/pallas_call | solution.py:328
  20.3 0.9 %collective-permute-done.6.both_off = f32[112,128]{1,0:T(8,128)S(1)} collective-permute-done((f32[112,128]{1,0:T(8,128)S(1)}, f32[112,128]{1,0:T(8,128)S(1)}, u32[]{:S(2)}, u32[]{:S(2)}) %collective-permute-start.6) | collective-permute-done | bytes 57376 | tf_op jit(solution)/shard_map/ppermute | solution.py:403
  21.2 0.8 %collective-permute-done.5.two_off = f32[112,128]{1,0:T(8,128)S(1)} collective-permute-done((f32[112,128]{1,0:T(8,128)S(1)}, f32[112,128]{1,0:T(8,128)S(1)}, u32[]{:S(2)}, u32[]{:S(2)}) %collective-permute-start.5) | collective-permute-done | bytes 57376 | tf_op jit(solution)/shard_map/ppermute | solution.py:403
  22.0 0.4 %collective-permute-done.4.one_off = f32[112,128]{1,0:T(8,128)S(1)} collective-permute-done((f32[112,128]{1,0:T(8,128)S(1)}, f32[112,128]{1,0:T(8,128)S(1)}, u32[]{:S(2)}, u32[]{:S(2)}) %collective-permute-start.4) | collective-permute-done | bytes 57376 | tf_op jit(solution)/shard_map/ppermute | solution.py:403
  22.4 3.2 %collective-permute-start.9 = (f32[112,128]{1,0:T(8,128)S(1)}, f32[112,128]{1,0:T(8,128)S(1)}, u32[]{:S(2)}, u32[]{:S(2)}) collective-permute-start(f32[112,128]{1,0:T(8,128)S(1)} %line_sum.1.line), channel_id=1, source_target_pairs={{0,12},{1,13},{2,14},{3,15},{4,8},{5,9},{6,10},{7,11},{8,4},{9,5},... | collective-permute-start | bytes 172040 | tf_op jit(solution)/shard_map/ppermute | solution.py:403
  25.6 0.3 %collective-permute-start.8 = (f32[112,128]{1,0:T(8,128)S(1)}, f32[112,128]{1,0:T(8,128)S(1)}, u32[]{:S(2)}, u32[]{:S(2)}) collective-permute-start(f32[112,128]{1,0:T(8,128)S(1)} %line_sum.1.line), channel_id=1, source_target_pairs={{0,4},{1,5},{2,6},{3,7},{4,0},{5,1},{6,2},{7,3},{8,12},{9,13},{10,... | collective-permute-start | bytes 172040 | tf_op jit(solution)/shard_map/ppermute | solution.py:403
  25.9 0.9 %collective-permute-start.7 = (f32[112,128]{1,0:T(8,128)S(1)}, f32[112,128]{1,0:T(8,128)S(1)}, u32[]{:S(2)}, u32[]{:S(2)}) collective-permute-start(f32[112,128]{1,0:T(8,128)S(1)} %line_sum.1.line), channel_id=1, source_target_pairs={{0,8},{1,9},{2,10},{3,11},{4,12},{5,13},{6,14},{7,15},{8,0},{9,1},... | collective-permute-start | bytes 172040 | tf_op jit(solution)/shard_map/ppermute | solution.py:403
  26.9 0.0 collective-permute-done.2.g_far
  26.9 1.6 %far_input.1 = (bf16[32,4,8,128]{3,2,1,0:T(8,128)(2,1)}, f32[8,128]{1,0:T(8,128)S(1)}) custom-call(bf16[2,3,256,768]{3,2,1,0:T(8,128)(2,1)S(1)} %spread_filters.1.after.spread, bf16[32,6,8,128]{3,2,1,0:T(8,128)(2,1)S(1)} %collective-permute-done.2.g_far, f32[256,512]{1,0:T(8,128)S(1)} %near_input.1.near.after), custom_call_target="tpu_custom_call" | custom-call | flops 301989888 | bytes 4194304 | tf_op jit(solution)/shard_map/far_input/pallas_call | solution.py:350
  28.5 0.1 collective-permute-done.9.diagonal
  28.5 2.2 %collective-permute-done.8.across = f32[112,128]{1,0:T(8,128)S(1)} collective-permute-done((f32[112,128]{1,0:T(8,128)S(1)}, f32[112,128]{1,0:T(8,128)S(1)}, u32[]{:S(2)}, u32[]{:S(2)}) %collective-permute-start.8) | collective-permute-done | bytes 57376 | tf_op jit(solution)/shard_map/ppermute | solution.py:403
  30.7 0.0 collective-permute-done.7.beside
  30.7 0.1 collective-permute-start.10
  30.8 0.2 prepare.1.ready
  31.0 1.1 %collective-permute-done.10.other = f32[2,112,128]{2,1,0:T(8,128)S(1)} collective-permute-done((f32[2,112,128]{2,1,0:T(8,128)S(1)}, f32[2,112,128]{2,1,0:T(8,128)S(1)}, u32[]{:S(2)}, u32[]{:S(2)}) %collective-permute-start.10) | collective-permute-done | bytes 114720 | tf_op jit(solution)/shard_map/ppermute | solution.py:364
  32.1 1.0 %filter_finish.1 = (f32[27,32,64]{2,1,0:T(8,128)}, f32[1,64]{1,0:T(1,128)}) custom-call(f32[4,112,128]{2,1,0:T(8,128)S(1)} %prepare.1.ready, f32[2,112,128]{2,1,0:T(8,128)S(1)} %collective-permute-done.10.other), custom_call_target="tpu_custom_call" | custom-call | flops 262144 | bytes 1048576 | tf_op jit(solution)/shard_map/filter_finish/pallas_call | solution.py:250
  (3 shorter events, 0.0 us)
Async XLA Ops:
  1.6 11.0 %collective-permute-start = (bf16[16,9,8,128]{3,2,1,0:T(8,128)(2,1)S(1)}, bf16[16,9,8,128]{3,2,1,0:T(8,128)(2,1)S(1)}, u32[]{:S(2)}, u32[]{:S(2)}) collective-permute-start(bf16[16,9,8,128]{3,2,1,0:T(8,128)(2,1)S(1)} %dynamic-slice_bitcast_fusion), channel_id=1, source_target_pairs={{0,16},{8,24},{16,0},{24,8},{1,17},{9,25},{17,1},{25,9},{2,18},{10... | collective-permute-start | bytes 884744 | tf_op jit(solution)/shard_map/ppermute | solution.py:364
  4.7 8.0 %collective-permute-start.1 = (bf16[32,4,8,128]{3,2,1,0:T(8,128)(2,1)}, bf16[32,4,8,128]{3,2,1,0:T(8,128)(2,1)S(1)}, u32[]{:S(2)}, u32[]{:S(2)}) collective-permute-start(bf16[32,4,8,128]{3,2,1,0:T(8,128)(2,1)} %bitcast.12), channel_id=1, source_target_pairs={{0,8},{8,0},{16,24},{24,16},{1,9},{9,1},{17,25},{25,17},{2,10},{10... | collective-permute-start | bytes 786440 | tf_op jit(solution)/shard_map/ppermute | solution.py:364
  6.2 1.0 %copy-start.1 = (bf16[1,16,16,8,128]{4,3,2,1,0:T(8,128)(2,1)S(1)}, bf16[1,16,16,8,128]{4,3,2,1,0:T(8,128)(2,1)}, u32[]{:S(2)}) copy-start(bf16[1,16,16,8,128]{4,3,2,1,0:T(8,128)(2,1)} %param.4) | copy-start | bytes 1572868
  7.2 0.9 %copy-start.3 = (bf16[1,32,4,8,128]{4,3,2,1,0:T(8,128)(2,1)S(1)}, bf16[1,32,4,8,128]{4,3,2,1,0:T(8,128)(2,1)}, u32[]{:S(2)}) copy-start(bf16[1,32,4,8,128]{4,3,2,1,0:T(8,128)(2,1)} %param.3) | copy-start | bytes 786436
  8.7 0.9 %copy-start = (bf16[27,64,32]{1,2,0:T(8,128)(2,1)S(1)}, bf16[27,64,32]{1,2,0:T(8,128)(2,1)}, u32[]{:S(2)}) copy-start(bf16[27,64,32]{1,2,0:T(8,128)(2,1)} %param.5) | copy-start | bytes 331780
  12.7 1.6 %copy-start.2 = (bf16[1,16,16,8,128]{4,3,2,1,0:T(8,128)(2,1)S(1)}, bf16[1,16,16,8,128]{4,3,2,1,0:T(8,128)(2,1)}, u32[]{:S(2)}) copy-start(bf16[1,16,16,8,128]{4,3,2,1,0:T(8,128)(2,1)} %param.4) | copy-start | bytes 1572868
  14.2 1.7 %collective-permute-start.3 = (f32[112,128]{1,0:T(8,128)S(1)}, f32[112,128]{1,0:T(8,128)S(1)}, u32[]{:S(2)}, u32[]{:S(2)}) collective-permute-start(f32[112,128]{1,0:T(8,128)S(1)} %get-tuple-element.17), channel_id=1, source_target_pairs={{0,1},{1,0},{2,3},{3,2},{4,5},{5,4},{6,7},{7,6},{8,9},{9,8},{10,11... | collective-permute-start | bytes 172040 | tf_op jit(solution)/shard_map/ppermute | solution.py:364
  14.3 12.6 %collective-permute-start.2 = (bf16[32,6,8,128]{3,2,1,0:T(8,128)(2,1)S(1)}, bf16[32,6,8,128]{3,2,1,0:T(8,128)(2,1)S(1)}, u32[]{:S(2)}, u32[]{:S(2)}) collective-permute-start(bf16[32,6,8,128]{3,2,1,0:T(8,128)(2,1)S(1)} %pass_on.1), channel_id=1, source_target_pairs={{0,8},{8,0},{16,24},{24,16},{1,9},{9,1},{17,25},{25,17},{2,10},{10... | collective-permute-start | bytes 1179656 | tf_op jit(solution)/shard_map/ppermute | solution.py:364
  15.9 5.3 %collective-permute-start.6 = (f32[112,128]{1,0:T(8,128)S(1)}, f32[112,128]{1,0:T(8,128)S(1)}, u32[]{:S(2)}, u32[]{:S(2)}) collective-permute-start(f32[112,128]{1,0:T(8,128)S(1)} %add.8.chip), channel_id=1, source_target_pairs={{0,18},{1,19},{2,16},{3,17},{4,22},{5,23},{6,20},{7,21},{8,26},{9,... | collective-permute-start | bytes 172040 | tf_op jit(solution)/shard_map/ppermute | solution.py:403
  17.8 4.2 %collective-permute-start.5 = (f32[112,128]{1,0:T(8,128)S(1)}, f32[112,128]{1,0:T(8,128)S(1)}, u32[]{:S(2)}, u32[]{:S(2)}) collective-permute-start(f32[112,128]{1,0:T(8,128)S(1)} %add.8.chip), channel_id=1, source_target_pairs={{0,2},{1,3},{2,0},{3,1},{4,6},{5,7},{6,4},{7,5},{8,10},{9,11},{10,... | collective-permute-start | bytes 172040 | tf_op jit(solution)/shard_map/ppermute | solution.py:403
  18.2 4.2 %collective-permute-start.4 = (f32[112,128]{1,0:T(8,128)S(1)}, f32[112,128]{1,0:T(8,128)S(1)}, u32[]{:S(2)}, u32[]{:S(2)}) collective-permute-start(f32[112,128]{1,0:T(8,128)S(1)} %add.8.chip), channel_id=1, source_target_pairs={{0,16},{1,17},{2,18},{3,19},{4,20},{5,21},{6,22},{7,23},{8,24},{9,... | collective-permute-start | bytes 172040 | tf_op jit(solution)/shard_map/ppermute | solution.py:403
  22.4 6.1 %collective-permute-start.9 = (f32[112,128]{1,0:T(8,128)S(1)}, f32[112,128]{1,0:T(8,128)S(1)}, u32[]{:S(2)}, u32[]{:S(2)}) collective-permute-start(f32[112,128]{1,0:T(8,128)S(1)} %line_sum.1.line), channel_id=1, source_target_pairs={{0,12},{1,13},{2,14},{3,15},{4,8},{5,9},{6,10},{7,11},{8,4},{9,5},... | collective-permute-start | bytes 172040 | tf_op jit(solution)/shard_map/ppermute | solution.py:403
  25.6 5.1 %collective-permute-start.8 = (f32[112,128]{1,0:T(8,128)S(1)}, f32[112,128]{1,0:T(8,128)S(1)}, u32[]{:S(2)}, u32[]{:S(2)}) collective-permute-start(f32[112,128]{1,0:T(8,128)S(1)} %line_sum.1.line), channel_id=1, source_target_pairs={{0,4},{1,5},{2,6},{3,7},{4,0},{5,1},{6,2},{7,3},{8,12},{9,13},{10,... | collective-permute-start | bytes 172040 | tf_op jit(solution)/shard_map/ppermute | solution.py:403
  25.9 4.7 %collective-permute-start.7 = (f32[112,128]{1,0:T(8,128)S(1)}, f32[112,128]{1,0:T(8,128)S(1)}, u32[]{:S(2)}, u32[]{:S(2)}) collective-permute-start(f32[112,128]{1,0:T(8,128)S(1)} %line_sum.1.line), channel_id=1, source_target_pairs={{0,8},{1,9},{2,10},{3,11},{4,12},{5,13},{6,14},{7,15},{8,0},{9,1},... | collective-permute-start | bytes 172040 | tf_op jit(solution)/shard_map/ppermute | solution.py:403
  30.7 1.4 %collective-permute-start.10 = (f32[2,112,128]{2,1,0:T(8,128)S(1)}, f32[2,112,128]{2,1,0:T(8,128)S(1)}, u32[]{:S(2)}, u32[]{:S(2)}) collective-permute-start(f32[2,112,128]{2,1,0:T(8,128)S(1)} %last_sum.1.mine), channel_id=1, source_target_pairs={{0,1},{1,0},{2,3},{3,2},{4,5},{5,4},{6,7},{7,6},{8,9},{9,8},{10,11... | collective-permute-start | bytes 344072 | tf_op jit(solution)/shard_map/ppermute | solution.py:364
